TPU v7x, 32 devices: a whole 2x2x4 slice. The times are simulated.
32 devices in a mesh: dp: 8 (over z, x), seq: 4 (over y, core).
Axes of the slice: x: 2, y: 2, z: 4, core: 2. Of those that a mesh axis runs over, the one named last changes fastest.
Arguments:
- src_input: bfloat16 [8, 1024, 512], P('dp', 'seq'), may hold values from -6 to 6
- tgt_input: bfloat16 [8, 1024, 512], P('dp', 'seq'), may hold values from -6 to 6
- out_cotangent: bfloat16 [8, 1024, 512], P('dp', 'seq'), may hold values from -6 to 6
- src_lengths: int32 [8, 4], P('dp'), may hold values from 1 to 769, 1024 in all within a row
- tgt_lengths: int32 [8, 4], P('dp'), may hold values from 1 to 769, 1024 in all within a row
- enc_expert: int32 [8, 1], P('dp'), may hold values from 0 to 3
- dec_expert: int32 [8, 1], P('dp'), may hold values from 0 to 3
- norm_gains: bfloat16 [5, 512], P(None, 'dp'), may hold values from 0.5 to 1.5
- norm_biases: bfloat16 [5, 512], P(None, 'dp'), may hold values from -3 to 3
- qkv_weight: bfloat16 [3, 3, 512, 512], P(None, None, 'dp', 'seq'), may hold values from -0.25 to 0.25
- out_weight: bfloat16 [3, 512, 512], P(None, 'seq', 'dp'), may hold values from -0.5 to 0.5
- expert_up: bfloat16 [2, 4, 512, 2048], P(None, None, 'dp', 'seq'), may hold values from -0.25 to 0.25
- expert_down: bfloat16 [2, 4, 2048, 512], P(None, None, 'seq', 'dp'), may hold values from -0.125 to 0.125
Outputs:
- decoder_output: float32 [8, 1024, 512], P('dp', 'seq')
- src_grad: float32 [8, 1024, 512], P('dp', 'seq')
- tgt_grad: float32 [8, 1024, 512], P('dp', 'seq')
- gain_grad: float32 [5, 512], P(None, 'dp')
- bias_grad: float32 [5, 512], P(None, 'dp')
- qkv_grad: float32 [3, 3, 512, 512], P(None, None, 'dp', 'seq')
- out_grad: float32 [3, 512, 512], P(None, 'seq', 'dp')
- up_grad: float32 [2, 4, 512, 2048], P(None, None, 'dp', 'seq')
- down_grad: float32 [2, 4, 2048, 512], P(None, None, 'seq', 'dp')
- sublayer_rms: float32 [8, 2, 5], P('dp')
Inputs may be any that keep to these rules, and one draw needn't show every extreme that they name: `src_lengths`: each row's 4 source lengths sum to 1024; the longest is 769. `tgt_lengths`: each row's 4 target lengths sum to 1024; the longest is 769.
All inputs are finite; a program needn't handle non-finite values.
Results may differ from a plain program's by a relative error of at most 0.024.
Values may be sent and summed in bfloat16 or wider, within the bound.
A program may use at most 192 MiB of HBM per device.

v0:
```python
import jax
import jax.numpy as jnp
from jax import lax
from jax.sharding import PartitionSpec as P

HEAD_DIM = 64


EPSILON = 1e-05
MASKED = -1e30


def normalize(values, gain, shift):
    average = jnp.mean(values, -1, keepdims=True)
    centered = values - average
    variance = jnp.mean(centered * centered, -1, keepdims=True)
    return centered * lax.rsqrt(variance + EPSILON) * gain + shift


def norm_backward(values, gain, shift, upstream):
    unused, pullback = jax.vjp(normalize, values, gain, shift)
    return pullback(upstream)


def segment_ids(lengths, length):
    bounds = jnp.cumsum(lengths, -1)
    places = jnp.arange(length, dtype=jnp.int32)[:, None]
    return jnp.sum((places >= bounds[..., None, :]).astype(jnp.int32), -1)


def split_heads(tensor):
    return tensor.reshape(tensor.shape[0], -1, HEAD_DIM)


def masked_scores(heads_query, heads_key, seg_query, seg_key, causal):
    scores = jnp.einsum(
        "qhd,khd->hqk", heads_query, heads_key, preferred_element_type=jnp.float32
    ) * HEAD_DIM ** (-0.5)
    allowed = seg_query[:, None] == seg_key[None, :]
    if causal:
        places = jnp.arange(seg_query.shape[0])
        allowed = allowed & (places[:, None] >= places[None, :])
    return jnp.where(allowed[None], scores, MASKED)


def project(rows, weight):
    return jnp.einsum("rld,de->rle", rows, weight, preferred_element_type=jnp.float32)


def attend_forward(query_rows, key_rows, weights, seg_query, seg_key, causal):
    query = project(query_rows, weights[0]).astype(jnp.bfloat16)
    keys = project(key_rows, weights[1]).astype(jnp.bfloat16)
    values = project(key_rows, weights[2]).astype(jnp.bfloat16)

    def per_row(items):
        row_query, row_key, row_value, row_sq, row_sk = items
        scores = masked_scores(split_heads(row_query), split_heads(row_key), row_sq, row_sk, causal)
        highest = jnp.max(scores, -1, keepdims=True)
        expos = jnp.exp(scores - highest)
        totals = jnp.sum(expos, -1, keepdims=True)
        probs = (expos / totals).astype(jnp.bfloat16)
        mixed = jnp.einsum(
            "hqk,khd->qhd", probs, split_heads(row_value), preferred_element_type=jnp.float32
        )
        return (mixed.reshape(row_query.shape).astype(jnp.bfloat16), highest + jnp.log(totals))

    mixed, logsum = lax.map(per_row, (query, keys, values, seg_query, seg_key))
    return (query, keys, values, mixed, logsum)


def attend_backward(
    saved, query_rows, key_rows, upstream_rows, weights, out_w, seg_query, seg_key, causal
):
    query, keys, values, mixed, logsum = saved
    out_change = jnp.einsum("rle,rld->ed", mixed, upstream_rows, preferred_element_type=jnp.float32)
    mixed_change = jnp.einsum(
        "rld,ed->rle", upstream_rows, out_w, preferred_element_type=jnp.float32
    ).astype(jnp.bfloat16)

    def per_row(items):
        row_query, row_key, row_value, row_logsum, row_change, row_sq, row_sk = items
        heads_query = split_heads(row_query)
        heads_key = split_heads(row_key)
        heads_value = split_heads(row_value)
        heads_change = split_heads(row_change)
        scores = masked_scores(heads_query, heads_key, row_sq, row_sk, causal)
        exact = jnp.exp(scores - row_logsum)
        probs = exact.astype(jnp.bfloat16)
        probs_change = jnp.einsum(
            "qhd,khd->hqk", heads_change, heads_value, preferred_element_type=jnp.float32
        )
        value_change = jnp.einsum(
            "hqk,qhd->khd", probs, heads_change, preferred_element_type=jnp.float32
        )
        inner = jnp.sum(probs_change * exact, -1, keepdims=True)
        score_change = (exact * (probs_change - inner)).astype(jnp.bfloat16)
        query_change = jnp.einsum(
            "hqk,khd->qhd", score_change, heads_key, preferred_element_type=jnp.float32
        ) * HEAD_DIM ** (-0.5)
        key_change = jnp.einsum(
            "hqk,qhd->khd", score_change, heads_query, preferred_element_type=jnp.float32
        ) * HEAD_DIM ** (-0.5)
        row_shape = row_query.shape
        return (
            query_change.reshape(row_shape).astype(jnp.bfloat16),
            key_change.reshape(row_shape).astype(jnp.bfloat16),
            value_change.reshape(row_shape).astype(jnp.bfloat16),
        )

    query_change, key_change, value_change = lax.map(
        per_row, (query, keys, values, logsum, mixed_change, seg_query, seg_key)
    )
    weight_change = jnp.stack(
        [
            jnp.einsum("rld,rle->de", query_rows, query_change, preferred_element_type=jnp.float32),
            jnp.einsum("rld,rle->de", key_rows, key_change, preferred_element_type=jnp.float32),
            jnp.einsum("rld,rle->de", key_rows, value_change, preferred_element_type=jnp.float32),
        ]
    )
    from_query = jnp.einsum(
        "rle,de->rld", query_change, weights[0], preferred_element_type=jnp.float32
    )
    from_keys = jnp.einsum(
        "rle,de->rld", key_change, weights[1], preferred_element_type=jnp.float32
    )
    from_keys = from_keys + jnp.einsum(
        "rle,de->rld", value_change, weights[2], preferred_element_type=jnp.float32
    )
    return (from_query, from_keys, weight_change, out_change)


def expert_forward(rows, up_all, down_all, picks):
    up_pick = up_all[picks]
    down_pick = down_all[picks]
    hidden = jnp.einsum("rld,rdf->rlf", rows, up_pick, preferred_element_type=jnp.float32)
    active = jax.nn.gelu(hidden).astype(jnp.bfloat16)
    branch = jnp.einsum("rlf,rfd->rld", active, down_pick, preferred_element_type=jnp.float32)
    return (hidden, active, branch)


def expert_backward(rows, hidden, active, upstream_rows, up_all, down_all, picks):
    up_pick = up_all[picks]
    down_pick = down_all[picks]
    active_change = jnp.einsum(
        "rld,rfd->rlf", upstream_rows, down_pick, preferred_element_type=jnp.float32
    )
    unused, gelu_back = jax.vjp(jax.nn.gelu, hidden)
    hidden_change = gelu_back(active_change)[0].astype(jnp.bfloat16)
    rows_change = jnp.einsum(
        "rlf,rdf->rld", hidden_change, up_pick, preferred_element_type=jnp.float32
    )
    up_pick_change = jnp.einsum(
        "rld,rlf->rdf", rows, hidden_change, preferred_element_type=jnp.float32
    )
    down_pick_change = jnp.einsum(
        "rlf,rld->rfd", active, upstream_rows, preferred_element_type=jnp.float32
    )
    matches = picks[None, :] == jnp.arange(up_all.shape[0], dtype=jnp.int32)[:, None]
    up_change = jnp.sum(jnp.where(matches[:, :, None, None], up_pick_change[None], 0.0), 1)
    down_change = jnp.sum(jnp.where(matches[:, :, None, None], down_pick_change[None], 0.0), 1)
    return (rows_change, up_change, down_change)


def spread(values):
    return lax.all_gather(values, "seq", axis=1, tiled=True)


def fold(values):
    return lax.psum_scatter(values, "seq", scatter_dimension=1, tiled=True)


def spread_back(values):
    return lax.all_gather(values, "seq", axis=1, tiled=True)


def fold_back(values):
    return lax.psum_scatter(
        values.astype(jnp.bfloat16), "seq", scatter_dimension=1, tiled=True
    ).astype(jnp.float32)


def out_project(mixed, out_w):
    return jnp.einsum("rle,ed->rld", mixed, out_w, preferred_element_type=jnp.float32)


def squares(values):
    return jnp.sum(values * values, (1, 2))


def on_device(
    src_input,
    tgt_input,
    out_cotangent,
    src_lengths,
    tgt_lengths,
    enc_expert,
    dec_expert,
    norm_gains,
    norm_biases,
    qkv_weight,
    out_weight,
    expert_up,
    expert_down,
):
    gathered = (
        lax.all_gather(norm_gains, "dp", axis=1, tiled=True),
        lax.all_gather(norm_biases, "dp", axis=1, tiled=True),
        lax.all_gather(qkv_weight, "dp", axis=2, tiled=True),
        lax.all_gather(out_weight, "dp", axis=2, tiled=True),
        lax.all_gather(expert_up, "dp", axis=2, tiled=True),
        lax.all_gather(expert_down, "dp", axis=3, tiled=True),
    )
    gains_low, biases_low, projections, outputs, ups, downs = gathered
    gains = gains_low.astype(jnp.float32)
    shifts = biases_low.astype(jnp.float32)
    group = src_input.shape[1]
    width = src_input.shape[2]
    length = group * lax.axis_size("seq")
    src_doc = segment_ids(src_lengths, length)
    tgt_doc = segment_ids(tgt_lengths, length)
    enc_pick = enc_expert[:, 0]
    dec_pick = dec_expert[:, 0]
    source = src_input.astype(jnp.float32)
    target = tgt_input.astype(jnp.float32)
    rows_one = spread(normalize(source, gains[0], shifts[0]).astype(jnp.bfloat16))
    saved_one = attend_forward(rows_one, rows_one, projections[0], src_doc, src_doc, False)
    branch_one = fold(out_project(saved_one[3], outputs[0]))
    src_mid = source + branch_one
    rows_two = spread(normalize(src_mid, gains[1], shifts[1]).astype(jnp.bfloat16))
    hidden_two, active_two, branch = expert_forward(rows_two, ups[0], downs[0], enc_pick)
    branch_two = fold(branch)
    memory = src_mid + branch_two
    rows_three = spread(normalize(target, gains[2], shifts[2]).astype(jnp.bfloat16))
    saved_three = attend_forward(rows_three, rows_three, projections[1], tgt_doc, tgt_doc, True)
    branch_three = fold(out_project(saved_three[3], outputs[1]))
    tgt_one = target + branch_three
    normed_four = normalize(tgt_one, gains[3], shifts[3]).astype(jnp.bfloat16)
    rows_four, memory_rows = (
        lax.all_gather(normed_four, "seq", axis=1, tiled=True),
        lax.all_gather(memory.astype(jnp.bfloat16), "seq", axis=1, tiled=True),
    )
    saved_four = attend_forward(rows_four, memory_rows, projections[2], tgt_doc, src_doc, False)
    branch_four = fold(out_project(saved_four[3], outputs[2]))
    tgt_two = tgt_one + branch_four
    rows_five = spread(normalize(tgt_two, gains[4], shifts[4]).astype(jnp.bfloat16))
    hidden_five, active_five, branch = expert_forward(rows_five, ups[1], downs[1], dec_pick)
    branch_five = fold(branch)
    decoder_output = tgt_two + branch_five
    residual_squares = jnp.stack(
        [squares(source), squares(src_mid), squares(target), squares(tgt_one), squares(tgt_two)], 1
    )
    branch_squares = jnp.stack(
        [
            squares(branch_one),
            squares(branch_two),
            squares(branch_three),
            squares(branch_four),
            squares(branch_five),
        ],
        1,
    )
    stat_parts = jnp.stack([residual_squares, branch_squares], 1)
    gains_low, projections, outputs, ups, downs = (
        lax.all_gather(norm_gains, "dp", axis=1, tiled=True),
        lax.all_gather(qkv_weight, "dp", axis=2, tiled=True),
        lax.all_gather(out_weight, "dp", axis=2, tiled=True),
        lax.all_gather(expert_up, "dp", axis=2, tiled=True),
        lax.all_gather(expert_down, "dp", axis=3, tiled=True),
    )
    gains = gains_low.astype(jnp.float32)
    upstream = out_cotangent.astype(jnp.float32)
    gain_parts = [None] * 5
    bias_parts = [None] * 5
    upstream_rows = spread_back(upstream.astype(jnp.bfloat16))
    rows_change, up_dec, down_dec = expert_backward(
        rows_five, hidden_five, active_five, upstream_rows, ups[1], downs[1], dec_pick
    )
    input_change, gain_parts[4], bias_parts[4] = norm_backward(
        tgt_two, gains[4], shifts[4], fold_back(rows_change)
    )
    upstream = upstream + input_change
    upstream_rows = spread_back(upstream.astype(jnp.bfloat16))
    from_query, from_keys, cross_change, cross_out = attend_backward(
        saved_four,
        rows_four,
        memory_rows,
        upstream_rows,
        projections[2],
        outputs[2],
        tgt_doc,
        src_doc,
        False,
    )
    query_sum, memory_change = (
        lax.psum_scatter(
            from_query.astype(jnp.bfloat16), "seq", scatter_dimension=1, tiled=True
        ).astype(jnp.float32),
        lax.psum_scatter(
            from_keys.astype(jnp.bfloat16), "seq", scatter_dimension=1, tiled=True
        ).astype(jnp.float32),
    )
    input_change, gain_parts[3], bias_parts[3] = norm_backward(
        tgt_one, gains[3], shifts[3], query_sum
    )
    upstream = upstream + input_change
    upstream_rows = spread_back(upstream.astype(jnp.bfloat16))
    from_query, from_keys, self_change, self_out = attend_backward(
        saved_three,
        rows_three,
        rows_three,
        upstream_rows,
        projections[1],
        outputs[1],
        tgt_doc,
        tgt_doc,
        True,
    )
    input_change, gain_parts[2], bias_parts[2] = norm_backward(
        target, gains[2], shifts[2], fold_back(from_query + from_keys)
    )
    tgt_grad = upstream + input_change
    upstream = memory_change
    upstream_rows = spread_back(upstream.astype(jnp.bfloat16))
    rows_change, up_enc, down_enc = expert_backward(
        rows_two, hidden_two, active_two, upstream_rows, ups[0], downs[0], enc_pick
    )
    input_change, gain_parts[1], bias_parts[1] = norm_backward(
        src_mid, gains[1], shifts[1], fold_back(rows_change)
    )
    upstream = upstream + input_change
    upstream_rows = spread_back(upstream.astype(jnp.bfloat16))
    from_query, from_keys, enc_change, enc_out = attend_backward(
        saved_one,
        rows_one,
        rows_one,
        upstream_rows,
        projections[0],
        outputs[0],
        src_doc,
        src_doc,
        False,
    )
    input_change, gain_parts[0], bias_parts[0] = norm_backward(
        source, gains[0], shifts[0], fold_back(from_query + from_keys)
    )
    src_grad = upstream + input_change
    gain_total, bias_total, stat_total = lax.psum(
        (jnp.stack(gain_parts), jnp.stack(bias_parts), stat_parts), "seq"
    )
    sublayer_rms = jnp.sqrt(stat_total / (length * width))
    qkv_local = jnp.stack([enc_change, self_change, cross_change])
    out_local = jnp.stack([enc_out, self_out, cross_out])
    up_local = jnp.stack([up_enc, up_dec])
    down_local = jnp.stack([down_enc, down_dec])
    owned = (
        lax.psum_scatter(gain_total, "dp", scatter_dimension=1, tiled=True),
        lax.psum_scatter(bias_total, "dp", scatter_dimension=1, tiled=True),
        lax.psum_scatter(qkv_local, "dp", scatter_dimension=2, tiled=True),
        lax.psum_scatter(out_local, "dp", scatter_dimension=2, tiled=True),
        lax.psum_scatter(up_local, "dp", scatter_dimension=2, tiled=True),
        lax.psum_scatter(down_local, "dp", scatter_dimension=3, tiled=True),
    )
    return (
        decoder_output,
        src_grad,
        tgt_grad,
        owned[0],
        owned[1],
        owned[2],
        owned[3],
        owned[4],
        owned[5],
        sublayer_rms,
    )


def solution(mesh):
    placed = (
        P("dp", "seq", None),
        P("dp", "seq", None),
        P("dp", "seq", None),
        P("dp", None),
        P("dp", None),
        P("dp", None),
        P("dp", None),
        P(None, "dp"),
        P(None, "dp"),
        P(None, None, "dp", "seq"),
        P(None, "seq", "dp"),
        P(None, None, "dp", "seq"),
        P(None, None, "seq", "dp"),
    )
    return jax.shard_map(
        on_device,
        mesh=mesh,
        in_specs=placed,
        out_specs=(
            P("dp", "seq", None),
            P("dp", "seq", None),
            P("dp", "seq", None),
            P(None, "dp"),
            P(None, "dp"),
            P(None, None, "dp", "seq"),
            P(None, "seq", "dp"),
            P(None, None, "dp", "seq"),
            P(None, None, "seq", "dp"),
            P("dp", None, None),
        ),
        check_vma=False,
    )
```

profile of v0, /device:TPU:28, one launch (start us, length us, event | category | flops | bytes accessed | tf_op | source)
XLA Modules:
  0.0 1425.3 jit_solution(10939392273124229171)
XLA Ops:
  7.3 22.6 %all-gather.1 = bf16[8,64,5]{1,2,0:T(8,128)(2,1)S(1)} all-gather(bf16[1,64,5]{1,2,0:T(8,128)(2,1)} %bitcast.479), channel_id=1, replica_groups=mesh['dp'=8,'seq'=4] {'dp'}, dimensions={0}, use_global_device_ids=true | all-gather | bytes 5760 | tf_op jit(solution)/shard_map/all_gather | solution.py:207
  29.9 26.1 %all-gather = bf16[8,64,5]{1,2,0:T(8,128)(2,1)S(1)} all-gather(bf16[1,64,5]{1,2,0:T(8,128)(2,1)} %bitcast.480), channel_id=1, replica_groups=mesh['dp'=8,'seq'=4] {'dp'}, dimensions={0}, use_global_device_ids=true | all-gather | bytes 5760 | tf_op jit(solution)/shard_map/all_gather | solution.py:206
  64.1 32.1 %all_gather.60 = bf16[3,128,512]{1,2,0:T(8,128)(2,1)S(1)} all-gather(bf16[3,128,64]{1,2,0:T(8,128)(2,1)S(1)} %copy-done.70), channel_id=1, replica_groups=mesh['dp'=8,'seq'=4] {'dp'}, dimensions={2}, use_global_device_ids=true | all-gather | bytes 442368 | tf_op jit(solution)/shard_map/all_gather | solution.py:209
  99.1 21.6 %all-gather.19.cloned.1.call-done = bf16[3,3,512,128]{3,2,1,0:T(8,128)(2,1)} async-done(((bf16[3,3,64,128]{3,2,1,0:T(8,128)(2,1)}), bf16[3,3,512,128]{3,2,1,0:T(8,128)(2,1)}) %all-gather.19.cloned.1.call-update) | async-done | bytes 1179664 | tf_op jit(solution)/shard_map/all_gather | solution.py:208
  134.4 4.3 all-gather.17.cloned.1.call-done
  142.3 5.1 fusion.186
  147.4 25.2 %reduce-scatter.25.cloned.1.call-done = f32[1,256,512]{2,1,0:T(8,128)} async-done(((f32[1,1024,512]{2,1,0:T(8,128)}), f32[1,256,512]{2,1,0:T(8,128)}) %reduce-scatter.25.cloned.1.call-update) | async-done | bytes 524304 | tf_op jit(solution)/shard_map/reduce_scatter | solution.py:169
  175.8 4.7 fusion
  186.1 61.3 %all-gather.27.cloned.1.call-done = bf16[2,4,512,512]{2,3,1,0:T(8,128)(2,1)} async-done(((bf16[2,4,512,64]{2,3,1,0:T(8,128)(2,1)}), bf16[2,4,512,512]{2,3,1,0:T(8,128)(2,1)}) %all-gather.27.cloned.1.call-update) | async-done | bytes 4194320 | tf_op jit(solution)/shard_map/all_gather | solution.py:211
  247.4 4.4 fusion.183
  251.8 69.5 %all-gather.25.cloned.1.call-done = bf16[2,4,512,512]{3,2,1,0:T(8,128)(2,1)} async-done(((bf16[2,4,64,512]{3,2,1,0:T(8,128)(2,1)}), bf16[2,4,512,512]{3,2,1,0:T(8,128)(2,1)}) %all-gather.25.cloned.1.call-update) | async-done | bytes 4194320 | tf_op jit(solution)/shard_map/all_gather | solution.py:210
  321.4 4.5 fusion.182
  325.8 13.6 all-gather.23.cloned.1.call-done
  346.2 27.4 %reduce-scatter.23.cloned.1.call-done = f32[1,256,512]{2,1,0:T(8,128)} async-done(((f32[1,1024,512]{2,1,0:T(8,128)}), f32[1,256,512]{2,1,0:T(8,128)}) %reduce-scatter.23.cloned.1.call-update) | async-done | bytes 524304 | tf_op jit(solution)/shard_map/reduce_scatter | solution.py:169
  376.5 31.0 %reduce-scatter.27.cloned.1.call-done = f32[1,256,512]{2,1,0:T(8,128)} async-done(((f32[1,1024,512]{2,1,0:T(8,128)}), f32[1,256,512]{2,1,0:T(8,128)}) %reduce-scatter.27.cloned.1.call-update) | async-done | bytes 524304 | tf_op jit(solution)/shard_map/reduce_scatter | solution.py:169
  410.1 16.3 %all-gather.31.cloned.1.call-done = bf16[1,1024,512]{2,1,0:T(8,128)(2,1)} async-done(((bf16[1,256,512]{2,1,0:T(8,128)(2,1)}), bf16[1,1024,512]{2,1,0:T(8,128)(2,1)}) %all-gather.31.cloned.1.call-update) | async-done | bytes 1048592 | tf_op jit(solution)/shard_map/all_gather | solution.py:239
  428.1 17.3 %all-gather.29.cloned.1.call-done = bf16[1,1024,512]{2,1,0:T(8,128)(2,1)} async-done(((bf16[1,256,512]{2,1,0:T(8,128)(2,1)}), bf16[1,1024,512]{2,1,0:T(8,128)(2,1)}) %all-gather.29.cloned.1.call-update) | async-done | bytes 1048592 | tf_op jit(solution)/shard_map/all_gather | solution.py:240
  458.9 31.5 %reduce-scatter.29.cloned.1.call-done = f32[1,256,512]{2,1,0:T(8,128)} async-done(((f32[1,1024,512]{2,1,0:T(8,128)}), f32[1,256,512]{2,1,0:T(8,128)}) %reduce-scatter.29.cloned.1.call-update) | async-done | bytes 524304 | tf_op jit(solution)/shard_map/reduce_scatter | solution.py:169
  495.6 15.2 %all-gather.33.cloned.1.call-done = bf16[1,1024,512]{2,1,0:T(8,128)(2,1)} async-done(((bf16[1,256,512]{2,1,0:T(8,128)(2,1)}), bf16[1,1024,512]{2,1,0:T(8,128)(2,1)}) %all-gather.33.cloned.1.call-update) | async-done | bytes 1048592 | tf_op jit(solution)/shard_map/all_gather | solution.py:165
  514.1 14.8 %all-gather.35.cloned.1.call-done = bf16[1,1024,512]{2,1,0:T(8,128)(2,1)} async-done(((bf16[1,256,512]{2,1,0:T(8,128)(2,1)}), bf16[1,1024,512]{2,1,0:T(8,128)(2,1)}) %all-gather.35.cloned.1.call-update) | async-done | bytes 1048592 | tf_op jit(solution)/shard_map/all_gather | solution.py:173
  528.9 3.9 fusion.32
  536.7 3.9 convolution_bitcast_fusion
  540.7 21.0 %reduce-scatter.33.cloned.1.call-done = bf16[1,256,512]{2,1,0:T(8,128)(2,1)} async-done(((bf16[1,1024,512]{2,1,0:T(8,128)(2,1)}), bf16[1,256,512]{2,1,0:T(8,128)(2,1)}) %reduce-scatter.33.cloned.1.call-update) | async-done | bytes 262160 | tf_op jit(solution)/shard_map/reduce_scatter | solution.py:177
  563.8 31.9 %reduce-scatter.31.cloned.1.call-done = f32[1,256,512]{2,1,0:T(8,128)} async-done(((f32[1,1024,512]{2,1,0:T(8,128)}), f32[1,256,512]{2,1,0:T(8,128)}) %reduce-scatter.31.cloned.1.call-update) | async-done | bytes 524304 | tf_op jit(solution)/shard_map/reduce_scatter | solution.py:169
  600.4 16.8 %all-gather.37.cloned.1.call-done = bf16[1,1024,512]{2,1,0:T(8,128)(2,1)} async-done(((bf16[1,256,512]{2,1,0:T(8,128)(2,1)}), bf16[1,1024,512]{2,1,0:T(8,128)(2,1)}) %all-gather.37.cloned.1.call-update) | async-done | bytes 1048592 | tf_op jit(solution)/shard_map/all_gather | solution.py:173
  619.0 5.4 multiply_reduce_fusion.2
  634.9 25.0 %reduce-scatter.35.cloned.1.call-done = bf16[1,256,512]{2,1,0:T(8,128)(2,1)} async-done(((bf16[1,1024,512]{2,1,0:T(8,128)(2,1)}), bf16[1,256,512]{2,1,0:T(8,128)(2,1)}) %reduce-scatter.35.cloned.1.call-update) | async-done | bytes 262160 | tf_op jit(solution)/shard_map/reduce_scatter | solution.py:298
  666.4 11.9 all-gather.39.cloned.1.call-done
  686.0 20.3 %reduce-scatter.41.cloned.1.call-done = bf16[1,256,512]{2,1,0:T(8,128)(2,1)} async-done(((bf16[1,1024,512]{2,1,0:T(8,128)(2,1)}), bf16[1,256,512]{2,1,0:T(8,128)(2,1)}) %reduce-scatter.41.cloned.1.call-update) | async-done | bytes 262160 | tf_op jit(solution)/shard_map/reduce_scatter | solution.py:295
  708.2 26.2 %reduce-scatter.37.cloned.1.call-done = bf16[1,256,512]{2,1,0:T(8,128)(2,1)} async-done(((bf16[1,1024,512]{2,1,0:T(8,128)(2,1)}), bf16[1,256,512]{2,1,0:T(8,128)(2,1)}) %reduce-scatter.37.cloned.1.call-update) | async-done | bytes 262160 | tf_op jit(solution)/shard_map/reduce_scatter | solution.py:177
  739.7 4.0 fusion.72
  745.0 11.5 all-gather.41.cloned.1.call-done
  758.2 5.4 multiply_reduce_fusion.1
  777.7 5.3 multiply_reduce_fusion
  798.2 4.4 broadcast_select_fusion
  813.0 18.6 %reduce-scatter.43.cloned.1.call-done = bf16[1,256,512]{2,1,0:T(8,128)(2,1)} async-done(((bf16[1,1024,512]{2,1,0:T(8,128)(2,1)}), bf16[1,256,512]{2,1,0:T(8,128)(2,1)}) %reduce-scatter.43.cloned.1.call-update) | async-done | bytes 262160 | tf_op jit(solution)/shard_map/reduce_scatter | solution.py:177
  837.5 6.0 broadcast_select_fusion.1
  844.5 7.7 pad_maximum_fusion
  852.2 10.3 copy.146
  862.5 10.9 reshape.1206
  882.2 7.7 pad_maximum_fusion.1
  895.0 18.1 %all-reduce.4.cloned.1.call-done = f32[3,128,512]{1,0,2:T(4,128)} async-done(((f32[3,128,512]{1,0,2:T(4,128)}), f32[3,128,512]{1,0,2:T(4,128)}) %all-reduce.4.cloned.1.call-update) | async-done | bytes 786448
  920.1 57.7 %reduce-scatter.51.cloned.1.call-done = f32[64,5]{1,0:T(8,128)} async-done(((f32[512,5]{1,0:T(8,128)}), f32[64,5]{1,0:T(8,128)}) %reduce-scatter.51.cloned.1.call-update) | async-done | bytes 1296
  978.6 62.7 %reduce-scatter.53.cloned.1.call-done = f32[64,5]{1,0:T(8,128)} async-done(((f32[512,5]{1,0:T(8,128)}), f32[64,5]{1,0:T(8,128)}) %reduce-scatter.53.cloned.1.call-update) | async-done | bytes 1296
  1042.2 6.7 all-reduce.1
  1049.5 142.7 %reduce-scatter.49.cloned.1.call-done = f32[64,4096]{1,0:T(8,128)} async-done(((f32[512,4096]{1,0:T(8,128)}), f32[64,4096]{1,0:T(8,128)}) %reduce-scatter.49.cloned.1.call-update) | async-done | bytes 1048592
  1195.7 70.0 %reduce-scatter.45.cloned.1.call-done = f32[3,3,64,128]{3,2,1,0:T(8,128)} async-done(((f32[3,3,512,128]{3,2,1,0:T(8,128)}), f32[3,3,64,128]{3,2,1,0:T(8,128)}) %reduce-scatter.45.cloned.1.call-update) | async-done | bytes 294928 | tf_op jit(solution)/shard_map/reduce_scatter | solution.py:358
  1265.7 152.3 %reduce-scatter.47.cloned.1.call-done = f32[2,4,512,64]{2,3,1,0:T(8,128)} async-done(((f32[2,4,512,512]{2,3,1,0:T(8,128)}), f32[2,4,512,64]{2,3,1,0:T(8,128)}) %reduce-scatter.47.cloned.1.call-update) | async-done | bytes 1048592 | tf_op jit(solution)/shard_map/reduce_scatter | solution.py:361
  (411 shorter events, 189.8 us)
Async XLA Ops:
  7.2 55.1 %copy-start.9 = (bf16[1,256,512]{2,1,0:T(8,128)(2,1)S(1)}, bf16[1,256,512]{2,1,0:T(8,128)(2,1)}, u32[]{:S(2)}) copy-start(bf16[1,256,512]{2,1,0:T(8,128)(2,1)} %param.14) | copy-start | bytes 786436
  7.2 56.3 %copy-start.84 = (s32[1,4]{1,0:T(1,128)S(1)}, s32[1,4]{1,0:T(1,128)}, u32[]{:S(2)}) copy-start(s32[1,4]{1,0:T(1,128)} %param.17) | copy-start | bytes 52
  7.2 56.5 %copy-start.85 = (s32[1,4]{1,0:T(1,128)S(1)}, s32[1,4]{1,0:T(1,128)}, u32[]{:S(2)}) copy-start(s32[1,4]{1,0:T(1,128)} %param.16) | copy-start | bytes 52
  7.2 56.8 %copy-start.70 = (bf16[3,128,64]{1,2,0:T(8,128)(2,1)S(1)}, bf16[3,128,64]{1,2,0:T(8,128)(2,1)}, u32[]{:S(2)}) copy-start(bf16[3,128,64]{1,2,0:T(8,128)(2,1)} %param.23) | copy-start | bytes 147460
  7.2 91.9 %all-gather.21.cloned.1.call-start = ((), (), s32[]{:S(2)}) async-start(), calls=%async_computation.19 | async-start | bytes 1310720 | tf_op jit(solution)/shard_map/all_gather | solution.py:165
  56.2 42.9 %copy-start.68 = (f32[1,512]{1,0:T(1,128)}, f32[1,512]{1,0:T(1,128)S(1)}, u32[]{:S(2)}) copy-start(f32[1,512]{1,0:T(1,128)S(1)} %get-tuple-element.315) | copy-start | bytes 6148
  57.3 41.8 %copy-start.71 = (f32[256]{0:T(256)}, f32[256]{0:T(256)S(1)}, u32[]{:S(2)}) copy-start(f32[256]{0:T(256)S(1)} %broadcast_multiply_fusion.3) | copy-start | bytes 3076
  58.5 40.6 %copy-start.75 = (f32[256]{0:T(256)}, f32[256]{0:T(256)S(1)}, u32[]{:S(2)}) copy-start(f32[256]{0:T(256)S(1)} %fusion.171) | copy-start | bytes 3076
  60.4 60.4 %all-gather.19.cloned.1.call-start = ((), (), s32[]{:S(2)}) async-start(), calls=%async_computation.17 | async-start | bytes 1327104 | tf_op jit(solution)/shard_map/all_gather | solution.py:208
  61.1 77.6 %all-gather.17.cloned.1.call-start = ((), (), s32[]{:S(2)}) async-start(), calls=%async_computation.16 | async-start | bytes 1310720 | tf_op jit(solution)/shard_map/all_gather | solution.py:165
  62.3 36.8 %copy-start.73 = (f32[256]{0:T(256)}, f32[256]{0:T(256)S(1)}, u32[]{:S(2)}) copy-start(f32[256]{0:T(256)S(1)} %broadcast_multiply_fusion.4) | copy-start | bytes 3076
  63.4 109.1 %reduce-scatter.25.cloned.1.call-start = ((), (), s32[]{:S(2)}) async-start(), calls=%async_computation.20 | async-start | bytes 2621440 | tf_op jit(solution)/shard_map/reduce_scatter | solution.py:169
  96.2 87.4 %copy-start.24 = (bf16[3,128,512]{1,2,0:T(8,128)(2,1)}, bf16[3,128,512]{1,2,0:T(8,128)(2,1)S(1)}, u32[]{:S(2)}) copy-start(bf16[3,128,512]{1,2,0:T(8,128)(2,1)S(1)} %all_gather.60) | copy-start | bytes 1179652
  133.2 114.2 %all-gather.27.cloned.1.call-start = ((), (), s32[]{:S(2)}) async-start(), calls=%async_computation.23 | async-start | bytes 4718592 | tf_op jit(solution)/shard_map/all_gather | solution.py:211
  133.8 187.6 %all-gather.25.cloned.1.call-start = ((), (), s32[]{:S(2)}) async-start(), calls=%async_computation.22 | async-start | bytes 4718592 | tf_op jit(solution)/shard_map/all_gather | solution.py:210
  134.4 205.1 %all-gather.23.cloned.1.call-start = ((), (), s32[]{:S(2)}) async-start(), calls=%async_computation.21 | async-start | bytes 1310720 | tf_op jit(solution)/shard_map/all_gather | solution.py:165
  142.3 30.3 %copy-start.10 = (bf16[1,256,512]{2,1,0:T(8,128)(2,1)S(1)}, bf16[1,256,512]{2,1,0:T(8,128)(2,1)}, u32[]{:S(2)}) copy-start(bf16[1,256,512]{2,1,0:T(8,128)(2,1)} %param.13) | copy-start | bytes 786436
  175.6 198.0 %reduce-scatter.23.cloned.1.call-start = ((), (), s32[]{:S(2)}) async-start(), calls=%async_computation.18 | async-start | bytes 2621440 | tf_op jit(solution)/shard_map/reduce_scatter | solution.py:169
  185.4 222.2 %reduce-scatter.27.cloned.1.call-start = ((), (), s32[]{:S(2)}) async-start(), calls=%async_computation.24 | async-start | bytes 2621440 | tf_op jit(solution)/shard_map/reduce_scatter | solution.py:169
  346.1 80.3 %all-gather.31.cloned.1.call-start = ((), (), s32[]{:S(2)}) async-start(), calls=%async_computation.26 | async-start | bytes 1310720 | tf_op jit(solution)/shard_map/all_gather | solution.py:239
  376.5 68.9 %all-gather.29.cloned.1.call-start = ((), (), s32[]{:S(2)}) async-start(), calls=%async_computation.25 | async-start | bytes 1310720 | tf_op jit(solution)/shard_map/all_gather | solution.py:240
  410.1 80.4 %reduce-scatter.29.cloned.1.call-start = ((), (), s32[]{:S(2)}) async-start(), calls=%async_computation.27 | async-start | bytes 2621440 | tf_op jit(solution)/shard_map/reduce_scatter | solution.py:169
  458.8 51.9 %all-gather.33.cloned.1.call-start = ((), (), s32[]{:S(2)}) async-start(), calls=%async_computation.28 | async-start | bytes 1310720 | tf_op jit(solution)/shard_map/all_gather | solution.py:165
  493.9 35.1 %all-gather.35.cloned.1.call-start = ((), (), s32[]{:S(2)}) async-start(), calls=%async_computation.30 | async-start | bytes 1310720 | tf_op jit(solution)/shard_map/all_gather | solution.py:173
  494.5 67.2 %reduce-scatter.33.cloned.1.call-start = ((), (), s32[]{:S(2)}) async-start(), calls=%async_computation.31 | async-start | bytes 1310720 | tf_op jit(solution)/shard_map/reduce_scatter | solution.py:177
  536.6 59.1 %reduce-scatter.31.cloned.1.call-start = ((), (), s32[]{:S(2)}) async-start(), calls=%async_computation.29 | async-start | bytes 2621440 | tf_op jit(solution)/shard_map/reduce_scatter | solution.py:169
  540.6 76.6 %all-gather.37.cloned.1.call-start = ((), (), s32[]{:S(2)}) async-start(), calls=%async_computation.32 | async-start | bytes 1310720 | tf_op jit(solution)/shard_map/all_gather | solution.py:173
  600.3 59.6 %reduce-scatter.35.cloned.1.call-start = ((), (), s32[]{:S(2)}) async-start(), calls=%async_computation.33 | async-start | bytes 1310720 | tf_op jit(solution)/shard_map/reduce_scatter | solution.py:298
  634.8 43.4 %all-gather.39.cloned.1.call-start = ((), (), s32[]{:S(2)}) async-start(), calls=%async_computation.34 | async-start | bytes 1310720 | tf_op jit(solution)/shard_map/all_gather | solution.py:173
  659.9 46.4 %reduce-scatter.41.cloned.1.call-start = ((), (), s32[]{:S(2)}) async-start(), calls=%async_computation.38 | async-start | bytes 1310720 | tf_op jit(solution)/shard_map/reduce_scatter | solution.py:295
  666.2 68.2 %reduce-scatter.37.cloned.1.call-start = ((), (), s32[]{:S(2)}) async-start(), calls=%async_computation.35 | async-start | bytes 1310720 | tf_op jit(solution)/shard_map/reduce_scatter | solution.py:177
  686.0 70.5 %all-gather.41.cloned.1.call-start = ((), (), s32[]{:S(2)}) async-start(), calls=%async_computation.36 | async-start | bytes 1310720 | tf_op jit(solution)/shard_map/all_gather | solution.py:173
  739.6 36.4 %all-gather.43.cloned.1.call-start = ((), (), s32[]{:S(2)}) async-start(), calls=%async_computation.39 | async-start | bytes 1310720 | tf_op jit(solution)/shard_map/all_gather | solution.py:173
  744.9 66.8 %reduce-scatter.39.cloned.1.call-start = ((), (), s32[]{:S(2)}) async-start(), calls=%async_computation.37 | async-start | bytes 1310720 | tf_op jit(solution)/shard_map/reduce_scatter | solution.py:177
  775.6 55.9 %reduce-scatter.43.cloned.1.call-start = ((), (), s32[]{:S(2)}) async-start(), calls=%async_computation.40 | async-start | bytes 1310720 | tf_op jit(solution)/shard_map/reduce_scatter | solution.py:177
  795.6 117.4 %all-reduce.4.cloned.1.call-start = ((), (), s32[]{:S(2)}) async-start(), calls=%async_computation.46 | async-start | bytes 2097152
  808.9 25.7 %copy-start.82 = (f32[256]{0:T(256)S(1)}, f32[256]{0:T(256)}, u32[]{:S(2)}) copy-start(f32[256]{0:T(256)} %copy-done.81) | copy-start | bytes 3076
  808.9 25.7 %copy-start.78 = (f32[256]{0:T(256)S(1)}, f32[256]{0:T(256)}, u32[]{:S(2)}) copy-start(f32[256]{0:T(256)} %copy-done.77) | copy-start | bytes 3076
  811.4 166.4 %reduce-scatter.51.cloned.1.call-start = ((), (), s32[]{:S(2)}) async-start(), calls=%async_computation.44 | async-start | bytes 294912
  837.5 203.9 %reduce-scatter.53.cloned.1.call-start = ((), (), s32[]{:S(2)}) async-start(), calls=%async_computation.45 | async-start | bytes 294912
  844.5 347.7 %reduce-scatter.49.cloned.1.call-start = ((), (), s32[]{:S(2)}) async-start(), calls=%async_computation.43 | async-start | bytes 9437184
  873.5 392.2 %reduce-scatter.45.cloned.1.call-start = ((), (), s32[]{:S(2)}) async-start(), calls=%async_computation.41 | async-start | bytes 2654208 | tf_op jit(solution)/shard_map/reduce_scatter | solution.py:358
  882.1 535.9 %reduce-scatter.47.cloned.1.call-start = ((), (), s32[]{:S(2)}) async-start(), calls=%async_computation.42 | async-start | bytes 9437184 | tf_op jit(solution)/shard_map/reduce_scatter | solution.py:361
  889.9 28.1 %copy-start.47 = (bf16[1,256,512]{2,1,0:T(8,128)(2,1)S(1)}, bf16[1,256,512]{2,1,0:T(8,128)(2,1)}, u32[]{:S(2)}) copy-start(bf16[1,256,512]{2,1,0:T(8,128)(2,1)} %reduce-scatter.43.cloned.1.call-done) | copy-start | bytes 786436
  889.9 28.1 %copy-start.48 = (f32[1,256,512]{2,1,0:T(8,128)S(1)}, f32[1,256,512]{2,1,0:T(8,128)}, u32[]{:S(2)}) copy-start(f32[1,256,512]{2,1,0:T(8,128)} %get-tuple-element.288) | copy-start | bytes 1572868
  889.9 29.2 %copy-start.15 = (f32[1,256,512]{2,1,0:T(8,128)S(1)}, f32[1,256,512]{2,1,0:T(8,128)}, u32[]{:S(2)}) copy-start(f32[1,256,512]{2,1,0:T(8,128)} %copy-done.14) | copy-start | bytes 1572868
  889.9 29.1 %copy-start.45 = (bf16[1,256,512]{2,1,0:T(8,128)(2,1)S(1)}, bf16[1,256,512]{2,1,0:T(8,128)(2,1)}, u32[]{:S(2)}) copy-start(bf16[1,256,512]{2,1,0:T(8,128)(2,1)} %reduce-scatter.35.cloned.1.call-done) | copy-start | bytes 786436
  889.9 29.1 %copy-start.46 = (bf16[1,256,512]{2,1,0:T(8,128)(2,1)S(1)}, bf16[1,256,512]{2,1,0:T(8,128)(2,1)}, u32[]{:S(2)}) copy-start(bf16[1,256,512]{2,1,0:T(8,128)(2,1)} %reduce-scatter.39.cloned.1.call-done) | copy-start | bytes 786436
  (79 other events, 332.3 us)
Sparse Core Ops, SparseCore 0:
  60.5 17.1 all-gather.20
  79.9 40.7 all-gather.18
  122.9 15.7 all-gather.16
  141.1 31.4 reduce-scatter.24
  174.8 72.5 all-gather.26
  249.7 71.6 all-gather.24
  323.6 15.8 all-gather.22
  342.1 31.4 reduce-scatter.22
  376.1 31.4 reduce-scatter.26
  409.6 16.7 all-gather.30
  428.6 16.7 all-gather.28
  459.0 31.4 reduce-scatter.28
  494.0 16.7 all-gather.32
  512.2 16.7 all-gather.34
  536.7 24.8 reduce-scatter.32
  564.2 31.4 reduce-scatter.30
  600.4 16.7 all-gather.36
  635.0 24.8 reduce-scatter.34
  661.5 16.7 all-gather.38
  681.4 24.8 reduce-scatter.40
  709.4 24.8 reduce-scatter.36
  739.7 16.7 all-gather.40
  758.7 16.7 all-gather.42
  778.5 24.9 reduce-scatter.38
  806.6 24.8 reduce-scatter.42
  835.3 77.7 all-reduce.3
  916.8 60.9 reduce-scatter.50
  981.1 60.2 reduce-scatter.52
  1045.0 147.1 reduce-scatter.48
  1196.5 69.1 reduce-scatter.44
  1270.4 147.6 reduce-scatter.46
where the time goes:
time: 1440 us; the launch traced here: 1430 us
  waiting for transfers between devices  1040 us (72%)
  matrix products  130 us (9%)
  blocking collectives  87.5 us (6%)
  other arithmetic  86.2 us (6%)
  local copies, waits for them, and re-layouts  61.5 us (4%)
  between operations  18.5 us (1%)
    unnamed x35, waiting for transfers between devices  284 us
    reduce_scatter x1, waiting for transfers between devices, on_device(): lax.psum_scatter(down_local, 'dp', scatter_dimension=3, tiled=True)  152 us
    reduce_scatter x5, waiting for transfers between devices, fold(): return lax.psum_scatter(values, 'seq', scatter_dimension=1, tiled=True)  147 us
    reduce_scatter x1, waiting for transfers between devices, on_device(): lax.psum_scatter(qkv_local, 'dp', scatter_dimension=2, tiled=True)  70 us
    all_gather x1, waiting for transfers between devices, on_device(): lax.all_gather(expert_up, 'dp', axis=2, tiled=True)  69.5 us
    reduce_scatter x4, waiting for transfers between devices, fold_back(): lax.psum_scatter(values.astype(jnp.bfloat16), 'seq', scatter_dimension=1,...  65.8 us
    all_gather x1, waiting for transfers between devices, on_device(): lax.all_gather(expert_down, 'dp', axis=3, tiled=True)  61.3 us
    all_gather x5, waiting for transfers between devices, spread_back(): return lax.all_gather(values, 'seq', axis=1, tiled=True)  55 us
  transfers between devices with their start and end apart: 31, of which 28 were waited for; matrix products, arithmetic and copies ran while one was open for 15% of the time, Pallas kernels for 0%

commit v1 on v0

v1 whole, which is shorter than its diff:
```python
import functools
import math
from types import SimpleNamespace

import jax
import jax.numpy as jnp
from jax import lax
from jax.experimental import pallas as pl
from jax.experimental.pallas import tpu as pltpu
from jax.sharding import PartitionSpec as P

HEAD_DIM = 64
EPSILON = 1e-05
MASKED = -1e30
LANES = 128
F32 = jnp.float32
BF16 = jnp.bfloat16
MESH = pl.DeviceIdType.MESH
GELU_A = math.sqrt(2.0 / math.pi)
GELU_B = 0.044715


def mm(a, b):
    return lax.dot_general(a, b, (((1,), (0,)), ((), ())), preferred_element_type=F32)


def mm_nt(a, b):
    return lax.dot_general(a, b, (((1,), (1,)), ((), ())), preferred_element_type=F32)


def mm_tn(a, b):
    return lax.dot_general(a, b, (((0,), (0,)), ((), ())), preferred_element_type=F32)


def centre(x):
    mean = jnp.mean(x, -1, keepdims=True)
    xc = x - mean
    var = jnp.mean(xc * xc, -1, keepdims=True)
    scale = lax.rsqrt(var + EPSILON)
    return xc * scale, scale


def norm(x, gain, shift):
    return centre(x)[0] * gain + shift


def norm_back(x, gain, up):
    xh, scale = centre(x)
    dgain = jnp.sum(up * xh, 0, keepdims=True)
    dbias = jnp.sum(up, 0, keepdims=True)
    dxh = up * gain
    m1 = jnp.mean(dxh, -1, keepdims=True)
    m2 = jnp.mean(dxh * xh, -1, keepdims=True)
    return scale * (dxh - m1 - xh * m2), dgain, dbias


def gelu_pair(x):
    square = x * x
    t = jnp.tanh(x * (GELU_A + (GELU_A * GELU_B) * square))
    half = 0.5 + 0.5 * t
    slope = half + (0.5 * x) * (1.0 - t * t) * (GELU_A + (3.0 * GELU_A * GELU_B) * square)
    return x * half, slope


def scratch_list(n, nb, cw, B, D, FQ):
    L, F2, KW = 4 * B, 2 * FQ, 2 * LANES

    def b(*shape):
        return pltpu.VMEM(shape, BF16)

    def f(*shape):
        return pltpu.VMEM(shape, F32)

    return dict(
        xrow=b(L, D),
        oth=b(B, D),
        nrow=b(L, D),
        wself=b(2, 4, D, KW),
        wx=b(4, D, KW),
        we0=b(2, D, F2),
        we1=b(2, D, F2),
        sendA=b(3, 4, cw, LANES),
        gtab=f(16, D),
        smallr=f(nb, 16, LANES),
        q=b(L, KW),
        k=b(L, KW),
        v=b(L, KW),
        o=b(L, KW),
        lseT=f(8, L),
        bias=f(B, L),
        biasT=f(L, B),
        part=f(2, B, D),
        cs=b(2, B, D),
        cr=b(2, B, D),
        mid=f(2, B, D),
        n2row=b(L, D),
        g0=b(L, F2),
        gp0=b(L, F2),
        mrow=b(L, D),
        fs=b(B, D),
        fr=b(B, D),
        t1=f(B, D),
        n4c=b(2 * B, D),
        q2=b(2 * B, KW),
        k2=b(L, KW),
        v2=b(L, KW),
        o2=b(2 * B, KW),
        lse2T=f(8, 2 * B),
        ds=b(B, D),
        dr=b(2, B, D),
        t2=f(B, D),
        n5c=b(2 * B, D),
        g1=b(2 * B, F2),
        gp1=b(2 * B, F2),
        b5c=b(2 * B, D),
        g4=f(B, D),
        b4c=b(2 * B, D),
        dqf=f(B, KW),
        dkf=f(L, KW),
        dvf=f(L, KW),
        dkb=b(L, KW),
        dvb=b(L, KW),
        drow=f(16, B),
        dmr=b(2, B, D),
        g3=f(B, D),
        brow=b(L, D),
        dmem=f(2, B, D),
        be=b(L, D),
        dq=b(L, KW),
        gA=b(4, D, KW),
        gE=b(2, D, F2),
        ylX=b(4, D, LANES),
        ylE1=b(2, D, FQ),
        qA=b(3, 4, D, LANES),
        qE=b(2, 2, D, FQ),
        dpA=b(3, nb, 4, cw, LANES),
        dpE=b(2, nb, 2, cw, FQ),
        acc=f(32, D),
        acc1=f(32, D),
        acc2=f(32, D),
        accc=f(32, D),
        accy=f(32, D),
        accd=f(nb, 16, LANES),
    )


def sem_list(nb):
    counts = dict(
        in_y=1,
        in_c=2,
        cot=1,
        small=nb,
        wself=2 * nb,
        wx=nb,
        we0=nb,
        we1=nb,
        wy_self=nb,
        wy_x=nb,
        wy_e0=nb,
        wy_e1=nb,
        rs1=2,
        n2=2,
        rs2=2,
        br3=1,
        m_y=2,
        m_c=2,
        n4=1,
        rs4=1,
        n5=1,
        rs5=1,
        rs6=1,
        b4=1,
        rs7q=1,
        rs7m=2,
        dm=2,
        g3=1,
        brow=2,
        be=2,
        rs8=2,
        rs9=2,
        fin=1,
        gy_s=1,
        gy_x=1,
        gy_e0=1,
        gy_e1=1,
        gd_a=3 * nb,
        gd_e=2 * nb,
        accc=1,
        accy=1,
        accd=nb,
    )
    base, at = {}, 0
    for name, number in counts.items():
        base[name] = at
        at = at + number
    return SimpleNamespace(**base), at


def step_kernel(cfg, names, *refs):
    n, nb, cw, B, D, FQ, E, inside = cfg
    L, F2, KW = 4 * B, 2 * FQ, 2 * LANES
    R = SimpleNamespace(**dict(zip(names, refs, strict=True)))
    K, _ = sem_list(nb)

    dp = lax.axis_index("dp")
    me = dp if inside else 0
    s = lax.axis_index("seq")
    h = lax.div(s, 2)
    c = lax.rem(s, 2)
    cp = 1 - c
    core = (dp, s + 1 - 2 * c)
    ypeer = (dp, s + 2 - 4 * h)
    is_a, is_b = h == 0, h == 1

    def rows(i, size=B):
        return pl.ds(pl.multiple_of(i * size, size), size)

    def lanes(i, size=LANES):
        return pl.ds(pl.multiple_of(i * size, size), size)

    def send(src, dst, name, to, i=0, j=None):
        return pltpu.make_async_remote_copy(
            src_ref=src,
            dst_ref=dst,
            send_sem=R.ss.at[name + i],
            recv_sem=R.rs.at[name + (i if j is None else j)],
            device_id=to,
            device_id_type=MESH,
        )

    def arrived(dst, name, i=0):
        send(dst, dst, name, core, i).wait_recv()

    def sent(src, name, i=0):
        send(src, src, name, core, i).wait_send()

    def loop(count, body, start=0):
        def step(i, carry):
            body(i)
            return carry

        lax.fori_loop(start, count, step, 0)

    def peer_of(i):
        return lax.rem(me + i, nb)

    barrier = pltpu.get_barrier_semaphore()
    for to in (core, ypeer):
        pl.semaphore_signal(barrier, inc=1, device_id=to, device_id_type=MESH)

    def greet(i):
        pl.semaphore_signal(barrier, inc=1, device_id=(peer_of(i), s), device_id_type=MESH)

    loop(nb, greet, 1)
    pl.semaphore_wait(barrier, nb + 1)

    small = R.small

    def small_copy(to, frm):
        return send(small, R.smallr.at[me], K.small, (to, s), to, me)

    if inside:
        loop(nb, lambda i: small_copy(peer_of(i), me).start(), 1)

    @pl.when(is_a)
    def _():
        R.xrow[rows(s)] = R.src[...]
        R.oth[...] = R.tgt[...]

    @pl.when(is_b)
    def _():
        R.xrow[rows(s)] = R.tgt[...]
        R.oth[...] = R.src[...]

    sy = s + 2 - 4 * h
    send(R.oth, R.xrow.at[rows(s)], K.in_y, ypeer).start()
    send(R.xrow.at[rows(s)], R.xrow.at[rows(s)], K.in_c, core, 0).start()
    R.b5c[rows(c)] = R.cot[...]
    send(R.b5c.at[rows(c)], R.b5c.at[rows(c)], K.cot, core).start()

    def wblock(buf, p, half, width):
        return buf.at[:, rows(p, cw), lanes(half, width)]

    def a_copy(buf, a, name, k, idx):
        p = peer_of(k)
        return send(R.sendA.at[a], wblock(buf, me, h, LANES), name, (p, s), idx + p, idx + me)

    def e_copy(l, name, k):
        p = peer_of(k)
        return send(wblock(R.gE, p, l, FQ), wblock((R.we0, R.we1)[l], me, h, FQ), name, (p, s), p, me)

    for a in range(3):
        if inside:
            for j in range(3):
                R.sendA[a, j] = R.qkv[a, j]
            R.sendA[a, 3] = R.wot[a]
        buf = R.wself.at[a] if a < 2 else R.wx
        piece = R.sendA if inside else R.wa
        for j in range(4):
            buf[j, rows(me, cw), lanes(h)] = piece[a, j]
    if inside:
        for a in range(2):
            loop(nb, lambda i, a=a: a_copy(R.wself.at[a], a, K.wself, i, a * nb).start(), 1)

    arrived(R.xrow.at[rows(sy)], K.in_y)
    send(R.xrow.at[rows(sy)], R.xrow.at[rows(sy)], K.in_c, core, 1).start()

    if inside:
        loop(nb, lambda i: arrived(R.smallr.at[0], K.small, peer_of(i)), 1)
        R.smallr[pl.ds(me, 1)] = small[...][None]
        per = LANES // cw
        for t in range(D // LANES):
            tile = R.smallr[t * per]
            for k in range(1, per):
                tile = tile + R.smallr[t * per + k]
            R.gtab[:, t * LANES:(t + 1) * LANES] = tile

        def chosen(p):
            for l in range(2):
                row = R.smallr[p, pl.ds(10 + l, 1), :]
                for m, held in enumerate((R.up, R.dnt)):
                    total = None
                    for e in range(E):
                        hit = jnp.where(row == float(e), 1.0, 0.0)
                        hit = jnp.concatenate([hit] * (FQ // LANES), axis=1)
                        term = held[l, e].astype(F32) * hit
                        total = term if total is None else total + term
                    R.gE[m, rows(p, cw), lanes(l, FQ)] = total.astype(BF16)

        loop(nb, chosen)
        for l in range(2):
            for m in range(2):
                (R.we0, R.we1)[l][m, rows(me, cw), lanes(h, FQ)] = R.gE[m, rows(me, cw), lanes(l, FQ)]
    else:
        R.gtab[...] = small[...]
        for l in range(2):
            for m in range(2):
                (R.we0, R.we1)[l][m, rows(me, cw), lanes(h, FQ)] = R.we[l, m]

    def forward(buf, name_in, base_in, name_y, width):
        def one(i):
            p = peer_of(i)
            if inside:

                @pl.when(i > 0)
                def _():
                    arrived(wblock(buf, p, h, width), name_in, base_in + p)

            send(wblock(buf, p, h, width), wblock(buf, p, h, width), name_y, ypeer, p).start()

        loop(nb, one)

    def own_arrived(buf, name_in, base_in, width):
        if inside:
            loop(nb, lambda i: arrived(wblock(buf, peer_of(i), h, width), name_in, base_in + peer_of(i)), 1)

    def y_arrived(buf, name_y, width):
        loop(nb, lambda i: arrived(wblock(buf, peer_of(i), 1 - h, width), name_y, peer_of(i)))

    def y_sent(buf, name_y, width):
        loop(nb, lambda i: sent(wblock(buf, peer_of(i), h, width), name_y, peer_of(i)))

    other = R.wself.at[1 - h]
    forward(other, K.wself, (1 - h) * nb, K.wy_self, LANES)
    own_arrived(R.wself.at[h], K.wself, h * nb, LANES)
    if inside:
        loop(nb, lambda i: e_copy(0, K.we0, i).start(), 1)
        loop(nb, lambda i: a_copy(R.wx, 2, K.wx, i, 0).start(), 1)
    y_arrived(R.wself.at[h], K.wy_self, LANES)

    R.acc[...] = jnp.zeros((32, D), F32)

    def tally(row, x):
        R.acc[pl.ds(row, 1), :] += jnp.sum(x, 0, keepdims=True)

    def gain(i):
        return R.gtab[pl.ds(i, 1), :]

    def shift(i):
        return R.gtab[pl.ds(5 + i, 1), :]

    def blk(j):
        return c + 2 * j

    def pblk(j):
        return cp + 2 * j

    def documents(lens, position):
        total = jnp.zeros(position.shape, F32)
        edge = 0
        for k in range(lens.shape[1]):
            edge = edge + lens[0, k]
            total = total + jnp.where(position >= edge, 1.0, 0.0)
        return total

    class Lengths:
        def __init__(self, pick):
            self.pick, self.shape = pick, R.slen.shape

        def __getitem__(self, at):
            return self.pick(at)

    src_lens = Lengths(lambda at: R.slen[at])
    tgt_lens = Lengths(lambda at: R.tlen[at])
    self_lens = Lengths(lambda at: jnp.where(is_a, R.slen[at], R.tlen[at]))

    def set_bias(buf, q_start, q_lens, k_lens, causal, q_axis):
        shape = (B, L) if q_axis == 0 else (L, B)
        thin_q = (B, 1) if q_axis == 0 else (1, B)
        thin_k = (1, L) if q_axis == 0 else (L, 1)
        q_pos = lax.broadcasted_iota(jnp.int32, thin_q, q_axis) + q_start
        k_pos = lax.broadcasted_iota(jnp.int32, thin_k, 1 - q_axis)
        same = documents(q_lens, q_pos) == documents(k_lens, k_pos)
        out = jnp.where(same, 0.0, MASKED)
        if causal is not None:
            limit = q_pos + jnp.where(causal, 0, L)
            out = jnp.where(k_pos <= limit, out, MASKED)
        buf[...] = jnp.broadcast_to(out, shape)

    lane_head = lax.div(lax.broadcasted_iota(jnp.int32, (1, KW), 1), HEAD_DIM)

    def head_row(hd):
        return jnp.where(lane_head == hd, 1.0, 0.0)

    heads = KW // HEAD_DIM

    def attend(q_blk, k_ref, v_ref):
        lane = lax.broadcasted_iota(jnp.int32, (1, LANES), 1)
        out = jnp.zeros((B, KW), F32)
        lse = jnp.zeros((B, LANES), F32)
        for hd in range(heads):
            hrow = head_row(hd)
            scores = mm_nt(q_blk * hrow.astype(BF16), k_ref[...]) + R.bias[...]
            top = jnp.max(scores, -1, keepdims=True)
            expos = jnp.exp(scores - top)
            total = jnp.sum(expos, -1, keepdims=True)
            out = out + mm(expos.astype(BF16), v_ref[...]) * (hrow / total)
            lse = lse + jnp.where(lane == hd, top + jnp.log(total), 0.0)
        return out.astype(BF16), jnp.transpose(lse)[0:8, :]

    def attend_back(q_blk, o_blk, do_blk, lse_ref, at, k_ref, v_ref):
        prod = do_blk.astype(F32) * o_blk.astype(F32)
        high = prod.astype(BF16)
        low = (prod - high.astype(F32)).astype(BF16)
        pick = lax.broadcasted_iota(jnp.int32, (16, KW), 0) == jnp.broadcast_to(lane_head, (16, KW))
        pick = jnp.where(pick, 1.0, 0.0).astype(BF16)
        R.drow[...] = mm_nt(pick, high) + mm_nt(pick, low)
        R.dqf[...] = jnp.zeros((B, KW), F32)

        def head(hd):
            hrow = head_row(hd)
            qm = q_blk * hrow.astype(BF16)
            dom = do_blk * hrow.astype(BF16)
            probs = jnp.exp(mm_nt(k_ref[...], qm) + R.biasT[...] - lse_ref[pl.ds(hd, 1), at])
            R.dvf[...] += mm(probs.astype(BF16), dom)
            change = probs * (mm_nt(v_ref[...], dom) - R.drow[pl.ds(hd, 1), :])
            change = change.astype(BF16)
            R.dkf[...] += mm(change, qm)
            R.dqf[...] += mm_tn(change, k_ref[...]) * hrow

        loop(heads, head)
        return R.dqf[...]

    scale = HEAD_DIM ** (-0.5)

    loop(2, lambda j: arrived(R.xrow.at[rows(pblk(j))], K.in_c, lax.rem(j + h, 2)))

    def self_project(i):
        x = R.xrow[rows(i)].astype(F32)
        y = norm(x, gain(2 * h), shift(2 * h)).astype(BF16)
        R.nrow[rows(i)] = y
        R.q[rows(i)] = mm(y, R.wself[h, 0]).astype(BF16) * jnp.asarray(scale, BF16)
        R.k[rows(i)] = mm(y, R.wself[h, 1]).astype(BF16)
        R.v[rows(i)] = mm(y, R.wself[h, 2]).astype(BF16)

    loop(4, self_project)

    def self_block(i):
        j = lax.rem(i, 2)
        b = jnp.where(i < 2, cp, c) + 2 * j
        set_bias(R.bias, b * B, self_lens, self_lens, is_b, 0)
        o, lse = attend(R.q[rows(b)], R.k, R.v)
        R.o[rows(b)] = o
        R.lseT[:, rows(b)] = lse
        y = mm_nt(o, R.wself[h, 3])

        @pl.when(i < 2)
        def _():
            R.cs[j] = y.astype(BF16)
            send(R.cs.at[j], R.cr.at[j], K.rs1, core, j).start()

        @pl.when(i >= 2)
        def _():
            R.part[j] = y

    loop(4, self_block)

    def self_end(j):
        arrived(R.cr.at[j], K.rs1, j)
        branch = R.part[j] + R.cr[j].astype(F32)
        x = R.xrow[rows(blk(j))].astype(F32)
        y = x + branch
        R.mid[j] = y
        tally(16 + 2 * h, x * x)
        tally(21 + 2 * h, branch * branch)

        @pl.when(is_a)
        def _():
            R.n2row[rows(blk(j))] = norm(y, gain(1), shift(1)).astype(BF16)
            send(R.n2row.at[rows(blk(j))], R.n2row.at[rows(blk(j))], K.n2, core, j).start()
            tally(17, y * y)

        @pl.when(is_b & (j == 0))
        def _():
            R.fs[...] = branch.astype(BF16)
            send(R.fs, R.fr, K.br3, ypeer).start()

    loop(2, self_end)

    @pl.when(is_b)
    def _():
        forward(R.we0, K.we0, 0, K.wy_e0, FQ)
        if inside:
            loop(nb, lambda i: e_copy(1, K.we1, i).start(), 1)
        forward(R.wx, K.wx, 0, K.wy_x, LANES)

    @pl.when(is_a)
    def _():
        own_arrived(R.we0, K.we0, 0, FQ)
        if inside:
            loop(nb, lambda i: e_copy(1, K.we1, i).start(), 1)
        y_arrived(R.we0, K.wy_e0, FQ)

        def block(i):
            j = lax.rem(i, 2)
            b = jnp.where(i < 2, c, cp) + 2 * j

            @pl.when(i >= 2)
            def _():
                arrived(R.n2row.at[rows(b)], K.n2, j)

            hid = mm(R.n2row[rows(b)], R.we0[0])
            act, slope = gelu_pair(hid)
            R.g0[rows(b)] = act.astype(BF16)
            R.gp0[rows(b)] = slope.astype(BF16)
            y = mm_nt(R.g0[rows(b)], R.we0[1])

            @pl.when(i < 2)
            def _():
                R.part[j] = y

            @pl.when(i >= 2)
            def _():
                sent(R.cs.at[j], K.rs1, j)
                R.cs[j] = y.astype(BF16)
                send(R.cs.at[j], R.cr.at[j], K.rs2, core, j).start()

        loop(4, block)
        forward(R.wx, K.wx, 0, K.wy_x, LANES)

        def end(j):
            arrived(R.cr.at[j], K.rs2, j)
            branch = R.part[j] + R.cr[j].astype(F32)
            tally(22, branch * branch)
            at = R.mrow.at[rows(blk(j))]
            R.mrow[rows(blk(j))] = (R.mid[j] + branch).astype(BF16)
            send(at, at, K.m_y, ypeer, j).start()
            send(at, at, K.m_c, core, j).start()

        loop(2, end)

    @pl.when(is_a)
    def _():
        arrived(R.fr, K.br3)
        R.t1[...] = R.tgt[...].astype(F32) + R.fr[...].astype(F32)

    @pl.when(is_b)
    def _():
        R.t1[...] = R.mid[1]

    one = R.t1[...]
    tally(19, one * one)
    R.n4c[rows(c)] = norm(one, gain(3), shift(3)).astype(BF16)
    send(R.n4c.at[rows(c)], R.n4c.at[rows(c)], K.n4, core).start()
    y_arrived(R.wx, K.wy_x, LANES)

    def cross_keys(b):
        y = R.mrow[rows(b)]
        R.k2[rows(b)] = mm(y, R.wx[1]).astype(BF16)
        R.v2[rows(b)] = mm(y, R.wx[2]).astype(BF16)

    arrived(R.n4c.at[rows(cp)], K.n4)

    def cross_query(i):
        R.q2[rows(i)] = mm(R.n4c[rows(i)], R.wx[0]).astype(BF16) * jnp.asarray(scale, BF16)

    loop(2, cross_query)

    def memory_block(i):
        j = lax.rem(i, 2)
        b = jnp.where(i < 2, c, cp) + 2 * j
        at = R.mrow.at[rows(b)]

        @pl.when((i < 2) & is_b)
        def _():
            arrived(at, K.m_y, j)
            send(at, at, K.m_c, core, j).start()

        @pl.when(i >= 2)
        def _():
            arrived(at, K.m_c, j)

        cross_keys(b)

    loop(4, memory_block)

    def cross_block(i):
        b = jnp.where(i < 1, cp, c)
        set_bias(R.bias, (2 * h + b) * B, tgt_lens, src_lens, None, 0)
        o, lse = attend(R.q2[rows(b)], R.k2, R.v2)
        R.o2[rows(b)] = o
        R.lse2T[:, rows(b)] = lse
        y = mm_nt(o, R.wx[3])

        @pl.when(i < 1)
        def _():
            R.ds[...] = y.astype(BF16)
            send(R.ds, R.dr.at[0], K.rs4, core).start()

        @pl.when(i >= 1)
        def _():
            R.part[0] = y

    loop(2, cross_block)
    forward(R.we1, K.we1, 0, K.wy_e1, FQ)
    arrived(R.dr.at[0], K.rs4)
    branch4 = R.part[0] + R.dr[0].astype(F32)
    tally(24, branch4 * branch4)
    two = R.t1[...] + branch4
    R.t2[...] = two
    tally(20, two * two)
    R.n5c[rows(c)] = norm(two, gain(4), shift(4)).astype(BF16)
    send(R.n5c.at[rows(c)], R.n5c.at[rows(c)], K.n5, core).start()
    y_arrived(R.we1, K.wy_e1, FQ)

    def dec_block(i):
        b = jnp.where(i < 1, c, cp)

        @pl.when(i >= 1)
        def _():
            arrived(R.n5c.at[rows(b)], K.n5)

        hid = mm(R.n5c[rows(b)], R.we1[0])
        act, slope = gelu_pair(hid)
        R.g1[rows(b)] = act.astype(BF16)
        R.gp1[rows(b)] = slope.astype(BF16)
        y = mm_nt(R.g1[rows(b)], R.we1[1])

        @pl.when(i < 1)
        def _():
            R.part[0] = y

        @pl.when(i >= 1)
        def _():
            sent(R.ds, K.rs4)
            R.ds[...] = y.astype(BF16)
            send(R.ds, R.dr.at[1], K.rs5, core).start()

    loop(2, dec_block)
    arrived(R.b5c.at[rows(cp)], K.cot)

    def dec_back(i):
        b = jnp.where(i < 1, cp, c)
        dact = mm(R.b5c[rows(b)], R.we1[1])
        R.gp1[rows(b)] = (dact * R.gp1[rows(b)].astype(F32)).astype(BF16)
        y = mm_nt(R.gp1[rows(b)], R.we1[0])

        @pl.when(i < 1)
        def _():
            sent(R.ds, K.rs5)
            R.ds[...] = y.astype(BF16)
            send(R.ds, R.dr.at[0], K.rs6, core).start()

        @pl.when(i >= 1)
        def _():
            R.part[1] = y

    loop(2, dec_back)
    arrived(R.dr.at[1], K.rs5)
    branch5 = R.part[0] + R.dr[1].astype(F32)
    tally(25, branch5 * branch5)
    R.dec[...] = R.t2[...] + branch5

    def add_norm(i, dgain, dbias):
        R.acc[pl.ds(i, 1), :] += dgain
        R.acc[pl.ds(5 + i, 1), :] += dbias

    arrived(R.dr.at[0], K.rs6)
    back, dgain, dbias = norm_back(R.t2[...], gain(4), R.part[1] + R.dr[0].astype(F32))
    add_norm(4, dgain, dbias)
    g4 = R.cot[...].astype(F32) + back
    R.g4[...] = g4
    R.b4c[rows(c)] = g4.astype(BF16)
    send(R.b4c.at[rows(c)], R.b4c.at[rows(c)], K.b4, core).start()

    def expert_grads(buf, x_ref, dh_ref, b_ref, g_ref):
        def part(i):
            at = lanes(i, 2 * LANES)
            buf[0, rows(i, 2 * LANES)] = mm_tn(x_ref[:, at], dh_ref[...]).astype(BF16)
            buf[1, rows(i, 2 * LANES)] = mm_tn(b_ref[:, at], g_ref[...]).astype(BF16)

        loop(D // (2 * LANES), part)

    def y_grad(buf, land, name, width):
        return send(buf.at[:, :, lanes(1 - h, width)], land, name, ypeer)

    def dp_a(a, i):
        p = peer_of(i)
        return send(R.qA.at[a, :, rows(p, cw), :], R.dpA.at[a, me], K.gd_a, (p, s), a * nb + p, a * nb + me)

    def dp_e(l, i):
        p = peer_of(i)
        return send(R.qE.at[l, :, rows(p, cw), :], R.dpE.at[l, me], K.gd_e, (p, s), l * nb + p, l * nb + me)

    if inside:

        def chosen_sent(i):
            for l in range(2):
                sent(wblock(R.gE, 0, l, FQ), (K.we0, K.we1)[l], peer_of(i))

        loop(nb, chosen_sent, 1)
    expert_grads(R.gE, R.n5c, R.gp1, R.b5c, R.g1)
    y_grad(R.gE, R.ylE1, K.gy_e1, FQ).start()

    arrived(R.b4c.at[rows(cp)], K.b4)
    R.dkf[...] = jnp.zeros((L, KW), F32)
    R.dvf[...] = jnp.zeros((L, KW), F32)

    def cross_back(i):
        b = jnp.where(i < 1, cp, c)
        do = mm(R.b4c[rows(b)], R.wx[3]).astype(BF16)
        set_bias(R.biasT, (2 * h + b) * B, tgt_lens, src_lens, None, 1)
        dq = attend_back(R.q2[rows(b)], R.o2[rows(b)], do, R.lse2T, rows(b), R.k2, R.v2)
        dq = (dq * scale).astype(BF16)
        R.dq[rows(b)] = dq
        y = mm_nt(dq, R.wx[0])

        @pl.when(i < 1)
        def _():
            sent(R.ds, K.rs6)
            R.ds[...] = y.astype(BF16)
            send(R.ds, R.dr.at[1], K.rs7q, core).start()

        @pl.when(i >= 1)
        def _():
            R.part[0] = y

    loop(2, cross_back)
    R.dkb[...] = R.dkf[...].astype(BF16)
    R.dvb[...] = R.dvf[...].astype(BF16)

    def memory_back(i):
        j = lax.rem(i, 2)
        b = jnp.where(i < 2, cp, c) + 2 * j
        y = mm_nt(R.dkb[rows(b)], R.wx[1]) + mm_nt(R.dvb[rows(b)], R.wx[2])

        @pl.when((i < 2) & is_a)
        def _():
            sent(R.cs.at[j], K.rs2, j)

        @pl.when((i < 2) & is_b)
        def _():
            sent(R.cs.at[j], K.rs1, j)

        @pl.when(i < 2)
        def _():
            R.cs[j] = y.astype(BF16)
            send(R.cs.at[j], R.cr.at[j], K.rs7m, core, j).start()

        @pl.when(i >= 2)
        def _():
            R.dmem[j] = y

    loop(4, memory_back)

    def memory_sum(j):
        arrived(R.cr.at[j], K.rs7m, j)
        y = R.dmem[j] + R.cr[j].astype(F32)
        R.dmem[j] = y

        @pl.when(is_b)
        def _():
            R.be[rows(j)] = y.astype(BF16)
            send(R.be.at[rows(j)], R.dmr.at[j], K.dm, ypeer, j).start()

    loop(2, memory_sum)

    arrived(R.dr.at[1], K.rs7q)
    back, dgain, dbias = norm_back(R.t1[...], gain(3), R.part[0] + R.dr[1].astype(F32))
    add_norm(3, dgain, dbias)
    g3 = R.g4[...] + back
    R.g3[...] = g3

    @pl.when(is_a)
    def _():
        R.fs[...] = g3.astype(BF16)
        send(R.fs, R.brow.at[rows(c)], K.g3, ypeer).start()

    def attn_grads(buf, xq_ref, xk_ref, dq_ref, o_ref, b_ref):
        def part(i):
            at, to = lanes(i, 2 * LANES), rows(i, 2 * LANES)
            buf[0, to] = mm_tn(xq_ref[:, at], dq_ref[...]).astype(BF16)
            buf[1, to] = mm_tn(xk_ref[:, at], R.dkb[...]).astype(BF16)
            buf[2, to] = mm_tn(xk_ref[:, at], R.dvb[...]).astype(BF16)
            buf[3, to] = mm_tn(b_ref[:, at], o_ref[...]).astype(BF16)

        loop(D // (2 * LANES), part)

    attn_grads(R.gA, R.n4c, R.mrow, R.dq.at[0:2 * B], R.o2, R.b4c)
    y_grad(R.gA, R.ylX, K.gy_x, LANES).start()

    def dp_e_start(l):
        if inside:
            loop(nb, lambda i: dp_e(l, i).start(), 1)

    def dp_a_start(a):
        if inside:
            loop(nb, lambda i: dp_a(a, i).start(), 1)

    def join_e1():
        arrived(R.ylE1, K.gy_e1)
        for m in range(2):
            total = R.gE[m, :, lanes(h, FQ)].astype(F32) + R.ylE1[m].astype(F32)
            R.qE[1, m] = total.astype(BF16)
        dp_e_start(1)

    def join_x():
        arrived(R.ylX, K.gy_x)
        for m in range(4):
            total = R.gA[m, :, lanes(h)].astype(F32) + R.ylX[m].astype(F32)
            R.qA[2, m] = total.astype(BF16)
        dp_a_start(2)

    join_e1()
    join_x()

    @pl.when(is_a)
    def _():
        def begin(j):
            arrived(R.dmr.at[j], K.dm, j)
            y = R.dmem[j] + R.dmr[j].astype(F32)
            R.dmem[j] = y
            at = R.be.at[rows(blk(j))]
            R.be[rows(blk(j))] = y.astype(BF16)
            send(at, at, K.be, core, j).start()

        loop(2, begin)

        def block(i):
            j = lax.rem(i, 2)
            b = jnp.where(i < 2, c, cp) + 2 * j

            @pl.when(i >= 2)
            def _():
                arrived(R.be.at[rows(b)], K.be, j)

            dact = mm(R.be[rows(b)], R.we0[1])
            R.gp0[rows(b)] = (dact * R.gp0[rows(b)].astype(F32)).astype(BF16)
            y = mm_nt(R.gp0[rows(b)], R.we0[0])

            @pl.when(i < 2)
            def _():
                R.part[j] = y

            @pl.when(i >= 2)
            def _():
                sent(R.cs.at[j], K.rs7m, j)
                R.cs[j] = y.astype(BF16)
                send(R.cs.at[j], R.cr.at[j], K.rs8, core, j).start()

        loop(4, block)

        def end(j):
            arrived(R.cr.at[j], K.rs8, j)
            up = R.part[j] + R.cr[j].astype(F32)
            back, dgain, dbias = norm_back(R.mid[j], gain(1), up)
            add_norm(1, dgain, dbias)
            g = R.dmem[j] + back
            R.dmem[j] = g
            at = R.brow.at[rows(blk(j))]
            R.brow[rows(blk(j))] = g.astype(BF16)
            send(at, at, K.brow, core, j).start()

        loop(2, end)
        y_grad(R.gE, R.ylE1, K.gy_e1, FQ).wait_send()
        expert_grads(R.gE, R.n2row, R.gp0, R.be, R.g0)
        y_grad(R.gE, R.qE.at[0], K.gy_e0, FQ).start()
        for m in range(2):
            R.qE[0, m] = R.gE[m, :, lanes(h, FQ)]
        dp_e_start(0)

    @pl.when(is_b)
    def _():
        R.brow[rows(blk(1))] = R.g3[...].astype(BF16)
        arrived(R.brow.at[rows(blk(0))], K.g3)
        for j in range(2):
            at = R.brow.at[rows(blk(j))]
            send(at, at, K.brow, core, j).start()

    R.dkf[...] = jnp.zeros((L, KW), F32)
    R.dvf[...] = jnp.zeros((L, KW), F32)

    def self_back(i):
        j = lax.rem(i, 2)
        b = jnp.where(i < 2, c, cp) + 2 * j

        @pl.when(i >= 2)
        def _():
            arrived(R.brow.at[rows(b)], K.brow, j)

        do = mm(R.brow[rows(b)], R.wself[h, 3]).astype(BF16)
        set_bias(R.biasT, b * B, self_lens, self_lens, is_b, 1)
        dq = attend_back(R.q[rows(b)], R.o[rows(b)], do, R.lseT, rows(b), R.k, R.v)
        R.dq[rows(b)] = (dq * scale).astype(BF16)

    loop(4, self_back)
    R.dkb[...] = R.dkf[...].astype(BF16)
    R.dvb[...] = R.dvf[...].astype(BF16)
    y_grad(R.gA, R.ylX, K.gy_x, LANES).wait_send()
    attn_grads(R.gA, R.nrow, R.nrow, R.dq, R.o, R.brow)
    y_grad(R.gA, R.qA.at[h], K.gy_s, LANES).start()
    for m in range(4):
        R.qA[h, m] = R.gA[m, :, lanes(h)]
    dp_a_start(h)

    def self_dx(i):
        j = lax.rem(i, 2)
        b = jnp.where(i < 2, cp, c) + 2 * j
        y = mm_nt(R.dq[rows(b)], R.wself[h, 0])
        y = y + mm_nt(R.dkb[rows(b)], R.wself[h, 1])
        y = y + mm_nt(R.dvb[rows(b)], R.wself[h, 2])

        @pl.when((i < 2) & is_a)
        def _():
            sent(R.cs.at[j], K.rs8, j)

        @pl.when((i < 2) & is_b)
        def _():
            sent(R.cs.at[j], K.rs7m, j)

        @pl.when(i < 2)
        def _():
            R.cs[j] = y.astype(BF16)
            send(R.cs.at[j], R.cr.at[j], K.rs9, core, j).start()

        @pl.when(i >= 2)
        def _():
            R.part[j] = y

    loop(4, self_dx)

    @pl.when(is_b)
    def _():
        arrived(R.qE.at[0], K.gy_e0)
        dp_e_start(0)

    def self_final(j):
        arrived(R.cr.at[j], K.rs9, j)
        x = R.xrow[rows(blk(j))].astype(F32)
        back, dgain, dbias = norm_back(x, gain(2 * h), R.part[j] + R.cr[j].astype(F32))
        add_norm(2 * h, dgain, dbias)

        @pl.when(is_a & (j == 0))
        def _():
            R.sgrad[...] = R.dmem[0] + back

        @pl.when(is_a & (j == 1))
        def _():
            sent(R.fs, K.g3)
            R.fs[...] = (R.dmem[1] + back).astype(BF16)
            send(R.fs, R.fr, K.fin, ypeer).start()

        @pl.when(is_b & (j == 0))
        def _():
            sent(R.fs, K.br3)
            R.fs[...] = back.astype(BF16)
            send(R.fs, R.fr, K.fin, ypeer).start()

        @pl.when(is_b & (j == 1))
        def _():
            R.tgrad[...] = R.g3[...] + back

    loop(2, self_final)

    send(R.acc, R.accc, K.accc, core).start()
    arrived(R.accc, K.accc)
    R.acc1[...] = R.acc[...] + R.accc[...]
    send(R.acc1, R.accy, K.accy, ypeer).start()

    arrived(R.qA.at[1 - h], K.gy_s)
    dp_a_start(1 - h)

    arrived(R.accy, K.accy)
    R.acc2[...] = R.acc1[...] + R.accy[...]
    R.stats[...] = R.acc2[16:32, :]
    arrived(R.fr, K.fin)

    @pl.when(is_a)
    def _():
        R.tgrad[...] = R.g3[...] + R.fr[...].astype(F32)

    @pl.when(is_b)
    def _():
        R.sgrad[...] = R.fr[...].astype(F32)

    if inside:

        def tile_of(p):
            return lanes(lax.div(p * cw, LANES))

        def acc_copy(i):
            p = peer_of(i)
            return send(R.acc2.at[0:16, tile_of(p)], R.accd.at[me], K.accd, (p, s), p, me)

        loop(nb, lambda i: acc_copy(i).start(), 1)

        for l in range(2):
            loop(nb, lambda i, l=l: arrived(R.dpE.at[l, peer_of(i)], K.gd_e, l * nb + peer_of(i)), 1)
            for m in range(2):
                R.dpE[l, pl.ds(me, 1), m] = R.qE[l, m, rows(me, cw), :][None]
            for m, total_ref in enumerate((R.gup, R.gdn)):

                def one_expert(e, l=l, m=m, total_ref=total_ref):
                    total = jnp.zeros((cw, FQ), F32)
                    for p in range(nb):
                        row = R.smallr[p, 10 + l:11 + l, :]
                        hit = jnp.where(row == e.astype(F32), 1.0, 0.0)
                        hit = jnp.concatenate([hit] * (FQ // LANES), axis=1)
                        total = total + R.dpE[l, p, m].astype(F32) * hit
                    total_ref[l, pl.ds(e, 1)] = total[None]

                loop(E, one_expert)

        def attn_total(a):
            loop(nb, lambda i: arrived(R.dpA.at[a, peer_of(i)], K.gd_a, a * nb + peer_of(i)), 1)
            for m in range(4):
                R.dpA[a, pl.ds(me, 1), m] = R.qA[a, m, rows(me, cw), :][None]
            for m in range(4):
                total = R.dpA[a, 0, m].astype(F32)
                for p in range(1, nb):
                    total = total + R.dpA[a, p, m].astype(F32)
                if m < 3:
                    R.gqkv[a, m] = total
                else:
                    R.gout[a] = total

        for a in (2, 0, 1):
            attn_total(a)

        loop(nb, lambda i: arrived(R.accd.at[peer_of(i)], K.accd, peer_of(i)), 1)
        total = R.acc2[0:16, tile_of(me)]

        def more(i):
            R.ggb[...] += R.accd[peer_of(i)]

        R.ggb[...] = total
        loop(nb, more, 1)
    else:
        R.ga[...] = R.qA[...]
        R.ge[...] = R.qE[...]
        R.gacc[...] = R.acc2[0:16, :]

    sent(R.oth, K.in_y)
    sent(R.oth, K.in_c, 0)
    sent(R.oth, K.in_c, 1)
    sent(R.oth, K.cot)
    y_sent(other, K.wy_self, LANES)
    y_sent(R.wx, K.wy_x, LANES)
    y_sent(R.we1, K.wy_e1, FQ)
    for name in (K.rs9, K.brow, K.m_c):
        for j in range(2):
            sent(R.oth, name, j)
    for name in (K.n4, K.n5, K.b4, K.rs7q, K.fin):
        sent(R.oth, name)
    y_grad(R.gA, R.qA.at[h], K.gy_s, LANES).wait_send()
    send(R.acc, R.accc, K.accc, core).wait_send()
    send(R.acc1, R.accy, K.accy, ypeer).wait_send()

    @pl.when(is_a)
    def _():
        for name in (K.n2, K.m_y, K.be):
            for j in range(2):
                sent(R.oth, name, j)
        y_grad(R.gE, R.qE.at[0], K.gy_e0, FQ).wait_send()

    @pl.when(is_b)
    def _():
        y_grad(R.gE, R.ylE1, K.gy_e1, FQ).wait_send()
        y_sent(R.we0, K.wy_e0, FQ)
        for j in range(2):
            sent(R.oth, K.dm, j)

    if inside:

        def drain(i):
            p = peer_of(i)
            small_copy(p, me).wait_send()
            for a in range(2):
                sent(R.sendA.at[a], K.wself, a * nb + p)
            sent(R.sendA.at[2], K.wx, p)
            for l in range(2):
                sent(R.dpE.at[l, 0], K.gd_e, l * nb + p)
            for a in range(3):
                sent(R.dpA.at[a, 0], K.gd_a, a * nb + p)
            sent(R.accd.at[0], K.accd, p)

        loop(nb, drain, 1)


def on_device(
    src_input,
    tgt_input,
    out_cotangent,
    src_lengths,
    tgt_lengths,
    enc_expert,
    dec_expert,
    norm_gains,
    norm_biases,
    qkv_weight,
    out_weight,
    expert_up,
    expert_down,
):
    n = lax.axis_size("dp")
    dp = lax.axis_index("dp")
    B, D = src_input.shape[1:]
    cw = norm_gains.shape[1]
    FQ = expert_up.shape[3]
    E = expert_up.shape[1]
    inside = cw % 16 == 0 and LANES % cw == 0
    wot = jnp.swapaxes(out_weight, 1, 2)
    dnt = jnp.swapaxes(expert_down, 2, 3)
    gb = jnp.concatenate([norm_gains, norm_biases], 0).astype(F32)
    if inside:
        nb, rowsize = n, cw
        at = lax.rem(dp * cw, LANES)
        small = lax.dynamic_update_slice(jnp.zeros((16, LANES), F32), gb, (0, at))
        picks = jnp.concatenate([enc_expert, dec_expert], 0).astype(F32)
        small = small.at[10:12].set(jnp.broadcast_to(picks, (2, LANES)))
        operands = dict(small=small, qkv=qkv_weight, wot=wot, up=expert_up, dnt=dnt)
        grads = dict(
            gqkv=jax.ShapeDtypeStruct((3, 3, cw, LANES), F32),
            gout=jax.ShapeDtypeStruct((3, cw, LANES), F32),
            gup=jax.ShapeDtypeStruct((2, E, cw, FQ), F32),
            gdn=jax.ShapeDtypeStruct((2, E, cw, FQ), F32),
            ggb=jax.ShapeDtypeStruct((16, LANES), F32),
        )
    else:
        nb, rowsize = 1, D
        small = lax.all_gather(gb, "dp", axis=1, tiled=True)
        small = jnp.concatenate([small, jnp.zeros((6, D), F32)], 0)
        wa = jnp.concatenate([qkv_weight, wot[:, None]], 1)
        wa = lax.all_gather(wa, "dp", axis=2, tiled=True)
        picks = jnp.stack([enc_expert[0, 0], dec_expert[0, 0]])
        we = jnp.stack([expert_up, dnt], 2)
        we = lax.all_gather(we, "dp", axis=3, tiled=True)
        we = jnp.stack([jnp.take(we[l], picks[l], axis=0) for l in range(2)])
        operands = dict(small=small, wa=wa, we=we)
        grads = dict(
            ga=jax.ShapeDtypeStruct((3, 4, D, LANES), BF16),
            ge=jax.ShapeDtypeStruct((2, 2, D, FQ), BF16),
            gacc=jax.ShapeDtypeStruct((16, D), F32),
        )
    cfg = (n, nb, rowsize, B, D, FQ, E, inside)
    scratch = scratch_list(n, nb, rowsize, B, D, FQ)
    count = sem_list(nb)[1]
    scratch.update(ss=pltpu.SemaphoreType.DMA((count,)), rs=pltpu.SemaphoreType.DMA((count,)))
    block = jax.ShapeDtypeStruct((B, D), F32)
    vmem = pl.BlockSpec(memory_space=pltpu.VMEM)
    smem = pl.BlockSpec(memory_space=pltpu.SMEM)
    lengths = dict(slen=src_lengths, tlen=tgt_lengths)
    operands = dict(src=src_input[0], tgt=tgt_input[0], cot=out_cotangent[0], **operands)
    results = dict(dec=block, sgrad=block, tgrad=block, stats=jax.ShapeDtypeStruct((16, D), F32), **grads)
    names = tuple(lengths) + tuple(operands) + tuple(results) + tuple(scratch)
    outs = pl.pallas_call(
        functools.partial(step_kernel, cfg, names),
        name="step",
        out_shape=tuple(results.values()),
        in_specs=[smem] * len(lengths) + [vmem] * len(operands),
        out_specs=[vmem] * len(results),
        scratch_shapes=list(scratch.values()),
        compiler_params=pltpu.CompilerParams(
            collective_id=1, has_side_effects=True, vmem_limit_bytes=62 << 20
        ),
        cost_estimate=pl.CostEstimate(flops=17 << 30, bytes_accessed=8 << 20, transcendentals=16 << 20),
    )(*lengths.values(), *operands.values())
    dec, sgrad, tgrad, stats = outs[:4]
    length = B * lax.axis_size("seq")
    rms = jnp.sqrt(jnp.sum(stats[:10], 1) / (length * D)).reshape(1, 2, 5)
    if inside:
        gqkv, gout, gup, gdn, ggb = outs[4:]
        own = lax.dynamic_slice(ggb, (0, at), (16, cw))
        gains, biases = own[0:5], own[5:10]
    else:
        ga, ge, gacc = outs[4:]

        def total(x, axis):
            return lax.psum_scatter(x, "dp", scatter_dimension=axis, tiled=True)

        gains, biases = total(gacc[0:5], 1), total(gacc[5:10], 1)
        ga = total(ga.astype(F32), 2)
        gqkv, gout = ga[:, :3], ga[:, 3]
        match = (picks[:, None] == jnp.arange(E, dtype=jnp.int32)[None]).astype(F32)
        ge = ge.astype(F32)[:, None] * match[:, :, None, None, None]
        ge = total(ge, 3)
        gup, gdn = ge[:, :, 0], ge[:, :, 1]
    return (
        dec[None],
        sgrad[None],
        tgrad[None],
        gains,
        biases,
        gqkv,
        jnp.swapaxes(gout, 1, 2),
        gup,
        jnp.swapaxes(gdn, 2, 3),
        rms,
    )


def solution(mesh):
    placed = (
        P("dp", "seq", None),
        P("dp", "seq", None),
        P("dp", "seq", None),
        P("dp", None),
        P("dp", None),
        P("dp", None),
        P("dp", None),
        P(None, "dp"),
        P(None, "dp"),
        P(None, None, "dp", "seq"),
        P(None, "seq", "dp"),
        P(None, None, "dp", "seq"),
        P(None, None, "seq", "dp"),
    )
    return jax.shard_map(
        on_device,
        mesh=mesh,
        in_specs=placed,
        out_specs=(
            P("dp", "seq", None),
            P("dp", "seq", None),
            P("dp", "seq", None),
            P(None, "dp"),
            P(None, "dp"),
            P(None, None, "dp", "seq"),
            P(None, "seq", "dp"),
            P(None, None, "dp", "seq"),
            P(None, None, "seq", "dp"),
            P("dp", None, None),
        ),
        check_vma=False,
    )
```

time: 1440 us -> 283 us (0.20); the launches traced: 1430 us -> 283 us
  waiting for transfers between devices: 1040 us -> 0 us
  Pallas kernels: 0 us -> 269 us
  matrix products: 130 us -> 0 us
  blocking collectives: 87.5 us -> 0 us
  other arithmetic: 86.2 us -> 0.97 us
  local copies, waits for them, and re-layouts: 61.5 us -> 11.3 us
  between operations: 18.5 us -> 1.99 us
    reduce_scatter x13 -> x0, waiting for transfers between devices: 480 us -> none  [the longest x1 152 us: on_device(): lax.psum_scatter(down_local, 'dp', scatter_dimension=3, tiled=True)]
    unnamed x35 -> x0, waiting for transfers between devices: 284 us -> none
    all_gather x14 -> x0, waiting for transfers between devices: 274 us -> none  [the longest x1 69.5 us: on_device(): lax.all_gather(expert_up, 'dp', axis=2, tiled=True)]
    pallas_call x0 -> x1, Pallas kernels: none -> 269 us  [on_device(): pl.pallas_call(functools.partial(step_kernel, cfg, names), name='step', o...]
    dot_general x66 -> x0, matrix products: 130 us -> none  [the longest x3 16.2 us: per_row(): jnp.einsum('qhd,khd->hqk', heads_change, heads_value, preferred_element_t...]
    all_gather x3 -> x0, blocking collectives: 80.8 us -> none  [the longest x1 32.1 us: on_device(): lax.all_gather(out_weight, 'dp', axis=2, tiled=True)]
    reduce_sum x25 -> x1, other arithmetic: 35.8 us -> 0.88 us  [on_device(): rms = jnp.sqrt(jnp.sum(stats[:10], 1) / (length * D)).reshape(1, 2, 5)]
    unnamed x203 -> x27, local copies, waits for them, and re-layouts: 43.4 us -> 9.43 us
  transfers between devices with their start and end apart: 31 -> 0, of which waited for: 28 -> 0; matrix products, arithmetic and copies ran while one was open for 15% -> 0% of each run, Pallas kernels for 0% -> 0%
where the time goes in v1:
time: 283 us
  Pallas kernels  269 us (95%)
  local copies, waits for them, and re-layouts  11.3 us (4%)
    pallas_call x1, Pallas kernels, on_device(): pl.pallas_call(functools.partial(step_kernel, cfg, names), name='step', o...  269 us
    unnamed x27, local copies, waits for them, and re-layouts  9.43 us

profile of v1, /device:TPU:28, one launch (start us, length us, event | category | flops | bytes accessed | tf_op | source)
XLA Modules:
  0.0 282.9 jit_solution(11872341198930702275)
XLA Ops:
  1.9 0.1 add_convert_fusion
  2.0 0.0 copy-start.9
  2.0 0.0 copy-start.8
  2.0 0.7 copy-done.9
  2.7 0.0 copy-done.8
  2.7 0.5 dynamic_update_slice.3
  3.2 0.1 constant_dynamic-update-slice_fusion.refs_5_
  3.3 0.0 copy-start.7
  3.3 0.6 copy-done.7
  3.9 268.6 %step.1 = (f32[256,512]{1,0:T(8,128)}, f32[256,512]{1,0:T(8,128)}, f32[256,512]{1,0:T(8,128)}, f32[16,512]{1,0:T(8,128)}, f32[3,3,64,128]{3,2,1,0:T(8,128)}, /*i...) custom-call(s32[1,4]{1,0:T(1,128)} %refs_0_.1, ...), custom_call_target="tpu_custom_call" | custom-call | flops 18253611008 | bytes 8388608 | tf_op jit(solution)/shard_map/step/pallas_call | solution.py:1186
  272.5 0.0 copy-start.6
  272.5 0.9 slice_reduce_fusion
  273.4 0.7 sqrt.14
  274.1 0.0 copy-done.6
  274.1 0.7 fusion
  274.8 0.0 copy-start.3
  274.8 1.9 copy.34
  276.7 0.0 copy-done.3
  276.7 0.0 copy-start.2
  276.7 0.0 copy-start.4
  276.7 0.8 copy.35
  277.5 0.4 copy-done.2
  277.9 0.0 copy-start.1
  277.9 0.8 copy.36
  278.7 0.0 copy-done.4
  278.7 0.0 copy-start.5
  278.7 0.7 copy.37
  279.4 0.2 copy-done.5
  279.7 0.6 copy.38
  280.3 0.0 copy-done.1
  280.3 0.0 copy-start
  280.3 1.0 copy.39
  281.3 0.6 copy-done
  281.9 1.0 copy.40
  (3 shorter events, 0.0 us)
Async XLA Ops:
  2.0 0.7 copy-start.9
  2.0 0.7 copy-start.8
  3.3 0.6 copy-start.7
  272.5 1.6 copy-start.6
  274.8 1.9 copy-start.3
  276.7 1.2 copy-start.2
  276.7 2.0 copy-start.4
  277.9 2.4 copy-start.1
  278.7 1.0 copy-start.5
  280.3 1.6 copy-start

commit v2 on v1

v2 whole, which is shorter than its diff:
```python
import functools
import math
from types import SimpleNamespace

import jax
import jax.numpy as jnp
from jax import lax
from jax.experimental import pallas as pl
from jax.experimental.pallas import tpu as pltpu
from jax.sharding import PartitionSpec as P

HEAD_DIM = 64
EPSILON = 1e-05
MASKED = -1e30
LANES = 128
F32 = jnp.float32
BF16 = jnp.bfloat16
MESH = pl.DeviceIdType.MESH
GELU_A = math.sqrt(2.0 / math.pi)
GELU_B = 0.044715


def mm(a, b):
    return lax.dot_general(a, b, (((1,), (0,)), ((), ())), preferred_element_type=F32)


def mm_nt(a, b):
    return lax.dot_general(a, b, (((1,), (1,)), ((), ())), preferred_element_type=F32)


def mm_tn(a, b):
    return lax.dot_general(a, b, (((0,), (0,)), ((), ())), preferred_element_type=F32)


def centre(x):
    mean = jnp.mean(x, -1, keepdims=True)
    xc = x - mean
    var = jnp.mean(xc * xc, -1, keepdims=True)
    scale = lax.rsqrt(var + EPSILON)
    return xc * scale, scale


def norm(x, gain, shift):
    return centre(x)[0] * gain + shift


def norm_back(x, gain, up):
    xh, scale = centre(x)
    dgain = jnp.sum(up * xh, 0, keepdims=True)
    dbias = jnp.sum(up, 0, keepdims=True)
    dxh = up * gain
    m1 = jnp.mean(dxh, -1, keepdims=True)
    m2 = jnp.mean(dxh * xh, -1, keepdims=True)
    return scale * (dxh - m1 - xh * m2), dgain, dbias


def gelu_pair(x):
    square = x * x
    t = jnp.tanh(x * (GELU_A + (GELU_A * GELU_B) * square))
    half = 0.5 + 0.5 * t
    slope = half + (0.5 * x) * (1.0 - t * t) * (GELU_A + (3.0 * GELU_A * GELU_B) * square)
    return x * half, slope


def scratch_list(nb, cw, B, D, FQ, inside):
    L, F2, KW = 4 * B, 2 * FQ, 2 * LANES

    def b(*shape):
        return pltpu.VMEM(shape, BF16)

    def f(*shape):
        return pltpu.VMEM(shape, F32)

    out = dict(
        xrow=b(L, D),
        oth=b(B, D),
        nrow=b(L, D),
        wself=b(2, 4, D, KW),
        wx=b(4, D, KW),
        we0=b(2, D, F2),
        we1=b(2, D, FQ),
        gtab=f(16, D),
        q=b(L, KW),
        k=b(L, KW),
        v=b(L, KW),
        o=b(L, KW),
        do=b(L, KW),
        lseT=f(8, L),
        drowT=f(16, L),
        bias=f(B, L),
        biasT=f(L, B),
        part=f(2, B, D),
        cs=b(2, B, D),
        cr=b(2, B, D),
        mid=f(2, B, D),
        n2row=b(L, D),
        g0=b(L, F2),
        gp0=b(L, F2),
        mrow=b(L, D),
        fs=b(B, D),
        fr=b(B, D),
        t1=f(B, D),
        n4c=b(2 * B, D),
        q2=b(2 * B, KW),
        k2=b(L, KW),
        v2=b(L, KW),
        o2=b(2 * B, KW),
        lse2T=f(8, 2 * B),
        ds=b(B, D),
        dr=b(2, B, D),
        t2=f(B, D),
        n5=b(L, D),
        b5=b(L, D),
        g1=b(L, FQ),
        dh1=b(L, FQ),
        es=b(3, B, D),
        er=b(3, B, D),
        es6=b(3, B, D),
        er6=b(3, B, D),
        g4=f(B, D),
        last=f(B, D),
        b4c=b(2 * B, D),
        dkf=f(L, LANES),
        dvf=f(L, LANES),
        dkb=b(L, KW),
        dvb=b(L, KW),
        dmr=b(2, B, D),
        g3=f(B, D),
        brow=b(L, D),
        dmem=f(2, B, D),
        be=b(L, D),
        dq=b(L, KW),
        gA=b(4, D, KW),
        gE=b(2, D, F2),
        ylX=b(4, D, LANES),
        acc=f(32, D),
        acc1=f(32, D),
        acc2=f(32, D),
        accc=f(32, D),
        accy=f(32, D),
    )
    if inside:
        out.update(
            small=f(16, LANES),
            smallr=f(nb, 16, LANES),
            sendA=b(3, 4, cw, LANES),
            qA=b(3, 4, D, LANES),
            pA=b(3, 4, D // 2, LANES),
            qE=b(2, 2, D, FQ),
            accd=f(nb, 16, LANES),
        )
    return out


def sem_list(nb):
    counts = dict(
        in_y=1,
        in_c=2,
        b5=3,
        small=nb,
        wa=3 * nb,
        wr=3 * nb,
        we0=nb,
        we1=nb,
        wy_self=nb,
        wy_x=nb,
        wy_e0=nb,
        rs1=2,
        n2=2,
        rs2=2,
        br3=1,
        m_y=2,
        m_c=2,
        n4=1,
        rs4=1,
        n5=3,
        rs5=3,
        rs6=3,
        b4=1,
        rs7q=1,
        rs7m=2,
        dm=2,
        g3=1,
        brow=2,
        be=2,
        rs8=2,
        rs9=2,
        fin=1,
        gy_s=2,
        gy_x=1,
        gy_e0=2,
        gd_a=3 * nb,
        gd_x=3 * nb,
        gd_e=2 * nb,
        accc=1,
        accy=1,
        accd=nb,
        here=5,
    )
    base, at = {}, 0
    for name, number in counts.items():
        base[name] = at
        at = at + number
    return SimpleNamespace(**base), at


def step_kernel(cfg, names, *refs):
    nb, cw, B, D, FQ, E, inside = cfg
    L, F2, KW = 4 * B, 2 * FQ, 2 * LANES
    R = SimpleNamespace(**dict(zip(names, refs, strict=True)))
    K, _ = sem_list(nb)

    dp = lax.axis_index("dp")
    me = dp if inside else 0
    s = lax.axis_index("seq")
    h = lax.div(s, 2)
    c = lax.rem(s, 2)
    cp = 1 - c
    sc = s + 1 - 2 * c
    sy = s + 2 - 4 * h
    core, ypeer = (dp, sc), (dp, sy)
    is_a, is_b = h == 0, h == 1

    def rows(i, size=B):
        return pl.ds(pl.multiple_of(i * size, size), size)

    def lanes(i, size=LANES):
        return pl.ds(pl.multiple_of(i * size, size), size)

    def send(src, dst, name, to, i=0, j=None):
        return pltpu.make_async_remote_copy(
            src_ref=src,
            dst_ref=dst,
            send_sem=R.ss.at[name + i],
            recv_sem=R.rs.at[name + (i if j is None else j)],
            device_id=to,
            device_id_type=MESH,
        )

    def arrived(dst, name, i=0):
        send(dst, dst, name, core, i).wait_recv()

    def sent(src, name, i=0):
        send(src, src, name, core, i).wait_send()

    def loop(count, body, start=0):
        def step(i, carry):
            body(i)
            return carry

        lax.fori_loop(start, count, step, 0)

    def to_peer(i):
        return lax.rem(me + i, nb)

    def from_peer(i):
        return lax.rem(me + nb - i, nb)

    pair = me + 1 - 2 * lax.rem(me, 2)

    barrier = pltpu.get_barrier_semaphore()
    for to in (core, ypeer):
        pl.semaphore_signal(barrier, inc=1, device_id=to, device_id_type=MESH)

    def greet(i):
        pl.semaphore_signal(barrier, inc=1, device_id=(to_peer(i), s), device_id_type=MESH)

    loop(nb, greet, 1)

    if inside:
        R.small[...] = jnp.zeros((16, LANES), F32)
        for k in range(LANES // cw):

            @pl.when(lax.rem(dp, LANES // cw) == k)
            def _(k=k):
                R.small[0:5, k * cw:(k + 1) * cw] = R.gains[...].astype(F32)
                R.small[5:10, k * cw:(k + 1) * cw] = R.biases[...].astype(F32)

        R.small[10:11, :] = jnp.broadcast_to(R.epick[0, 0].astype(F32), (1, LANES))
        R.small[11:12, :] = jnp.broadcast_to(R.dpick[0, 0].astype(F32), (1, LANES))

    @pl.when(is_a)
    def _():
        R.xrow[rows(s)] = R.src[...]
        R.oth[...] = R.tgt[...]

    @pl.when(is_b)
    def _():
        R.xrow[rows(s)] = R.tgt[...]
        R.oth[...] = R.src[...]

    R.b5[rows(s)] = R.cot[...]
    for a in range(3):
        if inside:
            for j in range(3):
                R.sendA[a, j] = R.qkv[a, j]
            R.sendA[a, 3] = R.wot[a]
        buf = R.wself.at[a] if a < 2 else R.wx
        piece = R.sendA if inside else R.wa
        for j in range(4):
            buf[j, rows(me, cw), lanes(h)] = piece[a, j]
    pl.semaphore_wait(barrier, nb + 1)

    def small_copy(p):
        return send(R.small, R.smallr.at[me], K.small, (p, s), p, me)

    def wblock(buf, p, half, width):
        return buf.at[:, rows(p, cw), lanes(half, width)]

    def held(a):
        return R.wself.at[a] if a < 2 else R.wx

    def a_copy(a, p):
        return send(R.sendA.at[a], wblock(held(a), me, h, LANES), K.wa, (p, s), a * nb + p, a * nb + me)

    def a_relay(a, p):
        at = wblock(held(a), p, h, LANES)
        return send(at, at, K.wr, (pair, s), a * nb + p)

    def y_block(buf, p, name, width):
        at = wblock(buf, p, h, width)
        return send(at, at, name, ypeer, p)

    def same_side(i):
        return lax.rem(me + 2 * i, nb)

    def e_copy(l, p):
        at = wblock(R.we0, me, h, FQ) if l == 0 else R.we1.at[:, rows(me, cw), :]
        return send(wblock(R.gE, p, l, FQ), at, (K.we0, K.we1)[l], (p, s), p, me)

    def row_copy(buf, block, name, to, i=0):
        at = buf.at[rows(block)]
        return send(at, at, name, to, i)

    if inside:
        loop(nb, lambda i: small_copy(to_peer(i)).start(), 1)
    send(R.oth, R.xrow.at[rows(s)], K.in_y, ypeer).start()
    row_copy(R.xrow, s, K.in_c, core, 0).start()
    if inside:

        def spread_self(i):
            for a in range(2):
                a_copy(a, same_side(i)).start()

        loop(nb // 2, spread_self, 1)
        for a in range(2):
            a_copy(a, pair).start()
    other = R.wself.at[1 - h]
    y_block(other, me, K.wy_self, LANES).start()

    if inside:
        loop(nb, lambda i: arrived(R.smallr.at[0], K.small, from_peer(i)), 1)
        R.smallr[pl.ds(me, 1)] = R.small[...][None]
        per = LANES // cw
        for t in range(D // LANES):
            tile = R.smallr[t * per]
            for k in range(1, per):
                tile = tile + R.smallr[t * per + k]
            R.gtab[:, t * LANES:(t + 1) * LANES] = tile

        def chosen(l, p):
            row = R.smallr[p, pl.ds(10 + l, 1), :]
            for m, shard in enumerate((R.up, R.dnt)):
                total = None
                for e in range(E):
                    hit = jnp.where(row == float(e), 1.0, 0.0)
                    hit = jnp.concatenate([hit] * (FQ // LANES), axis=1)
                    term = shard[l, e].astype(F32) * hit
                    total = term if total is None else total + term
                R.gE[m, rows(p, cw), lanes(l, FQ)] = total.astype(BF16)

        loop(nb, lambda p: chosen(0, p))
        for m in range(2):
            R.we0[m, rows(me, cw), lanes(h, FQ)] = R.gE[m, rows(me, cw), lanes(0, FQ)]

    arrived(R.xrow.at[rows(sy)], K.in_y)
    row_copy(R.xrow, sy, K.in_c, core, 1).start()

    if inside:

        def near(i):
            p = same_side(i)
            for a in range(2):
                arrived(wblock(held(a), p, h, LANES), K.wa, a * nb + p)
                a_relay(a, p).start()
            y_block(other, p, K.wy_self, LANES).start()

        def far(i):
            p = lax.rem(pair + 2 * i, nb)
            for a in range(2):
                arrived(wblock(held(a), p, h, LANES), K.wr, a * nb + p)
            y_block(other, p, K.wy_self, LANES).start()

        for a in range(2):
            arrived(wblock(held(a), pair, h, LANES), K.wa, a * nb + pair)
        y_block(other, pair, K.wy_self, LANES).start()
        loop(nb // 2, near, 1)
        e_copy(0, pair).start()
        loop(nb // 2, lambda i: e_copy(0, same_side(i)).start(), 1)
        loop(nb // 2, far, 1)
        loop(nb // 2, lambda i: e_copy(0, lax.rem(pair + 2 * i, nb)).start(), 1)
        loop(nb, lambda p: chosen(1, p))
        for m in range(2):
            R.we1[m, rows(me, cw), :] = R.gE[m, rows(me, cw), lanes(1, FQ)]
    else:
        R.gtab[...] = R.small[...]
        for m in range(2):
            R.we0[m, rows(me, cw), lanes(h, FQ)] = R.we[0, m]
            R.we1[m, rows(me, cw), :] = R.we[1, m]

    def send_x():
        if inside:
            loop(nb // 2, lambda i: a_copy(2, same_side(i)).start(), 1)
            a_copy(2, pair).start()

    def near_x():
        def one(i):
            arrived(wblock(R.wx, 0, h, LANES), K.wa, 2 * nb + same_side(i))
            a_relay(2, same_side(i)).start()

        if inside:
            loop(nb // 2, one, 1)

    def send_e1():
        if inside:
            loop(nb, lambda i: e_copy(1, to_peer(i)).start(), 1)

    def finish_x():
        if inside:
            arrived(wblock(R.wx, pair, h, LANES), K.wa, 2 * nb + pair)
            loop(nb // 2, lambda i: arrived(wblock(R.wx, 0, h, LANES), K.wr, 2 * nb + lax.rem(pair + 2 * i, nb)), 1)
        loop(nb, lambda i: y_block(R.wx, to_peer(i), K.wy_x, LANES).start())

    def pass_e0(p):
        if inside:

            @pl.when(p != me)
            def _():
                arrived(wblock(R.we0, p, h, FQ), K.we0, p)

        y_block(R.we0, p, K.wy_e0, FQ).start()

    def y_arrived(buf, name, width):
        loop(nb, lambda i: arrived(wblock(buf, 0, h, width), name, to_peer(i)))

    def y_sent(buf, name, width):
        loop(nb, lambda i: sent(wblock(buf, 0, h, width), name, to_peer(i)))

    @pl.when(is_b)
    def _():
        pass_e0(me)
        if inside:
            pass_e0(pair)

    y_arrived(R.wself.at[h], K.wy_self, LANES)

    R.acc[...] = jnp.zeros((32, D), F32)

    def tally(row, x):
        R.acc[pl.ds(row, 1), :] += jnp.sum(x, 0, keepdims=True)

    def gain(i):
        return R.gtab[pl.ds(i, 1), :]

    def shift(i):
        return R.gtab[pl.ds(5 + i, 1), :]

    def blk(j):
        return c + 2 * j

    def pblk(j):
        return cp + 2 * j

    def src_len(k):
        return R.slen[0, k]

    def tgt_len(k):
        return R.tlen[0, k]

    def self_len(k):
        return jnp.where(is_a, R.slen[0, k], R.tlen[0, k])

    docs = R.slen.shape[1]

    def set_bias(buf, q_start, q_len, k_len, causal, q_axis):
        shape = (B, L) if q_axis == 0 else (L, B)
        q_pos = lax.broadcasted_iota(jnp.int32, (B, 1) if q_axis == 0 else (1, B), q_axis) + q_start
        k_pos = lax.broadcasted_iota(jnp.int32, shape, 1 - q_axis)
        first = jnp.zeros(q_pos.shape, jnp.int32)
        last = jnp.zeros(q_pos.shape, jnp.int32) + k_len(0)
        edge = 0
        for k in range(docs):
            edge = edge + q_len(k)
            passed = q_pos >= edge
            first = first + jnp.where(passed, k_len(k), 0)
            if k + 1 < docs:
                last = last + jnp.where(passed, k_len(k + 1), 0)
        if causal is not None:
            last = jnp.minimum(last, q_pos + jnp.where(causal, 1, L))
        buf[...] = jnp.where((k_pos >= first) & (k_pos < last), 0.0, MASKED)

    lane_head = lax.div(lax.broadcasted_iota(jnp.int32, (1, KW), 1), HEAD_DIM)
    heads = KW // HEAD_DIM

    def attend(q_blk, k_ref, v_ref):
        lane = lax.broadcasted_iota(jnp.int32, (1, LANES), 1)
        out = jnp.zeros((B, KW), F32)
        lse = jnp.zeros((B, LANES), F32)
        for hd in range(heads):
            hrow = jnp.where(lane_head == hd, 1.0, 0.0)
            scores = mm_nt(q_blk * hrow.astype(BF16), k_ref[...]) + R.bias[...]
            top = jnp.max(scores, -1, keepdims=True)
            expos = jnp.exp(scores - top)
            total = jnp.sum(expos, -1, keepdims=True)
            out = out + mm(expos.astype(BF16), v_ref[...]) * (hrow / total)
            lse = lse + jnp.where(lane == hd, top + jnp.log(total), 0.0)
        return out.astype(BF16), jnp.transpose(lse)[0:8, :]

    scale = HEAD_DIM ** (-0.5)

    def row_sums(o_blk, do_blk):
        prod = do_blk.astype(F32) * o_blk.astype(F32)
        high = prod.astype(BF16)
        low = (prod - high.astype(F32)).astype(BF16)
        pick = lax.broadcasted_iota(jnp.int32, (16, KW), 0) == jnp.broadcast_to(lane_head, (16, KW))
        pick = jnp.where(pick, 1.0, 0.0).astype(BF16)
        return mm_nt(pick, high) + mm_nt(pick, low)

    half_head = lax.div(lax.broadcasted_iota(jnp.int32, (1, LANES), 1), HEAD_DIM)

    def back_half(t, count, block_of, first_pass, q_ref, o_ref, lse_ref, k_ref, v_ref, bias_of):
        lt = lanes(t)
        R.dkf[...] = jnp.zeros((L, LANES), F32)
        R.dvf[...] = jnp.zeros((L, LANES), F32)

        def block(i):
            b = block_of(i)
            if first_pass is not None:
                do = first_pass(i, b)
                R.do[rows(b)] = do
                R.drowT[:, rows(b)] = row_sums(o_ref[rows(b)], do)
            bias_of(b)
            q_blk, do_blk = q_ref[rows(b), lt], R.do[rows(b), lt]
            total = jnp.zeros((B, LANES), F32)
            for u in range(LANES // HEAD_DIM):
                hrow = jnp.where(half_head == u, 1.0, 0.0)
                hlow = hrow.astype(BF16)
                at = pl.ds(2 * t + u, 1)
                qm, dom = q_blk * hlow, do_blk * hlow
                probs = jnp.exp(mm_nt(k_ref[:, lt], qm) + R.biasT[...] - lse_ref[at, rows(b)])
                R.dvf[...] += mm(probs.astype(BF16), dom)
                change = probs * (mm_nt(v_ref[:, lt], dom) - R.drowT[at, rows(b)])
                change = change.astype(BF16)
                R.dkf[...] += mm(change, qm)
                total = total + mm_tn(change, k_ref[:, lt]) * hrow
            R.dq[rows(b), lt] = (total * scale).astype(BF16)

        loop(count, block)
        R.dkb[:, lt] = R.dkf[...].astype(BF16)
        R.dvb[:, lt] = R.dvf[...].astype(BF16)

    def half_grads(t, xq_ref, xk_ref, dq_ref, o_ref, b_ref, after=None):
        lt = lanes(t)

        def part(i):
            at, to = lanes(i, 2 * LANES), rows(i, 2 * LANES)
            R.gA[0, to, lt] = mm_tn(xq_ref[:, at], dq_ref[:, lt]).astype(BF16)
            R.gA[1, to, lt] = mm_tn(xk_ref[:, at], R.dkb[:, lt]).astype(BF16)
            R.gA[2, to, lt] = mm_tn(xk_ref[:, at], R.dvb[:, lt]).astype(BF16)
            R.gA[3, to, lt] = mm_tn(b_ref[:, at], o_ref[:, lt]).astype(BF16)
            if after is not None:
                after(i)

        loop(D // (2 * LANES), part)

    loop(2, lambda j: arrived(R.xrow.at[rows(pblk(j))], K.in_c, lax.rem(j + h, 2)))

    def self_project(i):
        x = R.xrow[rows(i)].astype(F32)
        y = norm(x, gain(2 * h), shift(2 * h)).astype(BF16)
        R.nrow[rows(i)] = y
        R.q[rows(i)] = mm(y, R.wself[h, 0]).astype(BF16) * jnp.asarray(scale, BF16)
        R.k[rows(i)] = mm(y, R.wself[h, 1]).astype(BF16)
        R.v[rows(i)] = mm(y, R.wself[h, 2]).astype(BF16)

    loop(4, self_project)

    def self_block(i):
        j = lax.rem(i, 2)
        b = jnp.where(i < 2, cp, c) + 2 * j
        set_bias(R.bias, b * B, self_len, self_len, is_b, 0)
        o, lse = attend(R.q[rows(b)], R.k, R.v)
        R.o[rows(b)] = o
        R.lseT[:, rows(b)] = lse
        y = mm_nt(o, R.wself[h, 3])

        @pl.when(i < 2)
        def _():
            R.cs[j] = y.astype(BF16)
            send(R.cs.at[j], R.cr.at[j], K.rs1, core, j).start()

        @pl.when(i >= 2)
        def _():
            R.part[j] = y

        @pl.when(is_b & (i == 0))
        def _():
            loop(nb // 2, lambda k: pass_e0(same_side(k)), 1)

        @pl.when(i == 1)
        def _():
            send_x()

    loop(4, self_block)

    @pl.when(is_b)
    def _():
        loop(nb // 2, lambda k: pass_e0(lax.rem(pair + 2 * k, nb)), 1)

    near_x()

    @pl.when(is_b)
    def _():
        send_e1()
        y_sent(R.we0, K.wy_e0, FQ)

    def self_end(j):
        arrived(R.cr.at[j], K.rs1, j)
        branch = R.part[j] + R.cr[j].astype(F32)
        x = R.xrow[rows(blk(j))].astype(F32)
        y = x + branch
        R.mid[j] = y
        tally(16 + 2 * h, x * x)
        tally(21 + 2 * h, branch * branch)

        @pl.when(is_a)
        def _():
            R.n2row[rows(blk(j))] = norm(y, gain(1), shift(1)).astype(BF16)
            row_copy(R.n2row, blk(j), K.n2, core, j).start()
            tally(17, y * y)

        @pl.when(is_b & (j == 0))
        def _():
            R.fs[...] = branch.astype(BF16)
            send(R.fs, R.fr, K.br3, ypeer).start()

    loop(2, self_end)

    @pl.when(is_b)
    def _():
        finish_x()

    @pl.when(is_a)
    def _():
        if inside:
            loop(nb, lambda i: arrived(wblock(R.we0, 0, h, FQ), K.we0, from_peer(i)), 1)
        send_e1()
        finish_x()
        y_arrived(R.we0, K.wy_e0, FQ)

        def block(i):
            j = lax.rem(i, 2)
            b = jnp.where(i < 2, c, cp) + 2 * j

            @pl.when(i >= 2)
            def _():
                arrived(R.n2row.at[rows(b)], K.n2, j)

            hid = mm(R.n2row[rows(b)], R.we0[0])
            act, slope = gelu_pair(hid)
            R.g0[rows(b)] = act.astype(BF16)
            R.gp0[rows(b)] = slope.astype(BF16)
            y = mm_nt(R.g0[rows(b)], R.we0[1])

            @pl.when(i < 2)
            def _():
                R.part[j] = y

            @pl.when(i >= 2)
            def _():
                sent(R.cs.at[j], K.rs1, j)
                R.cs[j] = y.astype(BF16)
                send(R.cs.at[j], R.cr.at[j], K.rs2, core, j).start()

        loop(4, block)

        def end(j):
            arrived(R.cr.at[j], K.rs2, j)
            branch = R.part[j] + R.cr[j].astype(F32)
            tally(22, branch * branch)
            R.mrow[rows(blk(j))] = (R.mid[j] + branch).astype(BF16)
            row_copy(R.mrow, blk(j), K.m_y, ypeer, j).start()
            row_copy(R.mrow, blk(j), K.m_c, core, j).start()

        loop(2, end)

    @pl.when(is_a)
    def _():
        arrived(R.fr, K.br3)
        R.t1[...] = R.tgt[...].astype(F32) + R.fr[...].astype(F32)

    @pl.when(is_b)
    def _():
        R.t1[...] = R.mid[1]

    one = R.t1[...]
    tally(19, one * one)
    R.n4c[rows(c)] = norm(one, gain(3), shift(3)).astype(BF16)
    row_copy(R.n4c, c, K.n4, core).start()
    y_arrived(R.wx, K.wy_x, LANES)

    arrived(R.n4c.at[rows(cp)], K.n4)
    row_copy(R.b5, s, K.b5, core, 0).start()
    row_copy(R.b5, s, K.b5, ypeer, 1).start()

    def cross_query(i):
        R.q2[rows(i)] = mm(R.n4c[rows(i)], R.wx[0]).astype(BF16) * jnp.asarray(scale, BF16)

    loop(2, cross_query)

    def memory_block(i):
        j = lax.rem(i, 2)
        b = jnp.where(i < 2, c, cp) + 2 * j

        @pl.when((i < 2) & is_b)
        def _():
            arrived(R.mrow.at[rows(b)], K.m_y, j)
            row_copy(R.mrow, b, K.m_c, core, j).start()

        @pl.when(i >= 2)
        def _():
            arrived(R.mrow.at[rows(b)], K.m_c, j)

        y = R.mrow[rows(b)]
        R.k2[rows(b)] = mm(y, R.wx[1]).astype(BF16)
        R.v2[rows(b)] = mm(y, R.wx[2]).astype(BF16)

    loop(4, memory_block)

    def cross_block(i):
        b = jnp.where(i < 1, cp, c)
        set_bias(R.bias, (2 * h + b) * B, tgt_len, src_len, None, 0)
        o, lse = attend(R.q2[rows(b)], R.k2, R.v2)
        R.o2[rows(b)] = o
        R.lse2T[:, rows(b)] = lse
        y = mm_nt(o, R.wx[3])

        @pl.when(i < 1)
        def _():
            R.ds[...] = y.astype(BF16)
            send(R.ds, R.dr.at[0], K.rs4, core).start()

        @pl.when(i >= 1)
        def _():
            R.part[0] = y

    loop(2, cross_block)
    arrived(R.dr.at[0], K.rs4)
    branch4 = R.part[0] + R.dr[0].astype(F32)
    two = R.t1[...] + branch4
    R.t2[...] = two
    R.n5[rows(s)] = norm(two, gain(4), shift(4)).astype(BF16)
    row_copy(R.n5, s, K.n5, ypeer, 1).start()
    row_copy(R.n5, s, K.n5, core, 0).start()
    tally(24, branch4 * branch4)
    tally(20, two * two)

    if inside:
        loop(nb, lambda i: arrived(R.we1.at[:, rows(0, cw), :], K.we1, from_peer(i)), 1)
    arrived(R.b5.at[rows(sc)], K.b5, 0)
    arrived(R.b5.at[rows(sy)], K.b5, 1)
    row_copy(R.b5, sy, K.b5, core, 2).start()

    def around(m):
        return 2 * lax.rem(h + lax.div(m, 2), 2) + lax.rem(c + lax.rem(m, 2), 2)

    def dec_block(m):
        b = around(m)
        hid = mm(R.n5[rows(b)], R.we1[0])
        act, slope = gelu_pair(hid)
        R.g1[rows(b)] = act.astype(BF16)
        dact = mm(R.b5[rows(b)], R.we1[1])
        R.dh1[rows(b)] = (dact * slope).astype(BF16)
        return mm_nt(R.dh1[rows(b)], R.we1[0])

    def dec_step(i):
        m = jnp.where(i < 2, i, 5 - i)

        @pl.when(i == 1)
        def _():
            arrived(R.n5.at[rows(sc)], K.n5, 0)

        @pl.when(i == 2)
        def _():
            arrived(R.n5.at[rows(sy)], K.n5, 1)
            row_copy(R.n5, sy, K.n5, core, 2).start()
            arrived(R.n5.at[rows(around(3))], K.n5, 2)
            arrived(R.b5.at[rows(around(3))], K.b5, 2)

        y = dec_block(m)

        @pl.when(i == 0)
        def _():
            R.part[1] = y

        @pl.when((i == 1) | (i == 2))
        def _():
            R.es6[i - 1] = y.astype(BF16)
            send(R.es6.at[i - 1], R.er6.at[i - 1], K.rs6, core, i - 1).start()

        @pl.when(i == 3)
        def _():
            arrived(R.er6.at[1], K.rs6, 1)
            R.es6[2] = (y + R.er6[1].astype(F32)).astype(BF16)
            send(R.es6.at[2], R.er6.at[2], K.rs6, ypeer, 2).start()

    loop(4, dec_step)

    def dec_forward(i):
        m = 3 - i
        y = mm_nt(R.g1[rows(around(m))], R.we1[1])

        @pl.when(m == 0)
        def _():
            R.last[...] = y

        @pl.when((m == 1) | (m == 3))
        def _():
            at = lax.div(m, 2)
            R.es[at] = y.astype(BF16)
            send(R.es.at[at], R.er.at[at], K.rs5, core, at).start()

        @pl.when(m == 2)
        def _():
            arrived(R.er.at[1], K.rs5, 1)
            R.es[2] = (y + R.er[1].astype(F32)).astype(BF16)
            send(R.es.at[2], R.er.at[2], K.rs5, ypeer, 2).start()

    loop(4, dec_forward)

    def dp_x(a, p):
        at = rows(lax.div(p, 2), cw)
        return send(R.qA.at[a, :, rows(p, cw), :], R.pA.at[a, :, at, :], K.gd_x, (pair, s), a * nb + p)

    def dp_a(a, p):
        return send(
            R.qA.at[a, :, rows(p, cw), :], R.dpA.at[a, lax.div(me, 2)], K.gd_a, (p, s), a * nb + p, a * nb + me
        )

    def dp_e(l, p):
        return send(R.qE.at[l, :, rows(p, cw), :], R.dpE.at[l, me], K.gd_e, (p, s), l * nb + p, l * nb + me)

    def here(src, dst, i):
        return pltpu.make_async_copy(src, dst, R.ss.at[K.here + i])

    def here_a(a):
        return here(R.qA.at[a, :, rows(me, cw), :], R.dpA.at[a, lax.div(me, 2)], a)

    def here_e(l):
        return here(R.qE.at[l, :, rows(me, cw), :], R.dpE.at[l, me], 3 + l)

    def owners(piece, start):
        if inside:

            def one(i):
                p = piece * (nb // 2) + lax.rem(me + i, nb // 2)

                @pl.when(p != me)
                def _():
                    start(p)

            loop(nb // 2, one)

    def dp_a_start(a, piece):
        if inside:

            def one(i):
                dp_x(a, piece * (nb // 2) + 2 * i + lax.rem(pair, 2)).start()

            loop(nb // 4, one)

    def dp_a_pass(a, piece):
        if inside:

            def one(i):
                p = piece * (nb // 2) + 2 * i + lax.rem(me, 2)
                at = rows(lax.div(p, 2), cw)
                arrived(R.pA.at[a, :, at, :], K.gd_x, a * nb + p)
                for m in range(4):
                    total = R.qA[a, m, rows(p, cw)].astype(F32) + R.pA[a, m, at].astype(F32)
                    R.qA[a, m, rows(p, cw)] = total.astype(BF16)

                @pl.when(p != me)
                def _():
                    dp_a(a, p).start()

            loop(nb // 4, one)

    def dp_e_start(l, piece):
        owners(piece, lambda p: dp_e(l, p).start())

    def keep_a(a):
        if inside:
            here_a(a).start()

    def keep_e(l):
        if inside:
            here_e(l).start()

    half_d = 2 * LANES

    def dec_grads(i):
        at, to = lanes(i, 2 * LANES), rows(i, 2 * LANES)
        R.qE[1, 0, to] = mm_tn(R.n5[:, at], R.dh1[...]).astype(BF16)
        R.qE[1, 1, to] = mm_tn(R.b5[:, at], R.g1[...]).astype(BF16)
        dp_e_start(1, i)

    loop(D // (2 * LANES), dec_grads)
    keep_e(1)

    def add_norm(i, dgain, dbias):
        R.acc[pl.ds(i, 1), :] += dgain
        R.acc[pl.ds(5 + i, 1), :] += dbias

    arrived(R.er6.at[0], K.rs6, 0)
    arrived(R.er6.at[2], K.rs6, 2)
    up = R.part[1] + R.er6[0].astype(F32) + R.er6[2].astype(F32)
    back, dgain, dbias = norm_back(R.t2[...], gain(4), up)
    g4 = R.cot[...].astype(F32) + back
    R.g4[...] = g4
    R.b4c[rows(c)] = g4.astype(BF16)
    row_copy(R.b4c, c, K.b4, core).start()
    add_norm(4, dgain, dbias)


    arrived(R.b4c.at[rows(cp)], K.b4)

    def cross_first(i, b):
        return mm(R.b4c[rows(b)], R.wx[3]).astype(BF16)

    def cross_bias(b):
        set_bias(R.biasT, (2 * h + b) * B, tgt_len, src_len, None, 1)

    for t in range(2):
        back_half(
            t, 2, lambda i: i, cross_first if t == 0 else None, R.q2, R.o2, R.lse2T, R.k2, R.v2, cross_bias
        )

    def memory_back(i):
        j = lax.rem(i, 2)
        b = jnp.where(i < 2, cp, c) + 2 * j
        y = mm_nt(R.dkb[rows(b)], R.wx[1]) + mm_nt(R.dvb[rows(b)], R.wx[2])

        @pl.when((i < 2) & is_a)
        def _():
            sent(R.cs.at[j], K.rs2, j)

        @pl.when((i < 2) & is_b)
        def _():
            sent(R.cs.at[j], K.rs1, j)

        @pl.when(i < 2)
        def _():
            R.cs[j] = y.astype(BF16)
            send(R.cs.at[j], R.cr.at[j], K.rs7m, core, j).start()

        @pl.when(i >= 2)
        def _():
            R.dmem[j] = y

    loop(4, memory_back)

    def cross_dx(i):
        b = jnp.where(i < 1, cp, c)
        y = mm_nt(R.dq[rows(b)], R.wx[0])

        @pl.when(i < 1)
        def _():
            sent(R.ds, K.rs4)
            R.ds[...] = y.astype(BF16)
            send(R.ds, R.dr.at[1], K.rs7q, core).start()

        @pl.when(i >= 1)
        def _():
            R.part[0] = y

    loop(2, cross_dx)

    def memory_sum(j):
        arrived(R.cr.at[j], K.rs7m, j)
        y = R.dmem[j] + R.cr[j].astype(F32)
        R.dmem[j] = y

        @pl.when(is_b)
        def _():
            R.be[rows(j)] = y.astype(BF16)
            send(R.be.at[rows(j)], R.dmr.at[j], K.dm, ypeer, j).start()

    loop(2, memory_sum)

    arrived(R.dr.at[1], K.rs7q)
    back, dgain, dbias = norm_back(R.t1[...], gain(3), R.part[0] + R.dr[1].astype(F32))
    g3 = R.g4[...] + back
    R.g3[...] = g3

    @pl.when(is_a)
    def _():
        R.fs[...] = g3.astype(BF16)
        send(R.fs, R.brow.at[rows(c)], K.g3, ypeer).start()

    add_norm(3, dgain, dbias)

    arrived(R.er.at[0], K.rs5, 0)
    arrived(R.er.at[2], K.rs5, 2)
    branch5 = R.last[...] + R.er[0].astype(F32) + R.er[2].astype(F32)
    tally(25, branch5 * branch5)
    R.dec[...] = R.t2[...] + branch5

    def cross_grads(t):
        half_grads(t, R.n4c, R.mrow, R.dq.at[0:2 * B], R.o2, R.b4c)

    def y_grad_x():
        return send(R.gA.at[:, :, lanes(1 - h)], R.ylX, K.gy_x, ypeer)

    def y_grad_s(i):
        at = rows(i, half_d)
        return send(R.gA.at[:, at, lanes(1 - h)], R.qA.at[h, :, at, :], K.gy_s, ypeer, i)

    cross_grads(1 - h)

    @pl.when(is_a)
    def _():
        y_grad_x().start()

    cross_grads(h)

    def join_x():
        arrived(R.ylX, K.gy_x)
        for m in range(4):
            total = R.gA[m, :, lanes(h)].astype(F32) + R.ylX[m].astype(F32)
            R.qA[2, m] = total.astype(BF16)
        for piece in range(2):
            dp_a_start(2, piece)

    def pass_a(a):
        for piece in range(2):
            dp_a_pass(a, piece)
        keep_a(a)

    if inside:

        def chosen_sent(i):
            for l in range(2):
                sent(wblock(R.gE, 0, l, FQ), (K.we0, K.we1)[l], to_peer(i))

        loop(nb, chosen_sent, 1)

    def e_grad(i):
        at = rows(i, half_d)
        return send(R.gE.at[:, at, lanes(1 - h, FQ)], R.qE.at[0, :, at, :], K.gy_e0, ypeer, i)

    @pl.when(is_a)
    def _():
        def block(i):
            j = lax.rem(i, 2)
            b = jnp.where(i < 2, c, cp) + 2 * j

            @pl.when(i < 2)
            def _():
                arrived(R.dmr.at[j], K.dm, j)
                x = R.dmem[j] + R.dmr[j].astype(F32)
                R.dmem[j] = x
                R.be[rows(b)] = x.astype(BF16)
                row_copy(R.be, b, K.be, core, j).start()

            @pl.when(i >= 2)
            def _():
                arrived(R.be.at[rows(b)], K.be, j)

            dact = mm(R.be[rows(b)], R.we0[1])
            R.gp0[rows(b)] = (dact * R.gp0[rows(b)].astype(F32)).astype(BF16)
            y = mm_nt(R.gp0[rows(b)], R.we0[0])

            @pl.when(i < 2)
            def _():
                R.part[j] = y

            @pl.when(i >= 2)
            def _():
                sent(R.cs.at[j], K.rs7m, j)
                R.cs[j] = y.astype(BF16)
                send(R.cs.at[j], R.cr.at[j], K.rs8, core, j).start()

        loop(4, block)

        def end(j):
            arrived(R.cr.at[j], K.rs8, j)
            up = R.part[j] + R.cr[j].astype(F32)
            back, dgain, dbias = norm_back(R.mid[j], gain(1), up)
            add_norm(1, dgain, dbias)
            g = R.dmem[j] + back
            R.dmem[j] = g
            R.brow[rows(blk(j))] = g.astype(BF16)
            row_copy(R.brow, blk(j), K.brow, core, j).start()

        loop(2, end)

        for half in (1, 0):

            def part(i, half=half):
                at, to, lf = lanes(i, 2 * LANES), rows(i, 2 * LANES), pl.ds(half * FQ, FQ)
                up_part = mm_tn(R.n2row[:, at], R.gp0[:, lf]).astype(BF16)
                down_part = mm_tn(R.be[:, at], R.g0[:, lf]).astype(BF16)
                if half == 1:
                    R.gE[0, to, lf] = up_part
                    R.gE[1, to, lf] = down_part
                    e_grad(i).start()
                else:
                    R.qE[0, 0, to] = up_part
                    R.qE[0, 1, to] = down_part
                    dp_e_start(0, i)

            loop(D // (2 * LANES), part)
        keep_e(0)

    @pl.when(is_b)
    def _():
        R.brow[rows(blk(1))] = R.g3[...].astype(BF16)
        arrived(R.brow.at[rows(blk(0))], K.g3)
        for j in range(2):
            row_copy(R.brow, blk(j), K.brow, core, j).start()

    def self_block_of(i):
        return jnp.where(i < 2, c, cp) + 2 * lax.rem(i, 2)

    def self_first(i, b):
        @pl.when(i >= 2)
        def _():
            arrived(R.brow.at[rows(b)], K.brow, lax.rem(i, 2))

        return mm(R.brow[rows(b)], R.wself[h, 3]).astype(BF16)

    def self_bias(b):
        set_bias(R.biasT, b * B, self_len, self_len, is_b, 1)

    def self_half(t, first_pass):
        back_half(t, 4, self_block_of, first_pass, R.q, R.o, R.lseT, R.k, R.v, self_bias)

    @pl.when(is_b)
    def _():
        for j in range(2):
            sent(R.be.at[rows(j)], K.dm, j)
        y_grad_x().start()

    self_half(1 - h, self_first)
    join_x()

    y_grad_x().wait_send()
    half_grads(1 - h, R.nrow, R.nrow, R.dq, R.o, R.brow, lambda i: y_grad_s(i).start())

    self_half(h, None)
    pass_a(2)

    def own_piece(i):
        at = rows(i, half_d)
        for m in range(4):
            R.qA[h, m, at] = R.gA[m, at, lanes(h)]
        dp_a_start(h, i)

    half_grads(h, R.nrow, R.nrow, R.dq, R.o, R.brow, own_piece)

    def other_pieces():
        for piece in range(2):
            at = rows(piece, half_d)
            arrived(R.qA.at[1 - h, :, at, :], K.gy_s, piece)
            dp_a_start(1 - h, piece)

    @pl.when(is_a)
    def _():
        other_pieces()

    def self_dx(i):
        j = lax.rem(i, 2)
        b = jnp.where(i < 2, cp, c) + 2 * j
        y = mm_nt(R.dq[rows(b)], R.wself[h, 0])
        y = y + mm_nt(R.dkb[rows(b)], R.wself[h, 1])
        y = y + mm_nt(R.dvb[rows(b)], R.wself[h, 2])

        @pl.when((i < 2) & is_a)
        def _():
            sent(R.cs.at[j], K.rs8, j)

        @pl.when((i < 2) & is_b)
        def _():
            sent(R.cs.at[j], K.rs7m, j)

        @pl.when(i < 2)
        def _():
            R.cs[j] = y.astype(BF16)
            send(R.cs.at[j], R.cr.at[j], K.rs9, core, j).start()

        @pl.when(i >= 2)
        def _():
            R.part[j] = y

    loop(4, self_dx)

    def self_final(i):
        j = jnp.where(is_a, 1 - i, i)
        arrived(R.cr.at[j], K.rs9, j)
        x = R.xrow[rows(blk(j))].astype(F32)
        back, dgain, dbias = norm_back(x, gain(2 * h), R.part[j] + R.cr[j].astype(F32))
        add_norm(2 * h, dgain, dbias)

        @pl.when(is_a & (j == 0))
        def _():
            R.sgrad[...] = R.dmem[0] + back

        @pl.when(is_a & (j == 1))
        def _():
            sent(R.fs, K.g3)
            R.fs[...] = (R.dmem[1] + back).astype(BF16)
            send(R.fs, R.fr, K.fin, ypeer).start()

        @pl.when(is_b & (j == 0))
        def _():
            sent(R.fs, K.br3)
            R.fs[...] = back.astype(BF16)
            send(R.fs, R.fr, K.fin, ypeer).start()

        @pl.when(is_b & (j == 1))
        def _():
            R.tgrad[...] = R.g3[...] + back

    loop(2, self_final)
    pass_a(h)

    @pl.when(is_a)
    def _():
        pass_a(1 - h)

    @pl.when(is_b)
    def _():
        for piece in range(2):
            arrived(R.qE.at[0, :, rows(piece, half_d), :], K.gy_e0, piece)
            dp_e_start(0, piece)
        keep_e(0)
        other_pieces()
        pass_a(1 - h)

    send(R.acc, R.accc, K.accc, core).start()
    arrived(R.accc, K.accc)
    R.acc1[...] = R.acc[...] + R.accc[...]
    send(R.acc1, R.accy, K.accy, ypeer).start()
    arrived(R.accy, K.accy)
    R.acc2[...] = R.acc1[...] + R.accy[...]
    R.stats[...] = R.acc2[16:32, :]

    if inside:

        def tile_of(p):
            return lanes(lax.div(p * cw, LANES))

        def acc_copy(p):
            return send(R.acc2.at[0:16, tile_of(p)], R.accd.at[me], K.accd, (p, s), p, me)

        loop(nb, lambda i: acc_copy(to_peer(i)).start(), 1)
        R.picks[...] = R.smallr[...]
    arrived(R.fr, K.fin)

    @pl.when(is_a)
    def _():
        R.tgrad[...] = R.g3[...] + R.fr[...].astype(F32)

    @pl.when(is_b)
    def _():
        R.sgrad[...] = R.fr[...].astype(F32)

    if inside:
        loop(nb, lambda i: arrived(R.accd.at[0], K.accd, from_peer(i)), 1)
        R.ggb[...] = R.acc2[0:16, tile_of(me)]

        def more(i):
            R.ggb[...] += R.accd[from_peer(i)]

        loop(nb, more, 1)
        for l in range(2):
            loop(nb, lambda i, l=l: arrived(R.dpE.at[l, 0], K.gd_e, l * nb + from_peer(i)), 1)
            here_e(l).wait()
        for a in range(3):
            loop(nb // 2, lambda i, a=a: arrived(R.dpA.at[a, 0], K.gd_a, a * nb + same_side(i)), 1)
            here_a(a).wait()
    else:
        R.gacc[...] = R.acc2[0:16, :]

    for name in (K.in_y, K.n4, K.b4, K.rs7q, K.fin):
        sent(R.oth, name)
    for name in (K.in_c, K.m_c, K.brow, K.rs9):
        for j in range(2):
            sent(R.oth, name, j)
    for name in (K.b5, K.n5, K.rs5, K.rs6):
        for j in range(3):
            sent(R.oth, name, j)
    y_sent(other, K.wy_self, LANES)
    y_sent(R.wx, K.wy_x, LANES)
    for piece in range(2):
        y_grad_s(piece).wait_send()
    sent(R.acc, K.accc)
    sent(R.acc1, K.accy)

    @pl.when(is_a)
    def _():
        for name in (K.n2, K.m_y, K.be):
            for j in range(2):
                sent(R.oth, name, j)
        for piece in range(2):
            e_grad(piece).wait_send()

    if inside:

        def drain_side(i):
            for a in range(3):
                sent(R.sendA.at[0], K.wa, a * nb + same_side(i))
                sent(R.sendA.at[0], K.wr, a * nb + same_side(i))
                sent(R.sendA.at[0], K.gd_a, a * nb + same_side(i))
                sent(R.sendA.at[0], K.gd_x, a * nb + lax.rem(pair + 2 * i, nb))

        for a in range(3):
            sent(R.sendA.at[0], K.wa, a * nb + pair)
            sent(R.sendA.at[0], K.gd_x, a * nb + pair)
        loop(nb // 2, drain_side, 1)

        def drain(i):
            p = to_peer(i)
            sent(R.small, K.small, p)
            for l in range(2):
                sent(R.qE.at[l, :, rows(0, cw), :], K.gd_e, l * nb + p)
            sent(R.accd.at[0], K.accd, p)

        loop(nb, drain, 1)


def close_kernel(cfg, names, *refs):
    nb, cw, B, D, FQ, E, _ = cfg
    R = SimpleNamespace(**dict(zip(names, refs, strict=True)))
    dp = lax.axis_index("dp")

    def copy(src, dst, i):
        return pltpu.make_async_copy(src, dst, R.sem.at[i])

    plain = [(R.dec, R.o_dec), (R.sgrad, R.o_sgrad), (R.tgrad, R.o_tgrad)]
    for i, (src, _) in enumerate(plain):
        copy(src, R.vp.at[i], i).start()
    for l in range(2):
        copy(R.dpE.at[l], R.ve.at[l], 3 + l).start()
    for a in range(3):
        copy(R.dpA.at[a], R.va.at[a], 5 + a).start()

    stats = jnp.sum(R.stats[...], -1, keepdims=True) * (1.0 / (4 * B * D))
    root = jnp.broadcast_to(jnp.sqrt(stats), (16, LANES))
    place = lax.broadcasted_iota(jnp.int32, (16, LANES), 0) - lax.broadcasted_iota(jnp.int32, (16, LANES), 1)
    for k in range(2):
        line = jnp.sum(jnp.where(place == 5 * k, root, 0.0), 0, keepdims=True)
        R.o_rms[0, k:k + 1, :] = line[:, 0:5]
    for k in range(LANES // cw):

        @pl.when(lax.rem(dp, LANES // cw) == k)
        def _(k=k):
            R.o_gain[...] = R.ggb[0:5, k * cw:(k + 1) * cw]
            R.o_bias[...] = R.ggb[5:10, k * cw:(k + 1) * cw]

    for i, (src, dst) in enumerate(plain):
        copy(src, R.vp.at[i], i).wait()
        copy(R.vp.at[i], dst, i).start()
    for l in range(2):
        copy(R.dpE.at[l], R.ve.at[l], 3 + l).wait()
        for e in range(E):
            hits = []
            for p in range(nb):
                hit = jnp.where(R.picks[p, 10 + l:11 + l, :] == float(e), 1.0, 0.0)
                hits.append(jnp.concatenate([hit] * (FQ // LANES), axis=1))
            for m, total_ref in enumerate((R.w_up, R.w_dn)):
                total = R.ve[l, 0, m].astype(F32) * hits[0]
                for p in range(1, nb):
                    total = total + R.ve[l, p, m].astype(F32) * hits[p]
                total_ref[l, e] = total
        copy(R.w_up.at[l], R.o_up.at[l], 8 + l).start()
        copy(R.w_dn.at[l], R.o_dn.at[l], 10 + l).start()
    for a in range(3):
        copy(R.dpA.at[a], R.va.at[a], 5 + a).wait()
        for m in range(4):
            total = R.va[a, 0, m].astype(F32)
            for p in range(1, nb // 2):
                total = total + R.va[a, p, m].astype(F32)
            if m < 3:
                R.w_qkv[a, m] = total
            else:
                R.w_out[a] = total
    copy(R.w_qkv, R.o_qkv, 12).start()
    copy(R.w_out, R.o_out, 13).start()
    for i, (_, dst) in enumerate(plain):
        copy(R.vp.at[i], dst, i).wait()
    for l in range(2):
        copy(R.w_up.at[l], R.o_up.at[l], 8 + l).wait()
        copy(R.w_dn.at[l], R.o_dn.at[l], 10 + l).wait()
    copy(R.w_qkv, R.o_qkv, 12).wait()
    copy(R.w_out, R.o_out, 13).wait()


def on_device(
    src_input,
    tgt_input,
    out_cotangent,
    src_lengths,
    tgt_lengths,
    enc_expert,
    dec_expert,
    norm_gains,
    norm_biases,
    qkv_weight,
    out_weight,
    expert_up,
    expert_down,
):
    n = lax.axis_size("dp")
    B, D = src_input.shape[1:]
    cw = norm_gains.shape[1]
    FQ = expert_up.shape[3]
    E = expert_up.shape[1]
    inside = cw % 16 == 0 and LANES % cw == 0 and n % 4 == 0
    wot = jnp.swapaxes(out_weight, 1, 2)
    dnt = jnp.swapaxes(expert_down, 2, 3)
    vmem = pl.BlockSpec(memory_space=pltpu.VMEM)
    smem = pl.BlockSpec(memory_space=pltpu.SMEM)
    anywhere = pl.BlockSpec(memory_space=pl.ANY)

    def f32(*shape):
        return jax.ShapeDtypeStruct(shape, F32)

    def bf16(*shape):
        return jax.ShapeDtypeStruct(shape, BF16)

    scalars = dict(slen=src_lengths, tlen=tgt_lengths)
    operands = dict(src=src_input[0], tgt=tgt_input[0], cot=out_cotangent[0])
    results = dict(dec=f32(B, D), sgrad=f32(B, D), tgrad=f32(B, D), stats=f32(16, D))
    far = {}
    if inside:
        nb, rowsize = n, cw
        scalars.update(epick=enc_expert, dpick=dec_expert)
        operands.update(gains=norm_gains, biases=norm_biases, qkv=qkv_weight, wot=wot, up=expert_up, dnt=dnt)
        results.update(ggb=f32(16, LANES), picks=f32(n, 16, LANES))
        far = dict(dpA=bf16(3, n // 2, 4, cw, LANES), dpE=bf16(2, n, 2, cw, FQ))
    else:
        nb, rowsize = 1, D
        gb = jnp.concatenate([norm_gains, norm_biases], 0).astype(F32)
        small = lax.all_gather(gb, "dp", axis=1, tiled=True)
        small = jnp.concatenate([small, jnp.zeros((6, D), F32)], 0)
        wa = jnp.concatenate([qkv_weight, wot[:, None]], 1)
        wa = lax.all_gather(wa, "dp", axis=2, tiled=True)
        picks = jnp.stack([enc_expert[0, 0], dec_expert[0, 0]])
        we = jnp.stack([expert_up, dnt], 2)
        we = lax.all_gather(we, "dp", axis=3, tiled=True)
        we = jnp.stack([jnp.take(we[l], picks[l], axis=0) for l in range(2)])
        operands.update(small=small, wa=wa, we=we)
        results.update(qA=bf16(3, 4, D, LANES), qE=bf16(2, 2, D, FQ), gacc=f32(16, D))
    cfg = (nb, rowsize, B, D, FQ, E, inside)
    scratch = scratch_list(nb, rowsize, B, D, FQ, inside)
    count = sem_list(nb)[1]
    scratch.update(ss=pltpu.SemaphoreType.DMA((count,)), rs=pltpu.SemaphoreType.DMA((count,)))
    names = tuple(scalars) + tuple(operands) + tuple(results) + tuple(far) + tuple(scratch)
    outs = pl.pallas_call(
        functools.partial(step_kernel, cfg, names),
        name="step",
        out_shape=tuple(results.values()) + tuple(far.values()),
        in_specs=[smem] * len(scalars) + [vmem] * len(operands),
        out_specs=[vmem] * len(results) + [anywhere] * len(far),
        scratch_shapes=list(scratch.values()),
        compiler_params=pltpu.CompilerParams(
            collective_id=1, has_side_effects=True, vmem_limit_bytes=63 << 20
        ),
        cost_estimate=pl.CostEstimate(flops=17 << 30, bytes_accessed=8 << 20, transcendentals=16 << 20),
    )(*scalars.values(), *operands.values())
    made = dict(zip(tuple(results) + tuple(far), outs, strict=True))
    if inside:
        near = dict(stats=vmem, ggb=vmem, picks=vmem, dec=anywhere, sgrad=anywhere, tgrad=anywhere)
        near.update(dpA=anywhere, dpE=anywhere)
        last = dict(
            o_dec=f32(B, D),
            o_sgrad=f32(B, D),
            o_tgrad=f32(B, D),
            o_gain=f32(5, cw),
            o_bias=f32(5, cw),
            o_qkv=f32(3, 3, cw, LANES),
            o_out=f32(3, cw, LANES),
            o_up=f32(2, E, cw, FQ),
            o_dn=f32(2, E, cw, FQ),
            o_rms=f32(1, 2, 5),
        )
        held = dict(
            vp=pltpu.VMEM((3, B, D), F32),
            ve=pltpu.VMEM((2, n, 2, cw, FQ), BF16),
            va=pltpu.VMEM((3, n // 2, 4, cw, LANES), BF16),
            w_up=pltpu.VMEM((2, E, cw, FQ), F32),
            w_dn=pltpu.VMEM((2, E, cw, FQ), F32),
            w_qkv=pltpu.VMEM((3, 3, cw, LANES), F32),
            w_out=pltpu.VMEM((3, cw, LANES), F32),
            sem=pltpu.SemaphoreType.DMA((14,)),
        )
        small_outs = [k in (3, 4, 9) for k in range(len(last))]
        dec, sgrad, tgrad, gains, biases, gqkv, gout, gup, gdn, rms = pl.pallas_call(
            functools.partial(close_kernel, cfg, tuple(near) + tuple(last) + tuple(held)),
            name="close",
            out_shape=tuple(last.values()),
            in_specs=list(near.values()),
            out_specs=[vmem if near_by else anywhere for near_by in small_outs],
            scratch_shapes=list(held.values()),
            compiler_params=pltpu.CompilerParams(vmem_limit_bytes=63 << 20),
            cost_estimate=pl.CostEstimate(flops=16 << 20, bytes_accessed=10 << 20, transcendentals=0),
        )(*[made[name] for name in near])
    else:
        dec, sgrad, tgrad, stats, ga, ge, gacc = outs

        def total(x, axis):
            return lax.psum_scatter(x, "dp", scatter_dimension=axis, tiled=True)

        gains, biases = total(gacc[0:5], 1), total(gacc[5:10], 1)
        ga = total(ga.astype(F32), 2)
        gqkv, gout = ga[:, :3], ga[:, 3]
        match = (picks[:, None] == jnp.arange(E, dtype=jnp.int32)[None]).astype(F32)
        ge = ge.astype(F32)[:, None] * match[:, :, None, None, None]
        ge = total(ge, 3)
        gup, gdn = ge[:, :, 0], ge[:, :, 1]
        length = B * lax.axis_size("seq")
        rms = jnp.sqrt(jnp.sum(stats[:10], 1) / (length * D)).reshape(1, 2, 5)
    return (
        dec[None],
        sgrad[None],
        tgrad[None],
        gains,
        biases,
        gqkv,
        jnp.swapaxes(gout, 1, 2),
        gup,
        jnp.swapaxes(gdn, 2, 3),
        rms,
    )


def solution(mesh):
    placed = (
        P("dp", "seq", None),
        P("dp", "seq", None),
        P("dp", "seq", None),
        P("dp", None),
        P("dp", None),
        P("dp", None),
        P("dp", None),
        P(None, "dp"),
        P(None, "dp"),
        P(None, None, "dp", "seq"),
        P(None, "seq", "dp"),
        P(None, None, "dp", "seq"),
        P(None, None, "seq", "dp"),
    )
    return jax.shard_map(
        on_device,
        mesh=mesh,
        in_specs=placed,
        out_specs=(
            P("dp", "seq", None),
            P("dp", "seq", None),
            P("dp", "seq", None),
            P(None, "dp"),
            P(None, "dp"),
            P(None, None, "dp", "seq"),
            P(None, "seq", "dp"),
            P(None, None, "dp", "seq"),
            P(None, None, "seq", "dp"),
            P("dp", None, None),
        ),
        check_vma=False,
    )
```

time: 283 us -> 203 us (0.72)
  Pallas kernels: 269 us -> 200 us
  local copies, waits for them, and re-layouts: 11.3 us -> 0 us
    pallas_call x1, Pallas kernels: 269 us -> 194 us  [on_device(): pl.pallas_call(functools.partial(step_kernel, cfg, names), name='step', o...]
    unnamed x27 -> x0, local copies, waits for them, and re-layouts: 9.43 us -> none
    pallas_call x0 -> x1, Pallas kernels: none -> 5.79 us  [on_device(): pl.pallas_call(functools.partial(close_kernel, cfg, tuple(near) + tuple(l...]
where the time goes in v2:
time: 203 us; the launch traced here: 202 us
  Pallas kernels  200 us (99%)
  between operations  2.13 us (1%)
    pallas_call x1, Pallas kernels, on_device(): pl.pallas_call(functools.partial(step_kernel, cfg, names), name='step', o...  194 us
    pallas_call x1, Pallas kernels, on_device(): pl.pallas_call(functools.partial(close_kernel, cfg, tuple(near) + tuple(l...  5.79 us

profile of v2, /device:TPU:28, one launch (start us, length us, event | category | flops | bytes accessed | tf_op | source)
XLA Modules:
  0.0 201.8 jit_solution(13692301815085623514)
XLA Ops:
  1.9 193.9 %step.1 = (f32[256,512]{1,0:T(8,128)}, f32[256,512]{1,0:T(8,128)}, f32[256,512]{1,0:T(8,128)}, f32[16,512]{1,0:T(8,128)}, f32[16,128]{1,0:T(8,128)}, /*index=5*/...) custom-call(s32[1,4]{1,0:T(1,128)} %refs_0_.1, s32[1,4]{1,0:T(1,128)} %refs_1_.1, ...), custom_call_target="tpu_custom_call" | custom-call | flops 18253611008 | bytes 8388608 | tf_op jit(solution)/shard_map/step/pallas_call | solution.py:1471
  195.8 5.8 %close.1 = (f32[256,512]{1,0:T(8,128)}, f32[256,512]{1,0:T(8,128)}, f32[256,512]{1,0:T(8,128)}, f32[5,64]{1,0:T(8,128)}, f32[5,64]{1,0:T(8,128)}, /*index=5*/f32...) custom-call(f32[16,512]{1,0:T(8,128)} %get-tuple-element.28.refs_0_,, ...), custom_call_target="tpu_custom_call" | custom-call | flops 16777216 | bytes 10485760 | tf_op jit(solution)/shard_map/close/pallas_call | solution.py:1510

commit v3 on v2

--- a/solution.py
+++ b/solution.py
@@ -77,7 +77,7 @@
         nrow=b(L, D),
         wself=b(2, 4, D, KW),
         wx=b(4, D, KW),
-        we0=b(2, D, F2),
+        we0=b(2, D, FQ),
         we1=b(2, D, FQ),
         gtab=f(16, D),
         q=b(L, KW),
@@ -94,8 +94,10 @@
         cr=b(2, B, D),
         mid=f(2, B, D),
         n2row=b(L, D),
-        g0=b(L, F2),
-        gp0=b(L, F2),
+        g0=b(L, FQ),
+        gp0=b(L, FQ),
+        ms=b(2, B, D),
+        dxr=b(2, B, D),
         mrow=b(L, D),
         fs=b(B, D),
         fr=b(B, D),
@@ -131,7 +133,6 @@
         be=b(L, D),
         dq=b(L, KW),
         gA=b(4, D, KW),
-        gE=b(2, D, F2),
         ylX=b(4, D, LANES),
         acc=f(32, D),
         acc1=f(32, D),
@@ -144,6 +145,7 @@
             small=f(16, LANES),
             smallr=f(nb, 16, LANES),
             sendA=b(3, 4, cw, LANES),
+            gE=b(2, D, F2),
             qA=b(3, 4, D, LANES),
             pA=b(3, 4, D // 2, LANES),
             qE=b(2, 2, D, FQ),
@@ -164,7 +166,6 @@
         we1=nb,
         wy_self=nb,
         wy_x=nb,
-        wy_e0=nb,
         rs1=2,
         n2=2,
         rs2=2,
@@ -188,7 +189,8 @@
         fin=1,
         gy_s=2,
         gy_x=1,
-        gy_e0=2,
+        dx=2,
+        n2y=2,
         gd_a=3 * nb,
         gd_x=3 * nb,
         gd_e=2 * nb,
@@ -250,12 +252,17 @@
 
         lax.fori_loop(start, count, step, 0)
 
+    def flip(a, m):
+        out, bit = a, 1
+        while bit < nb:
+            out = out + bit * lax.rem(lax.div(m, bit), 2) * (1 - 2 * lax.rem(lax.div(a, bit), 2))
+            bit = 2 * bit
+        return out
+
     def to_peer(i):
-        return lax.rem(me + i, nb)
-
-    def from_peer(i):
-        return lax.rem(me + nb - i, nb)
-
+        return flip(me, i)
+
+    from_peer = to_peer
     pair = me + 1 - 2 * lax.rem(me, 2)
 
     barrier = pltpu.get_barrier_semaphore()
@@ -322,10 +329,13 @@
         return send(at, at, name, ypeer, p)
 
     def same_side(i):
-        return lax.rem(me + 2 * i, nb)
+        return flip(me, 2 * i)
+
+    def far_side(i):
+        return flip(pair, 2 * i)
 
     def e_copy(l, p):
-        at = wblock(R.we0, me, h, FQ) if l == 0 else R.we1.at[:, rows(me, cw), :]
+        at = (R.we0, R.we1)[l].at[:, rows(me, cw), :]
         return send(wblock(R.gE, p, l, FQ), at, (K.we0, K.we1)[l], (p, s), p, me)
 
     def row_copy(buf, block, name, to, i=0):
@@ -371,7 +381,7 @@
 
         loop(nb, lambda p: chosen(0, p))
         for m in range(2):
-            R.we0[m, rows(me, cw), lanes(h, FQ)] = R.gE[m, rows(me, cw), lanes(0, FQ)]
+            R.we0[m, rows(me, cw), :] = R.gE[m, rows(me, cw), lanes(0, FQ)]
 
     arrived(R.xrow.at[rows(sy)], K.in_y)
     row_copy(R.xrow, sy, K.in_c, core, 1).start()
@@ -386,7 +396,7 @@
             y_block(other, p, K.wy_self, LANES).start()
 
         def far(i):
-            p = lax.rem(pair + 2 * i, nb)
+            p = far_side(i)
             for a in range(2):
                 arrived(wblock(held(a), p, h, LANES), K.wr, a * nb + p)
             y_block(other, p, K.wy_self, LANES).start()
@@ -395,23 +405,19 @@
             arrived(wblock(held(a), pair, h, LANES), K.wa, a * nb + pair)
         y_block(other, pair, K.wy_self, LANES).start()
         loop(nb // 2, near, 1)
+        loop(nb // 2, lambda i: a_copy(2, same_side(i)).start(), 1)
+        a_copy(2, pair).start()
+        loop(nb // 2, far, 1)
         e_copy(0, pair).start()
         loop(nb // 2, lambda i: e_copy(0, same_side(i)).start(), 1)
-        loop(nb // 2, far, 1)
-        loop(nb // 2, lambda i: e_copy(0, lax.rem(pair + 2 * i, nb)).start(), 1)
         loop(nb, lambda p: chosen(1, p))
         for m in range(2):
             R.we1[m, rows(me, cw), :] = R.gE[m, rows(me, cw), lanes(1, FQ)]
     else:
         R.gtab[...] = R.small[...]
         for m in range(2):
-            R.we0[m, rows(me, cw), lanes(h, FQ)] = R.we[0, m]
+            R.we0[m, rows(me, cw), :] = R.we[0, m]
             R.we1[m, rows(me, cw), :] = R.we[1, m]
-
-    def send_x():
-        if inside:
-            loop(nb // 2, lambda i: a_copy(2, same_side(i)).start(), 1)
-            a_copy(2, pair).start()
 
     def near_x():
         def one(i):
@@ -428,17 +434,8 @@
     def finish_x():
         if inside:
             arrived(wblock(R.wx, pair, h, LANES), K.wa, 2 * nb + pair)
-            loop(nb // 2, lambda i: arrived(wblock(R.wx, 0, h, LANES), K.wr, 2 * nb + lax.rem(pair + 2 * i, nb)), 1)
+            loop(nb // 2, lambda i: arrived(wblock(R.wx, 0, h, LANES), K.wr, 2 * nb + far_side(i)), 1)
         loop(nb, lambda i: y_block(R.wx, to_peer(i), K.wy_x, LANES).start())
-
-    def pass_e0(p):
-        if inside:
-
-            @pl.when(p != me)
-            def _():
-                arrived(wblock(R.we0, p, h, FQ), K.we0, p)
-
-        y_block(R.we0, p, K.wy_e0, FQ).start()
 
     def y_arrived(buf, name, width):
         loop(nb, lambda i: arrived(wblock(buf, 0, h, width), name, to_peer(i)))
@@ -446,12 +443,7 @@
     def y_sent(buf, name, width):
         loop(nb, lambda i: sent(wblock(buf, 0, h, width), name, to_peer(i)))
 
-    @pl.when(is_b)
-    def _():
-        pass_e0(me)
-        if inside:
-            pass_e0(pair)
-
+    near_x()
     y_arrived(R.wself.at[h], K.wy_self, LANES)
 
     R.acc[...] = jnp.zeros((32, D), F32)
@@ -528,31 +520,34 @@
 
     half_head = lax.div(lax.broadcasted_iota(jnp.int32, (1, LANES), 1), HEAD_DIM)
 
-    def back_half(t, count, block_of, first_pass, q_ref, o_ref, lse_ref, k_ref, v_ref, bias_of):
+    def back_half(t, count, block_of, first_pass, q_ref, o_ref, lse_ref, k_ref, v_ref, bias_of, hook=None):
         lt = lanes(t)
         R.dkf[...] = jnp.zeros((L, LANES), F32)
         R.dvf[...] = jnp.zeros((L, LANES), F32)
 
         def block(i):
             b = block_of(i)
+            if hook is not None:
+                hook(i)
             if first_pass is not None:
                 do = first_pass(i, b)
                 R.do[rows(b)] = do
                 R.drowT[:, rows(b)] = row_sums(o_ref[rows(b)], do)
             bias_of(b)
             q_blk, do_blk = q_ref[rows(b), lt], R.do[rows(b), lt]
-            total = jnp.zeros((B, LANES), F32)
-            for u in range(LANES // HEAD_DIM):
-                hrow = jnp.where(half_head == u, 1.0, 0.0)
-                hlow = hrow.astype(BF16)
-                at = pl.ds(2 * t + u, 1)
-                qm, dom = q_blk * hlow, do_blk * hlow
-                probs = jnp.exp(mm_nt(k_ref[:, lt], qm) + R.biasT[...] - lse_ref[at, rows(b)])
-                R.dvf[...] += mm(probs.astype(BF16), dom)
-                change = probs * (mm_nt(v_ref[:, lt], dom) - R.drowT[at, rows(b)])
-                change = change.astype(BF16)
-                R.dkf[...] += mm(change, qm)
-                total = total + mm_tn(change, k_ref[:, lt]) * hrow
+            pairs = range(LANES // HEAD_DIM)
+            masks = [jnp.where(half_head == u, 1.0, 0.0) for u in pairs]
+            lse = jnp.concatenate([lse_ref[pl.ds(2 * t + u, 1), rows(b)] for u in pairs], 1)
+            inner = jnp.concatenate([R.drowT[pl.ds(2 * t + u, 1), rows(b)] for u in pairs], 1)
+            bias = jnp.concatenate([R.biasT[...] for u in pairs], 1)
+            qm = jnp.concatenate([q_blk * mask.astype(BF16) for mask in masks], 0)
+            dom = jnp.concatenate([do_blk * mask.astype(BF16) for mask in masks], 0)
+            probs = jnp.exp(mm_nt(k_ref[:, lt], qm) + bias - lse)
+            change = (probs * (mm_nt(v_ref[:, lt], dom) - inner)).astype(BF16)
+            R.dvf[...] += mm(probs.astype(BF16), dom)
+            R.dkf[...] += mm(change, qm)
+            dq = mm_tn(change, k_ref[:, lt])
+            total = sum(dq[u * B:(u + 1) * B] * masks[u] for u in pairs)
             R.dq[rows(b), lt] = (total * scale).astype(BF16)
 
         loop(count, block)
@@ -603,26 +598,13 @@
         def _():
             R.part[j] = y
 
-        @pl.when(is_b & (i == 0))
-        def _():
-            loop(nb // 2, lambda k: pass_e0(same_side(k)), 1)
-
-        @pl.when(i == 1)
-        def _():
-            send_x()
+        @pl.when(i == 0)
+        def _():
+            if inside:
+                loop(nb // 2, lambda i: e_copy(0, far_side(i)).start(), 1)
+            finish_x()
 
     loop(4, self_block)
-
-    @pl.when(is_b)
-    def _():
-        loop(nb // 2, lambda k: pass_e0(lax.rem(pair + 2 * k, nb)), 1)
-
-    near_x()
-
-    @pl.when(is_b)
-    def _():
-        send_e1()
-        y_sent(R.we0, K.wy_e0, FQ)
 
     def self_end(j):
         arrived(R.cr.at[j], K.rs1, j)
@@ -636,6 +618,7 @@
         @pl.when(is_a)
         def _():
             R.n2row[rows(blk(j))] = norm(y, gain(1), shift(1)).astype(BF16)
+            row_copy(R.n2row, blk(j), K.n2y, ypeer, j).start()
             row_copy(R.n2row, blk(j), K.n2, core, j).start()
             tally(17, y * y)
 
@@ -646,53 +629,61 @@
 
     loop(2, self_end)
 
-    @pl.when(is_b)
-    def _():
-        finish_x()
-
-    @pl.when(is_a)
-    def _():
-        if inside:
-            loop(nb, lambda i: arrived(wblock(R.we0, 0, h, FQ), K.we0, from_peer(i)), 1)
-        send_e1()
-        finish_x()
-        y_arrived(R.we0, K.wy_e0, FQ)
-
-        def block(i):
-            j = lax.rem(i, 2)
-            b = jnp.where(i < 2, c, cp) + 2 * j
-
-            @pl.when(i >= 2)
-            def _():
-                arrived(R.n2row.at[rows(b)], K.n2, j)
-
-            hid = mm(R.n2row[rows(b)], R.we0[0])
-            act, slope = gelu_pair(hid)
-            R.g0[rows(b)] = act.astype(BF16)
-            R.gp0[rows(b)] = slope.astype(BF16)
-            y = mm_nt(R.g0[rows(b)], R.we0[1])
-
-            @pl.when(i < 2)
-            def _():
-                R.part[j] = y
-
-            @pl.when(i >= 2)
-            def _():
-                sent(R.cs.at[j], K.rs1, j)
-                R.cs[j] = y.astype(BF16)
-                send(R.cs.at[j], R.cr.at[j], K.rs2, core, j).start()
-
-        loop(4, block)
-
-        def end(j):
-            arrived(R.cr.at[j], K.rs2, j)
-            branch = R.part[j] + R.cr[j].astype(F32)
-            tally(22, branch * branch)
-            R.mrow[rows(blk(j))] = (R.mid[j] + branch).astype(BF16)
-            row_copy(R.mrow, blk(j), K.m_y, ypeer, j).start()
-            row_copy(R.mrow, blk(j), K.m_c, core, j).start()
-
-        loop(2, end)
+    if inside:
+        loop(nb, lambda i: arrived(R.we0.at[:, rows(0, cw), :], K.we0, from_peer(i)), 1)
+    send_e1()
+
+    def enc_sum(j):
+        arrived(R.cr.at[j], K.rs2, j)
+        y = R.part[j] + R.cr[j].astype(F32)
+        R.part[j] = y
+
+        @pl.when(is_a)
+        def _():
+            R.ms[j] = (R.mid[j] + y).astype(BF16)
+
+        @pl.when(is_b)
+        def _():
+            R.ms[j] = y.astype(BF16)
+
+        send(R.ms.at[j], R.dmr.at[j], K.m_y, ypeer, j).start()
+
+    def enc_block(i):
+        j = lax.div(i, 2)
+        own = lax.rem(i, 2) == 0
+        b = jnp.where(own, c, cp) + 2 * j
+
+        @pl.when(own & is_b)
+        def _():
+            arrived(R.n2row.at[rows(b)], K.n2y, j)
+            row_copy(R.n2row, b, K.n2, core, j).start()
+
+        @pl.when(jnp.logical_not(own))
+        def _():
+            arrived(R.n2row.at[rows(b)], K.n2, j)
+
+        hid = mm(R.n2row[rows(b)], R.we0[0])
+        act, slope = gelu_pair(hid)
+        R.g0[rows(b)] = act.astype(BF16)
+        R.gp0[rows(b)] = slope.astype(BF16)
+        y = mm_nt(R.g0[rows(b)], R.we0[1])
+
+        @pl.when(own)
+        def _():
+            R.part[j] = y
+
+        @pl.when(jnp.logical_not(own))
+        def _():
+            sent(R.cs.at[j], K.rs1, j)
+            R.cs[j] = y.astype(BF16)
+            send(R.cs.at[j], R.cr.at[j], K.rs2, core, j).start()
+
+        @pl.when(i == 2)
+        def _():
+            enc_sum(0)
+
+    loop(4, enc_block)
+    enc_sum(1)
 
     @pl.when(is_a)
     def _():
@@ -722,9 +713,20 @@
         j = lax.rem(i, 2)
         b = jnp.where(i < 2, c, cp) + 2 * j
 
-        @pl.when((i < 2) & is_b)
-        def _():
-            arrived(R.mrow.at[rows(b)], K.m_y, j)
+        @pl.when(i < 2)
+        def _():
+            arrived(R.dmr.at[j], K.m_y, j)
+            branch = R.part[j] + R.dmr[j].astype(F32)
+
+            @pl.when(is_a)
+            def _():
+                tally(22, branch * branch)
+                R.mrow[rows(b)] = (R.mid[j] + branch).astype(BF16)
+
+            @pl.when(is_b)
+            def _():
+                R.mrow[rows(b)] = branch.astype(BF16)
+
             row_copy(R.mrow, b, K.m_c, core, j).start()
 
         @pl.when(i >= 2)
@@ -863,7 +865,7 @@
         if inside:
 
             def one(i):
-                p = piece * (nb // 2) + lax.rem(me + i, nb // 2)
+                p = piece * (nb // 2) + lax.rem(to_peer(i), nb // 2)
 
                 @pl.when(p != me)
                 def _():
@@ -946,67 +948,58 @@
             t, 2, lambda i: i, cross_first if t == 0 else None, R.q2, R.o2, R.lse2T, R.k2, R.v2, cross_bias
         )
 
-    def memory_back(i):
-        j = lax.rem(i, 2)
-        b = jnp.where(i < 2, cp, c) + 2 * j
-        y = mm_nt(R.dkb[rows(b)], R.wx[1]) + mm_nt(R.dvb[rows(b)], R.wx[2])
-
-        @pl.when((i < 2) & is_a)
-        def _():
-            sent(R.cs.at[j], K.rs2, j)
-
-        @pl.when((i < 2) & is_b)
-        def _():
-            sent(R.cs.at[j], K.rs1, j)
-
-        @pl.when(i < 2)
-        def _():
-            R.cs[j] = y.astype(BF16)
-            send(R.cs.at[j], R.cr.at[j], K.rs7m, core, j).start()
-
-        @pl.when(i >= 2)
-        def _():
-            R.dmem[j] = y
-
-    loop(4, memory_back)
-
-    def cross_dx(i):
-        b = jnp.where(i < 1, cp, c)
-        y = mm_nt(R.dq[rows(b)], R.wx[0])
-
-        @pl.when(i < 1)
-        def _():
-            sent(R.ds, K.rs4)
-            R.ds[...] = y.astype(BF16)
-            send(R.ds, R.dr.at[1], K.rs7q, core).start()
-
-        @pl.when(i >= 1)
-        def _():
-            R.part[0] = y
-
-    loop(2, cross_dx)
-
     def memory_sum(j):
         arrived(R.cr.at[j], K.rs7m, j)
         y = R.dmem[j] + R.cr[j].astype(F32)
         R.dmem[j] = y
-
-        @pl.when(is_b)
-        def _():
-            R.be[rows(j)] = y.astype(BF16)
-            send(R.be.at[rows(j)], R.dmr.at[j], K.dm, ypeer, j).start()
-
-    loop(2, memory_sum)
+        sent(R.ms.at[j], K.m_y, j)
+        R.ms[j] = y.astype(BF16)
+        send(R.ms.at[j], R.dmr.at[j], K.dm, ypeer, j).start()
+
+    def memory_back(i):
+        j = lax.div(i, 2)
+        first = lax.rem(i, 2) == 0
+        b = jnp.where(first, cp, c) + 2 * j
+        y = mm_nt(R.dkb[rows(b)], R.wx[1]) + mm_nt(R.dvb[rows(b)], R.wx[2])
+
+        @pl.when(first)
+        def _():
+            sent(R.cs.at[j], K.rs2, j)
+            R.cs[j] = y.astype(BF16)
+            send(R.cs.at[j], R.cr.at[j], K.rs7m, core, j).start()
+
+        @pl.when(jnp.logical_not(first))
+        def _():
+            R.dmem[j] = y
+
+        @pl.when(i == 2)
+        def _():
+            memory_sum(0)
+
+    loop(4, memory_back)
+
+    def cross_dx(i):
+        b = jnp.where(i < 1, cp, c)
+        y = mm_nt(R.dq[rows(b)], R.wx[0])
+
+        @pl.when(i < 1)
+        def _():
+            sent(R.ds, K.rs4)
+            R.ds[...] = y.astype(BF16)
+            send(R.ds, R.dr.at[1], K.rs7q, core).start()
+
+        @pl.when(i >= 1)
+        def _():
+            R.part[0] = y
+
+    loop(2, cross_dx)
+
+    memory_sum(1)
 
     arrived(R.dr.at[1], K.rs7q)
     back, dgain, dbias = norm_back(R.t1[...], gain(3), R.part[0] + R.dr[1].astype(F32))
     g3 = R.g4[...] + back
     R.g3[...] = g3
-
-    @pl.when(is_a)
-    def _():
-        R.fs[...] = g3.astype(BF16)
-        send(R.fs, R.brow.at[rows(c)], K.g3, ypeer).start()
 
     add_norm(3, dgain, dbias)
 
@@ -1027,11 +1020,6 @@
         return send(R.gA.at[:, at, lanes(1 - h)], R.qA.at[h, :, at, :], K.gy_s, ypeer, i)
 
     cross_grads(1 - h)
-
-    @pl.when(is_a)
-    def _():
-        y_grad_x().start()
-
     cross_grads(h)
 
     def join_x():
@@ -1055,73 +1043,85 @@
 
         loop(nb, chosen_sent, 1)
 
-    def e_grad(i):
-        at = rows(i, half_d)
-        return send(R.gE.at[:, at, lanes(1 - h, FQ)], R.qE.at[0, :, at, :], K.gy_e0, ypeer, i)
-
     @pl.when(is_a)
     def _():
-        def block(i):
-            j = lax.rem(i, 2)
-            b = jnp.where(i < 2, c, cp) + 2 * j
-
-            @pl.when(i < 2)
-            def _():
-                arrived(R.dmr.at[j], K.dm, j)
-                x = R.dmem[j] + R.dmr[j].astype(F32)
-                R.dmem[j] = x
-                R.be[rows(b)] = x.astype(BF16)
-                row_copy(R.be, b, K.be, core, j).start()
-
-            @pl.when(i >= 2)
-            def _():
-                arrived(R.be.at[rows(b)], K.be, j)
-
-            dact = mm(R.be[rows(b)], R.we0[1])
-            R.gp0[rows(b)] = (dact * R.gp0[rows(b)].astype(F32)).astype(BF16)
-            y = mm_nt(R.gp0[rows(b)], R.we0[0])
-
-            @pl.when(i < 2)
-            def _():
-                R.part[j] = y
-
-            @pl.when(i >= 2)
-            def _():
-                sent(R.cs.at[j], K.rs7m, j)
-                R.cs[j] = y.astype(BF16)
-                send(R.cs.at[j], R.cr.at[j], K.rs8, core, j).start()
-
-        loop(4, block)
-
-        def end(j):
-            arrived(R.cr.at[j], K.rs8, j)
-            up = R.part[j] + R.cr[j].astype(F32)
-            back, dgain, dbias = norm_back(R.mid[j], gain(1), up)
-            add_norm(1, dgain, dbias)
-            g = R.dmem[j] + back
-            R.dmem[j] = g
-            R.brow[rows(blk(j))] = g.astype(BF16)
-            row_copy(R.brow, blk(j), K.brow, core, j).start()
-
-        loop(2, end)
-
-        for half in (1, 0):
-
-            def part(i, half=half):
-                at, to, lf = lanes(i, 2 * LANES), rows(i, 2 * LANES), pl.ds(half * FQ, FQ)
-                up_part = mm_tn(R.n2row[:, at], R.gp0[:, lf]).astype(BF16)
-                down_part = mm_tn(R.be[:, at], R.g0[:, lf]).astype(BF16)
-                if half == 1:
-                    R.gE[0, to, lf] = up_part
-                    R.gE[1, to, lf] = down_part
-                    e_grad(i).start()
-                else:
-                    R.qE[0, 0, to] = up_part
-                    R.qE[0, 1, to] = down_part
-                    dp_e_start(0, i)
-
-            loop(D // (2 * LANES), part)
-        keep_e(0)
+        R.fs[...] = R.g3[...].astype(BF16)
+
+    def enc_back_sum(j):
+        arrived(R.cr.at[j], K.rs8, j)
+        y = R.part[j] + R.cr[j].astype(F32)
+        R.part[j] = y
+
+        @pl.when(is_b)
+        def _():
+            sent(R.ms.at[j], K.dm, j)
+            R.ms[j] = y.astype(BF16)
+            send(R.ms.at[j], R.dxr.at[j], K.dx, ypeer, j).start()
+
+    def enc_back(i):
+        j = lax.div(i, 2)
+        own = lax.rem(i, 2) == 0
+        b = jnp.where(own, c, cp) + 2 * j
+
+        @pl.when(own)
+        def _():
+            arrived(R.dmr.at[j], K.dm, j)
+            x = R.dmem[j] + R.dmr[j].astype(F32)
+            R.dmem[j] = x
+            R.be[rows(b)] = x.astype(BF16)
+            row_copy(R.be, b, K.be, core, j).start()
+
+        @pl.when(jnp.logical_not(own))
+        def _():
+            arrived(R.be.at[rows(b)], K.be, j)
+
+        dact = mm(R.be[rows(b)], R.we0[1])
+        R.gp0[rows(b)] = (dact * R.gp0[rows(b)].astype(F32)).astype(BF16)
+        y = mm_nt(R.gp0[rows(b)], R.we0[0])
+
+        @pl.when(own)
+        def _():
+            R.part[j] = y
+
+        @pl.when(jnp.logical_not(own))
+        def _():
+            sent(R.cs.at[j], K.rs7m, j)
+            R.cs[j] = y.astype(BF16)
+            send(R.cs.at[j], R.cr.at[j], K.rs8, core, j).start()
+
+        @pl.when(i == 2)
+        def _():
+            enc_back_sum(0)
+
+        @pl.when((i == 2) & is_a)
+        def _():
+            send(R.fs, R.brow.at[rows(c)], K.g3, ypeer).start()
+
+    loop(4, enc_back)
+    enc_back_sum(1)
+
+    @pl.when(is_a)
+    def _():
+        y_grad_x().start()
+
+    def enc_grads(i):
+        at, to = lanes(i, 2 * LANES), rows(i, 2 * LANES)
+        R.qE[0, 0, to] = mm_tn(R.n2row[:, at], R.gp0[...]).astype(BF16)
+        R.qE[0, 1, to] = mm_tn(R.be[:, at], R.g0[...]).astype(BF16)
+        dp_e_start(0, i)
+
+    loop(D // (2 * LANES), enc_grads)
+    keep_e(0)
+
+    def enc_end(j):
+        arrived(R.dxr.at[j], K.dx, j)
+        up = R.part[j] + R.dxr[j].astype(F32)
+        back, dgain, dbias = norm_back(R.mid[j], gain(1), up)
+        add_norm(1, dgain, dbias)
+        g = R.dmem[j] + back
+        R.dmem[j] = g
+        R.brow[rows(blk(j))] = g.astype(BF16)
+        row_copy(R.brow, blk(j), K.brow, core, j).start()
 
     @pl.when(is_b)
     def _():
@@ -1131,35 +1131,45 @@
             row_copy(R.brow, blk(j), K.brow, core, j).start()
 
     def self_block_of(i):
-        return jnp.where(i < 2, c, cp) + 2 * lax.rem(i, 2)
+        return jnp.where(lax.rem(i, 2) == 0, c, cp) + 2 * lax.div(i, 2)
 
     def self_first(i, b):
-        @pl.when(i >= 2)
-        def _():
-            arrived(R.brow.at[rows(b)], K.brow, lax.rem(i, 2))
+        j = lax.div(i, 2)
+
+        @pl.when(is_a & (lax.rem(i, 2) == 0))
+        def _():
+            enc_end(j)
+
+        @pl.when(lax.rem(i, 2) == 1)
+        def _():
+            arrived(R.brow.at[rows(b)], K.brow, j)
 
         return mm(R.brow[rows(b)], R.wself[h, 3]).astype(BF16)
 
     def self_bias(b):
         set_bias(R.biasT, b * B, self_len, self_len, is_b, 1)
 
-    def self_half(t, first_pass):
-        back_half(t, 4, self_block_of, first_pass, R.q, R.o, R.lseT, R.k, R.v, self_bias)
+    def self_half(t, first_pass, hook=None):
+        back_half(t, 4, self_block_of, first_pass, R.q, R.o, R.lseT, R.k, R.v, self_bias, hook)
 
     @pl.when(is_b)
     def _():
         for j in range(2):
-            sent(R.be.at[rows(j)], K.dm, j)
+            sent(R.ms.at[j], K.dx, j)
         y_grad_x().start()
 
     self_half(1 - h, self_first)
-    join_x()
 
     y_grad_x().wait_send()
+
     half_grads(1 - h, R.nrow, R.nrow, R.dq, R.o, R.brow, lambda i: y_grad_s(i).start())
 
-    self_half(h, None)
-    pass_a(2)
+    def second_hook(i):
+        @pl.when(i == 2)
+        def _():
+            join_x()
+
+    self_half(h, None, second_hook)
 
     def own_piece(i):
         at = rows(i, half_d)
@@ -1174,10 +1184,6 @@
             at = rows(piece, half_d)
             arrived(R.qA.at[1 - h, :, at, :], K.gy_s, piece)
             dp_a_start(1 - h, piece)
-
-    @pl.when(is_a)
-    def _():
-        other_pieces()
 
     def self_dx(i):
         j = lax.rem(i, 2)
@@ -1186,16 +1192,9 @@
         y = y + mm_nt(R.dkb[rows(b)], R.wself[h, 1])
         y = y + mm_nt(R.dvb[rows(b)], R.wself[h, 2])
 
-        @pl.when((i < 2) & is_a)
+        @pl.when(i < 2)
         def _():
             sent(R.cs.at[j], K.rs8, j)
-
-        @pl.when((i < 2) & is_b)
-        def _():
-            sent(R.cs.at[j], K.rs7m, j)
-
-        @pl.when(i < 2)
-        def _():
             R.cs[j] = y.astype(BF16)
             send(R.cs.at[j], R.cr.at[j], K.rs9, core, j).start()
 
@@ -1204,6 +1203,7 @@
             R.part[j] = y
 
     loop(4, self_dx)
+    pass_a(2)
 
     def self_final(i):
         j = jnp.where(is_a, 1 - i, i)
@@ -1220,38 +1220,26 @@
         def _():
             sent(R.fs, K.g3)
             R.fs[...] = (R.dmem[1] + back).astype(BF16)
-            send(R.fs, R.fr, K.fin, ypeer).start()
 
         @pl.when(is_b & (j == 0))
         def _():
             sent(R.fs, K.br3)
             R.fs[...] = back.astype(BF16)
-            send(R.fs, R.fr, K.fin, ypeer).start()
 
         @pl.when(is_b & (j == 1))
         def _():
             R.tgrad[...] = R.g3[...] + back
 
     loop(2, self_final)
-    pass_a(h)
-
-    @pl.when(is_a)
-    def _():
-        pass_a(1 - h)
-
-    @pl.when(is_b)
-    def _():
-        for piece in range(2):
-            arrived(R.qE.at[0, :, rows(piece, half_d), :], K.gy_e0, piece)
-            dp_e_start(0, piece)
-        keep_e(0)
-        other_pieces()
-        pass_a(1 - h)
 
     send(R.acc, R.accc, K.accc, core).start()
+
+    other_pieces()
     arrived(R.accc, K.accc)
     R.acc1[...] = R.acc[...] + R.accc[...]
     send(R.acc1, R.accy, K.accy, ypeer).start()
+    send(R.fs, R.fr, K.fin, ypeer).start()
+    pass_a(h)
     arrived(R.accy, K.accy)
     R.acc2[...] = R.acc1[...] + R.accy[...]
     R.stats[...] = R.acc2[16:32, :]
@@ -1266,6 +1254,8 @@
 
         loop(nb, lambda i: acc_copy(to_peer(i)).start(), 1)
         R.picks[...] = R.smallr[...]
+
+    pass_a(1 - h)
     arrived(R.fr, K.fin)
 
     @pl.when(is_a)
@@ -1295,7 +1285,7 @@
 
     for name in (K.in_y, K.n4, K.b4, K.rs7q, K.fin):
         sent(R.oth, name)
-    for name in (K.in_c, K.m_c, K.brow, K.rs9):
+    for name in (K.in_c, K.m_c, K.brow, K.rs9, K.n2, K.be):
         for j in range(2):
             sent(R.oth, name, j)
     for name in (K.b5, K.n5, K.rs5, K.rs6):
@@ -1310,11 +1300,9 @@
 
     @pl.when(is_a)
     def _():
-        for name in (K.n2, K.m_y, K.be):
+        for name in (K.n2y, K.dm):
             for j in range(2):
                 sent(R.oth, name, j)
-        for piece in range(2):
-            e_grad(piece).wait_send()
 
     if inside:
 
@@ -1323,7 +1311,7 @@
                 sent(R.sendA.at[0], K.wa, a * nb + same_side(i))
                 sent(R.sendA.at[0], K.wr, a * nb + same_side(i))
                 sent(R.sendA.at[0], K.gd_a, a * nb + same_side(i))
-                sent(R.sendA.at[0], K.gd_x, a * nb + lax.rem(pair + 2 * i, nb))
+                sent(R.sendA.at[0], K.gd_x, a * nb + far_side(i))
 
         for a in range(3):
             sent(R.sendA.at[0], K.wa, a * nb + pair)
@@ -1374,16 +1362,12 @@
         copy(R.vp.at[i], dst, i).start()
     for l in range(2):
         copy(R.dpE.at[l], R.ve.at[l], 3 + l).wait()
-        for e in range(E):
-            hits = []
-            for p in range(nb):
-                hit = jnp.where(R.picks[p, 10 + l:11 + l, :] == float(e), 1.0, 0.0)
-                hits.append(jnp.concatenate([hit] * (FQ // LANES), axis=1))
-            for m, total_ref in enumerate((R.w_up, R.w_dn)):
-                total = R.ve[l, 0, m].astype(F32) * hits[0]
-                for p in range(1, nb):
-                    total = total + R.ve[l, p, m].astype(F32) * hits[p]
-                total_ref[l, e] = total
+        R.w_up[l] = jnp.zeros((E, cw, FQ), F32)
+        R.w_dn[l] = jnp.zeros((E, cw, FQ), F32)
+        for p in range(nb):
+            e = jnp.max(R.picks[p, 10 + l:11 + l, :]).astype(jnp.int32)
+            R.w_up[l, pl.ds(e, 1)] += R.ve[l, p, 0].astype(F32)[None]
+            R.w_dn[l, pl.ds(e, 1)] += R.ve[l, p, 1].astype(F32)[None]
         copy(R.w_up.at[l], R.o_up.at[l], 8 + l).start()
         copy(R.w_dn.at[l], R.o_dn.at[l], 10 + l).start()
     for a in range(3):
@@ -1427,7 +1411,7 @@
     cw = norm_gains.shape[1]
     FQ = expert_up.shape[3]
     E = expert_up.shape[1]
-    inside = cw % 16 == 0 and LANES % cw == 0 and n % 4 == 0
+    inside = cw % 16 == 0 and LANES % cw == 0 and n % 4 == 0 and n & (n - 1) == 0
     wot = jnp.swapaxes(out_weight, 1, 2)
     dnt = jnp.swapaxes(expert_down, 2, 3)
     vmem = pl.BlockSpec(memory_space=pltpu.VMEM)

time: 203 us -> 188 us (0.926)
  Pallas kernels: 200 us -> 186 us
    pallas_call x1, Pallas kernels: 194 us -> 181 us  [on_device(): pl.pallas_call(functools.partial(step_kernel, cfg, names), name='step', o...]
where the time goes in v3:
time: 188 us
  Pallas kernels  186 us (99%)
  between operations  2.13 us (1%)
    pallas_call x1, Pallas kernels, on_device(): pl.pallas_call(functools.partial(step_kernel, cfg, names), name='step', o...  181 us
    pallas_call x1, Pallas kernels, on_device(): pl.pallas_call(functools.partial(close_kernel, cfg, tuple(near) + tuple(l...  5.14 us

profile of v3, /device:TPU:28, one launch (start us, length us, event | category | flops | bytes accessed | tf_op | source)
XLA Modules:
  0.0 188.0 jit_solution(7453540083771356208)
XLA Ops:
  1.9 180.7 %step.1 = (f32[256,512]{1,0:T(8,128)}, f32[256,512]{1,0:T(8,128)}, f32[256,512]{1,0:T(8,128)}, f32[16,512]{1,0:T(8,128)}, f32[16,128]{1,0:T(8,128)}, /*index=5*/...) custom-call(s32[1,4]{1,0:T(1,128)} %refs_0_.1, s32[1,4]{1,0:T(1,128)} %refs_1_.1, ...), custom_call_target="tpu_custom_call" | custom-call | flops 18253611008 | bytes 8388608 | tf_op jit(solution)/shard_map/step/pallas_call | solution.py:1455
  182.6 5.1 %close.1 = (f32[256,512]{1,0:T(8,128)}, f32[256,512]{1,0:T(8,128)}, f32[256,512]{1,0:T(8,128)}, f32[5,64]{1,0:T(8,128)}, f32[5,64]{1,0:T(8,128)}, /*index=5*/f32...) custom-call(f32[16,512]{1,0:T(8,128)} %get-tuple-element.28.refs_0_,, ...), custom_call_target="tpu_custom_call" | custom-call | flops 16777216 | bytes 10485760 | tf_op jit(solution)/shard_map/close/pallas_call | solution.py:1494

commit v4 on v3

--- a/solution.py
+++ b/solution.py
@@ -133,12 +133,18 @@
         be=b(L, D),
         dq=b(L, KW),
         gA=b(4, D, KW),
+        gX=b(4, D, KW),
         ylX=b(4, D, LANES),
         acc=f(32, D),
         acc1=f(32, D),
         acc2=f(32, D),
         accc=f(32, D),
         accy=f(32, D),
+        dec=f(B, D),
+        sgrad=f(B, D),
+        tgrad=f(B, D),
+        stats=f(16, D),
+        ggb=f(16, LANES),
     )
     if inside:
         out.update(
@@ -159,13 +165,13 @@
         in_y=1,
         in_c=2,
         b5=3,
-        small=nb,
-        wa=3 * nb,
-        wr=3 * nb,
-        we0=nb,
-        we1=nb,
-        wy_self=nb,
-        wy_x=nb,
+        small=1,
+        wa=3 * (nb // 2),
+        wr=3 * (nb // 2),
+        we0=1,
+        we1=1,
+        wy_self=1,
+        wy_x=1,
         rs1=2,
         n2=2,
         rs2=2,
@@ -191,13 +197,14 @@
         gy_x=1,
         dx=2,
         n2y=2,
-        gd_a=3 * nb,
-        gd_x=3 * nb,
-        gd_e=2 * nb,
+        gd_a=3,
+        gd_x=6,
+        gd_e=2,
         accc=1,
         accy=1,
-        accd=nb,
+        accd=1,
         here=5,
+        put=6,
     )
     base, at = {}, 0
     for name, number in counts.items():
@@ -309,7 +316,7 @@
     pl.semaphore_wait(barrier, nb + 1)
 
     def small_copy(p):
-        return send(R.small, R.smallr.at[me], K.small, (p, s), p, me)
+        return send(R.small, R.smallr.at[me], K.small, (p, s))
 
     def wblock(buf, p, half, width):
         return buf.at[:, rows(p, cw), lanes(half, width)]
@@ -317,16 +324,17 @@
     def held(a):
         return R.wself.at[a] if a < 2 else R.wx
 
-    def a_copy(a, p):
-        return send(R.sendA.at[a], wblock(held(a), me, h, LANES), K.wa, (p, s), a * nb + p, a * nb + me)
-
-    def a_relay(a, p):
-        at = wblock(held(a), p, h, LANES)
-        return send(at, at, K.wr, (pair, s), a * nb + p)
+    def a_copy(a, i):
+        p = jnp.where(i == 0, pair, same_side(i))
+        return send(R.sendA.at[a], wblock(held(a), me, h, LANES), K.wa, (p, s), a * (nb // 2) + i)
+
+    def a_relay(a, i):
+        at = wblock(held(a), same_side(i), h, LANES)
+        return send(at, at, K.wr, (pair, s), a * (nb // 2) + i)
 
     def y_block(buf, p, name, width):
         at = wblock(buf, p, h, width)
-        return send(at, at, name, ypeer, p)
+        return send(at, at, name, ypeer)
 
     def same_side(i):
         return flip(me, 2 * i)
@@ -336,7 +344,7 @@
 
     def e_copy(l, p):
         at = (R.we0, R.we1)[l].at[:, rows(me, cw), :]
-        return send(wblock(R.gE, p, l, FQ), at, (K.we0, K.we1)[l], (p, s), p, me)
+        return send(wblock(R.gE, p, l, FQ), at, (K.we0, K.we1)[l], (p, s))
 
     def row_copy(buf, block, name, to, i=0):
         at = buf.at[rows(block)]
@@ -350,16 +358,16 @@
 
         def spread_self(i):
             for a in range(2):
-                a_copy(a, same_side(i)).start()
+                a_copy(a, i).start()
 
         loop(nb // 2, spread_self, 1)
         for a in range(2):
-            a_copy(a, pair).start()
+            a_copy(a, 0).start()
     other = R.wself.at[1 - h]
     y_block(other, me, K.wy_self, LANES).start()
 
     if inside:
-        loop(nb, lambda i: arrived(R.smallr.at[0], K.small, from_peer(i)), 1)
+        arrived(R.smallr.at[pl.ds(0, nb - 1)], K.small)
         R.smallr[pl.ds(me, 1)] = R.small[...][None]
         per = LANES // cw
         for t in range(D // LANES):
@@ -380,49 +388,72 @@
                 R.gE[m, rows(p, cw), lanes(l, FQ)] = total.astype(BF16)
 
         loop(nb, lambda p: chosen(0, p))
+        loop(nb // 2, lambda i: a_copy(2, i).start(), 1)
+        a_copy(2, 0).start()
         for m in range(2):
             R.we0[m, rows(me, cw), :] = R.gE[m, rows(me, cw), lanes(0, FQ)]
 
     arrived(R.xrow.at[rows(sy)], K.in_y)
     row_copy(R.xrow, sy, K.in_c, core, 1).start()
+
+    def gain(i):
+        return R.gtab[pl.ds(i, 1), :]
+
+    def shift(i):
+        return R.gtab[pl.ds(5 + i, 1), :]
+
+    def blk(j):
+        return c + 2 * j
+
+    def pblk(j):
+        return cp + 2 * j
+
+    def self_norms():
+        loop(2, lambda j: arrived(R.xrow.at[rows(pblk(j))], K.in_c, lax.rem(j + h, 2)))
+
+        def one(i):
+            x = R.xrow[rows(i)].astype(F32)
+            R.nrow[rows(i)] = norm(x, gain(2 * h), shift(2 * h)).astype(BF16)
+
+        loop(4, one)
 
     if inside:
 
         def near(i):
             p = same_side(i)
             for a in range(2):
-                arrived(wblock(held(a), p, h, LANES), K.wa, a * nb + p)
-                a_relay(a, p).start()
+                arrived(wblock(held(a), p, h, LANES), K.wa, a * (nb // 2) + i)
+                a_relay(a, i).start()
             y_block(other, p, K.wy_self, LANES).start()
 
         def far(i):
             p = far_side(i)
             for a in range(2):
-                arrived(wblock(held(a), p, h, LANES), K.wr, a * nb + p)
+                arrived(wblock(held(a), p, h, LANES), K.wr, a * (nb // 2) + i)
             y_block(other, p, K.wy_self, LANES).start()
 
         for a in range(2):
-            arrived(wblock(held(a), pair, h, LANES), K.wa, a * nb + pair)
+            arrived(wblock(held(a), pair, h, LANES), K.wa, a * (nb // 2))
         y_block(other, pair, K.wy_self, LANES).start()
         loop(nb // 2, near, 1)
-        loop(nb // 2, lambda i: a_copy(2, same_side(i)).start(), 1)
-        a_copy(2, pair).start()
-        loop(nb // 2, far, 1)
         e_copy(0, pair).start()
         loop(nb // 2, lambda i: e_copy(0, same_side(i)).start(), 1)
+        self_norms()
+        loop(nb // 2, far, 1)
         loop(nb, lambda p: chosen(1, p))
         for m in range(2):
             R.we1[m, rows(me, cw), :] = R.gE[m, rows(me, cw), lanes(1, FQ)]
     else:
         R.gtab[...] = R.small[...]
+        self_norms()
         for m in range(2):
             R.we0[m, rows(me, cw), :] = R.we[0, m]
             R.we1[m, rows(me, cw), :] = R.we[1, m]
 
     def near_x():
         def one(i):
-            arrived(wblock(R.wx, 0, h, LANES), K.wa, 2 * nb + same_side(i))
-            a_relay(2, same_side(i)).start()
+            arrived(wblock(R.wx, 0, h, LANES), K.wa, 2 * (nb // 2) + i)
+            a_relay(2, i).start()
 
         if inside:
             loop(nb // 2, one, 1)
@@ -433,15 +464,15 @@
 
     def finish_x():
         if inside:
-            arrived(wblock(R.wx, pair, h, LANES), K.wa, 2 * nb + pair)
-            loop(nb // 2, lambda i: arrived(wblock(R.wx, 0, h, LANES), K.wr, 2 * nb + far_side(i)), 1)
+            arrived(wblock(R.wx, pair, h, LANES), K.wa, 2 * (nb // 2))
+            loop(nb // 2, lambda i: arrived(wblock(R.wx, 0, h, LANES), K.wr, 2 * (nb // 2) + i), 1)
         loop(nb, lambda i: y_block(R.wx, to_peer(i), K.wy_x, LANES).start())
 
     def y_arrived(buf, name, width):
-        loop(nb, lambda i: arrived(wblock(buf, 0, h, width), name, to_peer(i)))
+        arrived(buf.at[:, :, lanes(1 - h, width)], name)
 
     def y_sent(buf, name, width):
-        loop(nb, lambda i: sent(wblock(buf, 0, h, width), name, to_peer(i)))
+        sent(buf.at[:, :, lanes(h, width)], name)
 
     near_x()
     y_arrived(R.wself.at[h], K.wy_self, LANES)
@@ -450,18 +481,6 @@
 
     def tally(row, x):
         R.acc[pl.ds(row, 1), :] += jnp.sum(x, 0, keepdims=True)
-
-    def gain(i):
-        return R.gtab[pl.ds(i, 1), :]
-
-    def shift(i):
-        return R.gtab[pl.ds(5 + i, 1), :]
-
-    def blk(j):
-        return c + 2 * j
-
-    def pblk(j):
-        return cp + 2 * j
 
     def src_len(k):
         return R.slen[0, k]
@@ -554,30 +573,28 @@
         R.dkb[:, lt] = R.dkf[...].astype(BF16)
         R.dvb[:, lt] = R.dvf[...].astype(BF16)
 
-    def half_grads(t, xq_ref, xk_ref, dq_ref, o_ref, b_ref, after=None):
+    def half_grads(to_ref, t, xq_ref, xk_ref, dq_ref, o_ref, b_ref, after=None):
         lt = lanes(t)
 
         def part(i):
             at, to = lanes(i, 2 * LANES), rows(i, 2 * LANES)
-            R.gA[0, to, lt] = mm_tn(xq_ref[:, at], dq_ref[:, lt]).astype(BF16)
-            R.gA[1, to, lt] = mm_tn(xk_ref[:, at], R.dkb[:, lt]).astype(BF16)
-            R.gA[2, to, lt] = mm_tn(xk_ref[:, at], R.dvb[:, lt]).astype(BF16)
-            R.gA[3, to, lt] = mm_tn(b_ref[:, at], o_ref[:, lt]).astype(BF16)
+            to_ref[0, to, lt] = mm_tn(xq_ref[:, at], dq_ref[:, lt]).astype(BF16)
+            to_ref[1, to, lt] = mm_tn(xk_ref[:, at], R.dkb[:, lt]).astype(BF16)
+            to_ref[2, to, lt] = mm_tn(xk_ref[:, at], R.dvb[:, lt]).astype(BF16)
+            to_ref[3, to, lt] = mm_tn(b_ref[:, at], o_ref[:, lt]).astype(BF16)
             if after is not None:
                 after(i)
 
         loop(D // (2 * LANES), part)
 
-    loop(2, lambda j: arrived(R.xrow.at[rows(pblk(j))], K.in_c, lax.rem(j + h, 2)))
-
     def self_project(i):
-        x = R.xrow[rows(i)].astype(F32)
-        y = norm(x, gain(2 * h), shift(2 * h)).astype(BF16)
-        R.nrow[rows(i)] = y
+        y = R.nrow[rows(i)]
         R.q[rows(i)] = mm(y, R.wself[h, 0]).astype(BF16) * jnp.asarray(scale, BF16)
         R.k[rows(i)] = mm(y, R.wself[h, 1]).astype(BF16)
         R.v[rows(i)] = mm(y, R.wself[h, 2]).astype(BF16)
 
+    if inside:
+        loop(nb // 2, lambda i: e_copy(0, far_side(i)).start(), 1)
     loop(4, self_project)
 
     def self_block(i):
@@ -600,8 +617,6 @@
 
         @pl.when(i == 0)
         def _():
-            if inside:
-                loop(nb // 2, lambda i: e_copy(0, far_side(i)).start(), 1)
             finish_x()
 
     loop(4, self_block)
@@ -630,7 +645,7 @@
     loop(2, self_end)
 
     if inside:
-        loop(nb, lambda i: arrived(R.we0.at[:, rows(0, cw), :], K.we0, from_peer(i)), 1)
+        arrived(R.we0.at[:, pl.ds(0, (nb - 1) * cw), :], K.we0)
     send_e1()
 
     def enc_sum(j):
@@ -640,6 +655,7 @@
 
         @pl.when(is_a)
         def _():
+            sent(R.n2row.at[rows(blk(j))], K.n2y, j)
             R.ms[j] = (R.mid[j] + y).astype(BF16)
 
         @pl.when(is_b)
@@ -768,7 +784,7 @@
     tally(20, two * two)
 
     if inside:
-        loop(nb, lambda i: arrived(R.we1.at[:, rows(0, cw), :], K.we1, from_peer(i)), 1)
+        arrived(R.we1.at[:, pl.ds(0, (nb - 1) * cw), :], K.we1)
     arrived(R.b5.at[rows(sc)], K.b5, 0)
     arrived(R.b5.at[rows(sy)], K.b5, 1)
     row_copy(R.b5, sy, K.b5, core, 2).start()
@@ -842,18 +858,36 @@
 
     def dp_x(a, p):
         at = rows(lax.div(p, 2), cw)
-        return send(R.qA.at[a, :, rows(p, cw), :], R.pA.at[a, :, at, :], K.gd_x, (pair, s), a * nb + p)
+        return send(R.qA.at[a, :, rows(p, cw), :], R.pA.at[a, :, at, :], K.gd_x, (pair, s), 2 * a + lax.div(p, nb // 2))
 
     def dp_a(a, p):
         return send(
-            R.qA.at[a, :, rows(p, cw), :], R.dpA.at[a, lax.div(me, 2)], K.gd_a, (p, s), a * nb + p, a * nb + me
+            R.qA.at[a, :, rows(p, cw), :], R.dpA.at[a, lax.div(me, 2)], K.gd_a, (p, s), a
         )
 
     def dp_e(l, p):
-        return send(R.qE.at[l, :, rows(p, cw), :], R.dpE.at[l, me], K.gd_e, (p, s), l * nb + p, l * nb + me)
+        return send(R.qE.at[l, :, rows(p, cw), :], R.dpE.at[l, me], K.gd_e, (p, s), l)
 
     def here(src, dst, i):
         return pltpu.make_async_copy(src, dst, R.ss.at[K.here + i])
+
+    def put_dec():
+        return here(R.dec, R.z_dec, 5)
+
+    def put_sgrad():
+        return here(R.sgrad, R.z_sgrad, 6)
+
+    def put_tgrad():
+        return here(R.tgrad, R.z_tgrad, 7)
+
+    def put_stats():
+        return here(R.stats, R.z_stats, 8)
+
+    def put_ggb():
+        return here(R.ggb, R.z_ggb, 9)
+
+    def put_picks():
+        return here(R.smallr, R.z_picks, 10)
 
     def here_a(a):
         return here(R.qA.at[a, :, rows(me, cw), :], R.dpA.at[a, lax.div(me, 2)], a)
@@ -881,13 +915,16 @@
 
             loop(nb // 4, one)
 
+    def x_part(a, piece):
+        return R.pA.at[a, :, rows(piece, nb // 4 * cw), :]
+
     def dp_a_pass(a, piece):
         if inside:
+            arrived(x_part(a, piece), K.gd_x, 2 * a + piece)
 
             def one(i):
                 p = piece * (nb // 2) + 2 * i + lax.rem(me, 2)
                 at = rows(lax.div(p, 2), cw)
-                arrived(R.pA.at[a, :, at, :], K.gd_x, a * nb + p)
                 for m in range(4):
                     total = R.qA[a, m, rows(p, cw)].astype(F32) + R.pA[a, m, at].astype(F32)
                     R.qA[a, m, rows(p, cw)] = total.astype(BF16)
@@ -1008,12 +1045,15 @@
     branch5 = R.last[...] + R.er[0].astype(F32) + R.er[2].astype(F32)
     tally(25, branch5 * branch5)
     R.dec[...] = R.t2[...] + branch5
+    put_dec().start()
+    if inside:
+        put_picks().start()
 
     def cross_grads(t):
-        half_grads(t, R.n4c, R.mrow, R.dq.at[0:2 * B], R.o2, R.b4c)
+        half_grads(R.gX, t, R.n4c, R.mrow, R.dq.at[0:2 * B], R.o2, R.b4c)
 
     def y_grad_x():
-        return send(R.gA.at[:, :, lanes(1 - h)], R.ylX, K.gy_x, ypeer)
+        return send(R.gX.at[:, :, lanes(1 - h)], R.ylX, K.gy_x, ypeer)
 
     def y_grad_s(i):
         at = rows(i, half_d)
@@ -1025,7 +1065,7 @@
     def join_x():
         arrived(R.ylX, K.gy_x)
         for m in range(4):
-            total = R.gA[m, :, lanes(h)].astype(F32) + R.ylX[m].astype(F32)
+            total = R.gX[m, :, lanes(h)].astype(F32) + R.ylX[m].astype(F32)
             R.qA[2, m] = total.astype(BF16)
         for piece in range(2):
             dp_a_start(2, piece)
@@ -1037,11 +1077,8 @@
 
     if inside:
 
-        def chosen_sent(i):
-            for l in range(2):
-                sent(wblock(R.gE, 0, l, FQ), (K.we0, K.we1)[l], to_peer(i))
-
-        loop(nb, chosen_sent, 1)
+        for l in range(2):
+            sent((R.we0, R.we1)[l].at[:, pl.ds(0, (nb - 1) * cw), :], (K.we0, K.we1)[l])
 
     @pl.when(is_a)
     def _():
@@ -1160,12 +1197,11 @@
 
     self_half(1 - h, self_first)
 
-    y_grad_x().wait_send()
-
-    half_grads(1 - h, R.nrow, R.nrow, R.dq, R.o, R.brow, lambda i: y_grad_s(i).start())
+
+    half_grads(R.gA, 1 - h, R.nrow, R.nrow, R.dq, R.o, R.brow, lambda i: y_grad_s(i).start())
 
     def second_hook(i):
-        @pl.when(i == 2)
+        @pl.when(i == 3)
         def _():
             join_x()
 
@@ -1177,7 +1213,7 @@
             R.qA[h, m, at] = R.gA[m, at, lanes(h)]
         dp_a_start(h, i)
 
-    half_grads(h, R.nrow, R.nrow, R.dq, R.o, R.brow, own_piece)
+    half_grads(R.gA, h, R.nrow, R.nrow, R.dq, R.o, R.brow, own_piece)
 
     def other_pieces():
         for piece in range(2):
@@ -1215,6 +1251,7 @@
         @pl.when(is_a & (j == 0))
         def _():
             R.sgrad[...] = R.dmem[0] + back
+            put_sgrad().start()
 
         @pl.when(is_a & (j == 1))
         def _():
@@ -1229,6 +1266,7 @@
         @pl.when(is_b & (j == 1))
         def _():
             R.tgrad[...] = R.g3[...] + back
+            put_tgrad().start()
 
     loop(2, self_final)
 
@@ -1243,6 +1281,7 @@
     arrived(R.accy, K.accy)
     R.acc2[...] = R.acc1[...] + R.accy[...]
     R.stats[...] = R.acc2[16:32, :]
+    put_stats().start()
 
     if inside:
 
@@ -1250,39 +1289,45 @@
             return lanes(lax.div(p * cw, LANES))
 
         def acc_copy(p):
-            return send(R.acc2.at[0:16, tile_of(p)], R.accd.at[me], K.accd, (p, s), p, me)
+            return send(R.acc2.at[0:16, tile_of(p)], R.accd.at[me], K.accd, (p, s))
 
         loop(nb, lambda i: acc_copy(to_peer(i)).start(), 1)
-        R.picks[...] = R.smallr[...]
-
     pass_a(1 - h)
     arrived(R.fr, K.fin)
 
     @pl.when(is_a)
     def _():
         R.tgrad[...] = R.g3[...] + R.fr[...].astype(F32)
+        put_tgrad().start()
 
     @pl.when(is_b)
     def _():
         R.sgrad[...] = R.fr[...].astype(F32)
+        put_sgrad().start()
 
     if inside:
-        loop(nb, lambda i: arrived(R.accd.at[0], K.accd, from_peer(i)), 1)
+        arrived(R.accd.at[pl.ds(0, nb - 1)], K.accd)
         R.ggb[...] = R.acc2[0:16, tile_of(me)]
 
         def more(i):
             R.ggb[...] += R.accd[from_peer(i)]
 
         loop(nb, more, 1)
+        put_ggb().start()
         for l in range(2):
-            loop(nb, lambda i, l=l: arrived(R.dpE.at[l, 0], K.gd_e, l * nb + from_peer(i)), 1)
+            arrived(R.dpE.at[l, pl.ds(0, nb - 1)], K.gd_e, l)
             here_e(l).wait()
         for a in range(3):
-            loop(nb // 2, lambda i, a=a: arrived(R.dpA.at[a, 0], K.gd_a, a * nb + same_side(i)), 1)
+            arrived(R.dpA.at[a, pl.ds(0, nb // 2 - 1)], K.gd_a, a)
             here_a(a).wait()
     else:
         R.gacc[...] = R.acc2[0:16, :]
 
+    for copy in (put_dec, put_sgrad, put_tgrad, put_stats):
+        copy().wait()
+    if inside:
+        put_ggb().wait()
+        put_picks().wait()
     for name in (K.in_y, K.n4, K.b4, K.rs7q, K.fin):
         sent(R.oth, name)
     for name in (K.in_c, K.m_c, K.brow, K.rs9, K.n2, K.be):
@@ -1293,6 +1338,7 @@
             sent(R.oth, name, j)
     y_sent(other, K.wy_self, LANES)
     y_sent(R.wx, K.wy_x, LANES)
+    y_grad_x().wait_send()
     for piece in range(2):
         y_grad_s(piece).wait_send()
     sent(R.acc, K.accc)
@@ -1300,32 +1346,26 @@
 
     @pl.when(is_a)
     def _():
-        for name in (K.n2y, K.dm):
-            for j in range(2):
-                sent(R.oth, name, j)
+        for j in range(2):
+            sent(R.oth, K.dm, j)
 
     if inside:
 
         def drain_side(i):
             for a in range(3):
-                sent(R.sendA.at[0], K.wa, a * nb + same_side(i))
-                sent(R.sendA.at[0], K.wr, a * nb + same_side(i))
-                sent(R.sendA.at[0], K.gd_a, a * nb + same_side(i))
-                sent(R.sendA.at[0], K.gd_x, a * nb + far_side(i))
-
+                sent(R.sendA.at[0], K.wa, a * (nb // 2) + i)
+                sent(R.sendA.at[0], K.wr, a * (nb // 2) + i)
+
+        loop(nb // 2, drain_side, 1)
         for a in range(3):
-            sent(R.sendA.at[0], K.wa, a * nb + pair)
-            sent(R.sendA.at[0], K.gd_x, a * nb + pair)
-        loop(nb // 2, drain_side, 1)
-
-        def drain(i):
-            p = to_peer(i)
-            sent(R.small, K.small, p)
-            for l in range(2):
-                sent(R.qE.at[l, :, rows(0, cw), :], K.gd_e, l * nb + p)
-            sent(R.accd.at[0], K.accd, p)
-
-        loop(nb, drain, 1)
+            sent(R.sendA.at[0], K.wa, a * (nb // 2))
+            sent(R.dpA.at[a, pl.ds(0, nb // 2 - 1)], K.gd_a, a)
+            for piece in range(2):
+                sent(x_part(a, piece), K.gd_x, 2 * a + piece)
+        for l in range(2):
+            sent(R.dpE.at[l, pl.ds(0, nb - 1)], K.gd_e, l)
+        sent(R.smallr.at[pl.ds(0, nb - 1)], K.small)
+        sent(R.accd.at[pl.ds(0, nb - 1)], K.accd)
 
 
 def close_kernel(cfg, names, *refs):
@@ -1336,7 +1376,7 @@
     def copy(src, dst, i):
         return pltpu.make_async_copy(src, dst, R.sem.at[i])
 
-    plain = [(R.dec, R.o_dec), (R.sgrad, R.o_sgrad), (R.tgrad, R.o_tgrad)]
+    plain = [(R.z_dec, R.o_dec), (R.z_sgrad, R.o_sgrad), (R.z_tgrad, R.o_tgrad)]
     for i, (src, _) in enumerate(plain):
         copy(src, R.vp.at[i], i).start()
     for l in range(2):
@@ -1344,7 +1384,7 @@
     for a in range(3):
         copy(R.dpA.at[a], R.va.at[a], 5 + a).start()
 
-    stats = jnp.sum(R.stats[...], -1, keepdims=True) * (1.0 / (4 * B * D))
+    stats = jnp.sum(R.z_stats[...], -1, keepdims=True) * (1.0 / (4 * B * D))
     root = jnp.broadcast_to(jnp.sqrt(stats), (16, LANES))
     place = lax.broadcasted_iota(jnp.int32, (16, LANES), 0) - lax.broadcasted_iota(jnp.int32, (16, LANES), 1)
     for k in range(2):
@@ -1354,8 +1394,8 @@
 
         @pl.when(lax.rem(dp, LANES // cw) == k)
         def _(k=k):
-            R.o_gain[...] = R.ggb[0:5, k * cw:(k + 1) * cw]
-            R.o_bias[...] = R.ggb[5:10, k * cw:(k + 1) * cw]
+            R.o_gain[...] = R.z_ggb[0:5, k * cw:(k + 1) * cw]
+            R.o_bias[...] = R.z_ggb[5:10, k * cw:(k + 1) * cw]
 
     for i, (src, dst) in enumerate(plain):
         copy(src, R.vp.at[i], i).wait()
@@ -1365,7 +1405,7 @@
         R.w_up[l] = jnp.zeros((E, cw, FQ), F32)
         R.w_dn[l] = jnp.zeros((E, cw, FQ), F32)
         for p in range(nb):
-            e = jnp.max(R.picks[p, 10 + l:11 + l, :]).astype(jnp.int32)
+            e = jnp.max(R.z_picks[p, 10 + l:11 + l, :]).astype(jnp.int32)
             R.w_up[l, pl.ds(e, 1)] += R.ve[l, p, 0].astype(F32)[None]
             R.w_dn[l, pl.ds(e, 1)] += R.ve[l, p, 1].astype(F32)[None]
         copy(R.w_up.at[l], R.o_up.at[l], 8 + l).start()
@@ -1426,14 +1466,14 @@
 
     scalars = dict(slen=src_lengths, tlen=tgt_lengths)
     operands = dict(src=src_input[0], tgt=tgt_input[0], cot=out_cotangent[0])
-    results = dict(dec=f32(B, D), sgrad=f32(B, D), tgrad=f32(B, D), stats=f32(16, D))
-    far = {}
+    results = {}
+    far = dict(z_dec=f32(B, D), z_sgrad=f32(B, D), z_tgrad=f32(B, D), z_stats=f32(16, D))
     if inside:
         nb, rowsize = n, cw
         scalars.update(epick=enc_expert, dpick=dec_expert)
         operands.update(gains=norm_gains, biases=norm_biases, qkv=qkv_weight, wot=wot, up=expert_up, dnt=dnt)
-        results.update(ggb=f32(16, LANES), picks=f32(n, 16, LANES))
-        far = dict(dpA=bf16(3, n // 2, 4, cw, LANES), dpE=bf16(2, n, 2, cw, FQ))
+        far.update(z_ggb=f32(16, LANES), z_picks=f32(n, 16, LANES))
+        far.update(dpA=bf16(3, n // 2, 4, cw, LANES), dpE=bf16(2, n, 2, cw, FQ))
     else:
         nb, rowsize = 1, D
         gb = jnp.concatenate([norm_gains, norm_biases], 0).astype(F32)
@@ -1466,7 +1506,7 @@
     )(*scalars.values(), *operands.values())
     made = dict(zip(tuple(results) + tuple(far), outs, strict=True))
     if inside:
-        near = dict(stats=vmem, ggb=vmem, picks=vmem, dec=anywhere, sgrad=anywhere, tgrad=anywhere)
+        near = dict(z_stats=vmem, z_ggb=vmem, z_picks=vmem, z_dec=anywhere, z_sgrad=anywhere, z_tgrad=anywhere)
         near.update(dpA=anywhere, dpE=anywhere)
         last = dict(
             o_dec=f32(B, D),
@@ -1502,7 +1542,7 @@
             cost_estimate=pl.CostEstimate(flops=16 << 20, bytes_accessed=10 << 20, transcendentals=0),
         )(*[made[name] for name in near])
     else:
-        dec, sgrad, tgrad, stats, ga, ge, gacc = outs
+        ga, ge, gacc, dec, sgrad, tgrad, stats = outs
 
         def total(x, axis):
             return lax.psum_scatter(x, "dp", scatter_dimension=axis, tiled=True)

time: 188 us -> 183 us (0.973)
  Pallas kernels: 186 us -> 180 us
    pallas_call x1, Pallas kernels: 181 us -> 175 us  [on_device(): pl.pallas_call(functools.partial(step_kernel, cfg, names), name='step', o...]
where the time goes in v4:
time: 183 us; the launch traced here: 182 us
  Pallas kernels  180 us (98%)
  between operations  2.13 us (1%)
    pallas_call x1, Pallas kernels, on_device(): pl.pallas_call(functools.partial(step_kernel, cfg, names), name='step', o...  175 us
    pallas_call x1, Pallas kernels, on_device(): pl.pallas_call(functools.partial(close_kernel, cfg, tuple(near) + tuple(l...  5.14 us

profile of v4, /device:TPU:28, one launch (start us, length us, event | category | flops | bytes accessed | tf_op | source)
XLA Modules:
  0.0 182.3 jit_solution(261733282342565690)
XLA Ops:
  1.9 175.0 %step.1 = (f32[256,512]{1,0:T(8,128)}, f32[256,512]{1,0:T(8,128)}, f32[256,512]{1,0:T(8,128)}, f32[16,512]{1,0:T(8,128)}, f32[16,128]{1,0:T(8,128)}, /*index=5*/...) custom-call(s32[1,4]{1,0:T(1,128)} %refs_0_.1, s32[1,4]{1,0:T(1,128)} %refs_1_.1, ...), custom_call_target="tpu_custom_call" | custom-call | flops 18253611008 | bytes 8388608 | tf_op jit(solution)/shard_map/step/pallas_call | solution.py:1495
  176.9 5.1 %close.1 = (f32[256,512]{1,0:T(8,128)}, f32[256,512]{1,0:T(8,128)}, f32[256,512]{1,0:T(8,128)}, f32[5,64]{1,0:T(8,128)}, f32[5,64]{1,0:T(8,128)}, /*index=5*/f32...) custom-call(f32[16,512]{1,0:T(8,128)} %get-tuple-element.28.refs_0_,, ...), custom_call_target="tpu_custom_call" | custom-call | flops 16777216 | bytes 10485760 | tf_op jit(solution)/shard_map/close/pallas_call | solution.py:1534
